TPU v7x, 32 devices: a whole 2x2x4 slice. The times are simulated.
32 devices in a mesh: narrow: 4 (over y, x), wide: 8 (over z, core).
Axes of the slice: x: 2, y: 2, z: 4, core: 2. Of those that a mesh axis runs over, the one named last changes fastest.
Arguments:
- tokens: bfloat16 [128, 496, 768], P(('narrow', 'wide')), may hold values from -6 to 6
- patch_order: int32 [128, 496], P(('narrow', 'wide')), may hold values from 0 to 495, each once within a row
- visible: int32 [128], P(('narrow', 'wide')), may hold values from 1 to 128, 12288 in all
- query_weight: bfloat16 [768, 768], P('wide'), may hold values from -0.21875 to 0.21875
- key_weight: bfloat16 [768, 768], P('wide'), may hold values from -0.21875 to 0.21875
- value_weight: bfloat16 [768, 768], P('wide'), may hold values from -0.21875 to 0.21875
- out_weight: bfloat16 [768, 768], P('wide'), may hold values from -1.75 to 1.75
- up_weight: bfloat16 [768, 3072], P('wide'), may hold values from -0.21875 to 0.21875
- down_weight: bfloat16 [3072, 768], P('wide'), may hold values from -0.21875 to 0.21875
- query_bias: bfloat16 [768], P('wide'), may hold values from -1.796875 to 1.796875
- value_bias: bfloat16 [768], P('wide'), may hold values from -1.796875 to 1.796875
- out_bias: bfloat16 [768], P('wide'), may hold values from -1.796875 to 1.796875
- up_bias: bfloat16 [3072], P('wide'), may hold values from -1.796875 to 1.796875
- down_bias: bfloat16 [768], P('wide'), may hold values from -1.796875 to 1.796875
- first_gain: bfloat16 [768], P('wide'), may hold values from 0.5 to 1.5
- first_shift: bfloat16 [768], P('wide'), may hold values from -1.796875 to 1.796875
- second_gain: bfloat16 [768], P('wide'), may hold values from 0.5 to 1.5
- second_shift: bfloat16 [768], P('wide'), may hold values from -1.796875 to 1.796875
- bias_table: bfloat16 [320, 12], P('wide'), may hold values from -5 to 5
- gate_weight: float32 [64, 8], replicated, may hold values from -0.75 to 0.75
- gate_bias: float32 [8], replicated, may hold values from -2.5 to 2.5
- gate_scale: float32 [12], replicated, may hold values from 0.5 to 2
- cotangent: bfloat16 [128, 128, 768], P(('narrow', 'wide')), may hold values from -6 to 6
Outputs:
- output: bfloat16 [128, 128, 768], P(('narrow', 'wide'))
- tokens_grad: bfloat16 [128, 496, 768], P(('narrow', 'wide'))
- query_weight_grad: float32 [768, 768], P('wide')
- key_weight_grad: float32 [768, 768], P('wide')
- value_weight_grad: float32 [768, 768], P('wide')
- out_weight_grad: float32 [768, 768], P('wide')
- up_weight_grad: float32 [768, 3072], P('wide')
- down_weight_grad: float32 [3072, 768], P('wide')
- query_bias_grad: float32 [768], P('wide')
- value_bias_grad: float32 [768], P('wide')
- out_bias_grad: float32 [768], P('wide')
- up_bias_grad: float32 [3072], P('wide')
- down_bias_grad: float32 [768], P('wide')
- first_gain_grad: float32 [768], P('wide')
- first_shift_grad: float32 [768], P('wide')
- second_gain_grad: float32 [768], P('wide')
- second_shift_grad: float32 [768], P('wide')
- bias_table_grad: float32 [320, 12], P('wide')
- gate_weight_grad: float32 [64, 8], replicated
- gate_bias_grad: float32 [8], replicated
- gate_scale_grad: float32 [12], replicated
Inputs may be any that keep to these rules, and one draw needn't show every extreme that they name: Each row of patch_order names every patch of a clip once. The most visible patches of a clip is exactly 128 in every draw.
All inputs are finite; a program needn't handle non-finite values. No bound on the sum of `visible` on one device may be relied on, other than what follows from the above.
Results may differ from a plain program's by a relative error of at most 0.023.
Values may be sent and summed in bfloat16 or wider, within the bound.
No kernel may reach another device: no remote copies, remote signals or barrier semaphores. Data moves between devices by JAX's collectives and lax.ppermute only.
A program may use at most 192 MiB of HBM per device.

v0:
```python
from functools import partial
import math

import jax
import jax.numpy as jnp
import numpy as np
from jax import lax
from jax.sharding import PartitionSpec as P

NUM_BUCKETS = 320


highest = lax.Precision.HIGHEST
deep_alpha = math.pow(24.0, 0.25)
norm_eps = 1e-05


def far_thresholds():
    distance = np.arange(80, 400000)
    ratio = np.log(np.maximum(distance, 1) / 80.0) / math.log(10.0)
    beyond = np.minimum(80 + np.floor(ratio * 80.0).astype(np.int64), 159)
    steps = [int(distance[np.searchsorted(beyond, 80 + level)]) for level in range(1, 80)]
    return np.asarray(steps, dtype=np.int32)


def pair_buckets(slots):
    relative = slots[None, :] - slots[:, None]
    magnitude = jnp.abs(relative)
    limits = jnp.asarray(far_thresholds())
    beyond = 80 + jnp.sum((magnitude[..., None] >= limits).astype(jnp.int32), -1)
    return jnp.where(relative > 0, 160, 0) + jnp.where(magnitude < 80, magnitude, beyond)


def norm_parts(values, gain, shift):
    center = values - jnp.mean(values, -1, keepdims=True)
    spread = jnp.mean(center * center, -1, keepdims=True)
    inverse = lax.rsqrt(spread + norm_eps)
    unit = center * inverse
    return (unit * gain + shift, unit, inverse)


def norm_back(grad, unit, inverse, gain):
    scaled = grad * gain
    return inverse * (
        scaled
        - jnp.mean(scaled, -1, keepdims=True)
        - unit * jnp.mean(scaled * unit, -1, keepdims=True)
    )


def project(inputs, matrix):
    return jnp.dot(inputs, matrix, preferred_element_type=jnp.float32)


def project_back(grad, matrix):
    return jnp.einsum("re,de->rd", grad, matrix, preferred_element_type=jnp.float32)


def weight_grad(inputs, grad):
    return jnp.einsum("rd,re->de", inputs, grad, preferred_element_type=jnp.float32)


def body(
    tokens,
    patch_order,
    visible,
    query_weight,
    key_weight,
    value_weight,
    out_weight,
    up_weight,
    down_weight,
    query_bias,
    value_bias,
    out_bias,
    up_bias,
    down_bias,
    first_gain,
    first_shift,
    second_gain,
    second_shift,
    bias_table,
    gate_weight,
    gate_bias,
    gate_scale,
    cotangent,
):
    gathered = (
        lax.all_gather(query_weight, "wide", axis=0, tiled=True),
        lax.all_gather(key_weight, "wide", axis=0, tiled=True),
        lax.all_gather(value_weight, "wide", axis=0, tiled=True),
        lax.all_gather(out_weight, "wide", axis=0, tiled=True),
        lax.all_gather(up_weight, "wide", axis=0, tiled=True),
        lax.all_gather(down_weight, "wide", axis=0, tiled=True),
        lax.all_gather(query_bias, "wide", axis=0, tiled=True),
        lax.all_gather(value_bias, "wide", axis=0, tiled=True),
        lax.all_gather(out_bias, "wide", axis=0, tiled=True),
        lax.all_gather(up_bias, "wide", axis=0, tiled=True),
        lax.all_gather(down_bias, "wide", axis=0, tiled=True),
        lax.all_gather(first_gain, "wide", axis=0, tiled=True),
        lax.all_gather(first_shift, "wide", axis=0, tiled=True),
        lax.all_gather(second_gain, "wide", axis=0, tiled=True),
        lax.all_gather(second_shift, "wide", axis=0, tiled=True),
        lax.all_gather(bias_table, "wide", axis=0, tiled=True),
    )
    (
        query_full,
        key_full,
        value_full,
        out_full,
        up_full,
        down_full,
        query_bias_full,
        value_bias_full,
        out_bias_full,
        up_bias_full,
        down_bias_full,
        first_gain_full,
        first_shift_full,
        second_gain_full,
        second_shift_full,
        table_full,
    ) = gathered
    clip_count, patch_count, model_width = tokens.shape
    visible_len = cotangent.shape[1]
    head_count = table_full.shape[1]
    head_dim = model_width // head_count
    row_count = clip_count * visible_len
    score_scale = head_dim ** (-0.5)
    head_shape = (clip_count, visible_len, head_count, head_dim)
    bucket_ids = jnp.arange(NUM_BUCKETS, dtype=jnp.int32)
    slots = patch_order[:, :visible_len]
    row_live = jnp.arange(visible_len, dtype=jnp.int32)[None, :] < visible[:, None]
    match = (
        slots[:, :, None] == jnp.arange(patch_count, dtype=jnp.int32)[None, None, :]
    ) & row_live[:, :, None]
    select = jnp.where(match, 1.0, 0.0).astype(jnp.bfloat16)
    picked = jnp.einsum("cvp,cpd->cvd", select, tokens, preferred_element_type=jnp.float32).astype(
        jnp.bfloat16
    )
    flat_rows = picked.reshape(row_count, model_width)
    picked_f32 = flat_rows.astype(jnp.float32)
    query_rows = (project(flat_rows, query_full) + query_bias_full.astype(jnp.float32)).astype(
        jnp.bfloat16
    )
    key_rows = project(flat_rows, key_full).astype(jnp.bfloat16)
    value_rows = (project(flat_rows, value_full) + value_bias_full.astype(jnp.float32)).astype(
        jnp.bfloat16
    )
    gate_input = picked_f32.reshape(head_shape)
    logits = jnp.einsum("cihe,ef->cihf", gate_input, gate_weight, precision=highest) + gate_bias
    gate_first = jax.nn.sigmoid(jnp.sum(logits[..., :4], -1))
    gate_second = jax.nn.sigmoid(jnp.sum(logits[..., 4:], -1))
    gate_value = gate_first * (gate_second * gate_scale - 1.0) + 2.0
    gate_heads = jnp.transpose(gate_value, (0, 2, 1))[..., None]
    buckets = jax.vmap(pair_buckets)(slots).reshape(clip_count, visible_len * visible_len)

    def clip_position(clip_buckets):
        onehot = (clip_buckets[:, None] == bucket_ids[None, :]).astype(jnp.bfloat16)
        pairs = jnp.dot(onehot, table_full, preferred_element_type=jnp.float32)
        return jnp.transpose(pairs.reshape(visible_len, visible_len, head_count), (2, 0, 1))

    position = lax.map(clip_position, buckets)
    key_live = row_live[:, None, None, :]

    def score_block():
        raw = (
            jnp.einsum(
                "cihe,cjhe->chij",
                query_rows.reshape(head_shape),
                key_rows.reshape(head_shape),
                preferred_element_type=jnp.float32,
            )
            * score_scale
        )
        return jnp.where(key_live, raw + gate_heads * position, -1000000000.0)

    scores = score_block()
    top_score = jnp.max(scores, -1, keepdims=True)
    log_total = top_score + jnp.log(jnp.sum(jnp.exp(scores - top_score), -1, keepdims=True))
    soft_weights = jnp.exp(scores - log_total)
    head_mixed = jnp.einsum(
        "chij,cjhe->cihe",
        soft_weights.astype(jnp.bfloat16),
        value_rows.reshape(head_shape),
        preferred_element_type=jnp.float32,
    )
    head_mixed = head_mixed.reshape(row_count, model_width).astype(jnp.bfloat16)
    attended = project(head_mixed, out_full) + out_bias_full.astype(jnp.float32)
    normed, unit_first, inverse_first = norm_parts(
        deep_alpha * picked_f32 + attended,
        first_gain_full.astype(jnp.float32),
        first_shift_full.astype(jnp.float32),
    )
    normed_low = normed.astype(jnp.bfloat16)
    hidden = project(normed_low, up_full) + up_bias_full.astype(jnp.float32)
    activated_f32, gelu_pull = jax.vjp(partial(jax.nn.gelu, approximate=False), hidden)
    activated = activated_f32.astype(jnp.bfloat16)
    branch = project(activated, down_full) + down_bias_full.astype(jnp.float32)
    result, unit_second, inverse_second = norm_parts(
        deep_alpha * normed + branch,
        second_gain_full.astype(jnp.float32),
        second_shift_full.astype(jnp.float32),
    )
    live_rows = row_live.reshape(row_count, 1).astype(jnp.float32)
    output = (result * live_rows).astype(jnp.bfloat16).reshape(clip_count, visible_len, model_width)
    regathered = (
        lax.all_gather(query_weight, "wide", axis=0, tiled=True),
        lax.all_gather(key_weight, "wide", axis=0, tiled=True),
        lax.all_gather(value_weight, "wide", axis=0, tiled=True),
        lax.all_gather(out_weight, "wide", axis=0, tiled=True),
        lax.all_gather(up_weight, "wide", axis=0, tiled=True),
        lax.all_gather(down_weight, "wide", axis=0, tiled=True),
        lax.all_gather(first_gain, "wide", axis=0, tiled=True),
        lax.all_gather(second_gain, "wide", axis=0, tiled=True),
    )
    (
        query_back,
        key_back,
        value_back,
        out_back,
        up_back,
        down_back,
        first_gain_back,
        second_gain_back,
    ) = regathered
    grad_result = cotangent.astype(jnp.float32).reshape(row_count, model_width) * live_rows
    second_gain_grad = jnp.sum(grad_result * unit_second, 0)
    second_shift_grad = jnp.sum(grad_result, 0)
    grad_pre_second = norm_back(
        grad_result, unit_second, inverse_second, second_gain_back.astype(jnp.float32)
    )
    grad_branch = grad_pre_second.astype(jnp.bfloat16)
    down_bias_grad = jnp.sum(grad_branch.astype(jnp.float32), 0)
    down_weight_grad = weight_grad(activated, grad_branch)
    grad_activated = project_back(grad_branch, down_back)
    grad_hidden = gelu_pull(grad_activated)[0].astype(jnp.bfloat16)
    up_bias_grad = jnp.sum(grad_hidden.astype(jnp.float32), 0)
    up_weight_grad = weight_grad(normed_low, grad_hidden)
    grad_normed = deep_alpha * grad_pre_second + project_back(grad_hidden, up_back)
    first_gain_grad = jnp.sum(grad_normed * unit_first, 0)
    first_shift_grad = jnp.sum(grad_normed, 0)
    grad_pre_first = norm_back(
        grad_normed, unit_first, inverse_first, first_gain_back.astype(jnp.float32)
    )
    grad_attended = grad_pre_first.astype(jnp.bfloat16)
    out_bias_grad = jnp.sum(grad_attended.astype(jnp.float32), 0)
    out_weight_grad = weight_grad(head_mixed, grad_attended)
    grad_mixed = project_back(grad_attended, out_back).astype(jnp.bfloat16).reshape(head_shape)
    scores = score_block()
    soft_weights = jnp.exp(scores - log_total)
    grad_soft = jnp.einsum(
        "cihe,cjhe->chij",
        grad_mixed,
        value_rows.reshape(head_shape),
        preferred_element_type=jnp.float32,
    )
    grad_value = jnp.einsum(
        "chij,cihe->cjhe",
        soft_weights.astype(jnp.bfloat16),
        grad_mixed,
        preferred_element_type=jnp.float32,
    )
    grad_value = grad_value.reshape(row_count, model_width).astype(jnp.bfloat16)
    grad_scores = (
        soft_weights * (grad_soft - jnp.sum(grad_soft * soft_weights, -1, keepdims=True))
    ).astype(jnp.bfloat16)
    grad_query = (
        (
            jnp.einsum(
                "chij,cjhe->cihe",
                grad_scores,
                key_rows.reshape(head_shape),
                preferred_element_type=jnp.float32,
            )
            * score_scale
        )
        .reshape(row_count, model_width)
        .astype(jnp.bfloat16)
    )
    grad_key = (
        (
            jnp.einsum(
                "chij,cihe->cjhe",
                grad_scores,
                query_rows.reshape(head_shape),
                preferred_element_type=jnp.float32,
            )
            * score_scale
        )
        .reshape(row_count, model_width)
        .astype(jnp.bfloat16)
    )
    grad_scores_f32 = grad_scores.astype(jnp.float32)
    grad_gate = jnp.transpose(jnp.sum(grad_scores_f32 * position, -1), (0, 2, 1))
    grad_pairs = jnp.transpose(grad_scores_f32 * gate_heads, (0, 2, 3, 1)).reshape(
        clip_count, visible_len * visible_len, head_count
    )

    def clip_table_grad(inputs):
        clip_buckets, clip_grad = inputs
        onehot = (clip_buckets[:, None] == bucket_ids[None, :]).astype(jnp.float32)
        return jnp.einsum("pb,ph->bh", onehot, clip_grad, precision=highest)

    bias_table_grad = jnp.sum(lax.map(clip_table_grad, (buckets, grad_pairs)), 0)
    grad_first = grad_gate * (gate_second * gate_scale - 1.0)
    grad_second = grad_gate * gate_first * gate_scale
    gate_scale_grad = jnp.sum(grad_gate * gate_first * gate_second, (0, 1))
    grad_logit_first = grad_first * gate_first * (1.0 - gate_first)
    grad_logit_second = grad_second * gate_second * (1.0 - gate_second)
    grad_logits = jnp.concatenate(
        [
            jnp.repeat(grad_logit_first[..., None], 4, -1),
            jnp.repeat(grad_logit_second[..., None], 4, -1),
        ],
        -1,
    )
    gate_bias_grad = jnp.sum(grad_logits, (0, 1, 2))
    gate_weight_grad = jnp.einsum("cihe,cihf->ef", gate_input, grad_logits, precision=highest)
    grad_gate_input = jnp.einsum(
        "cihf,ef->cihe", grad_logits, gate_weight, precision=highest
    ).reshape(row_count, model_width)
    query_bias_grad = jnp.sum(grad_query.astype(jnp.float32), 0)
    value_bias_grad = jnp.sum(grad_value.astype(jnp.float32), 0)
    query_weight_grad = weight_grad(flat_rows, grad_query)
    key_weight_grad = weight_grad(flat_rows, grad_key)
    value_weight_grad = weight_grad(flat_rows, grad_value)
    grad_picked = (
        deep_alpha * grad_pre_first
        + project_back(grad_query, query_back)
        + project_back(grad_key, key_back)
        + project_back(grad_value, value_back)
        + grad_gate_input
    )
    grad_picked = grad_picked.astype(jnp.bfloat16).reshape(clip_count, visible_len, model_width)
    tokens_grad = jnp.einsum(
        "cvp,cvd->cpd", select, grad_picked, preferred_element_type=jnp.float32
    ).astype(jnp.bfloat16)
    shard_sums = (
        lax.psum_scatter(
            query_weight_grad.astype(jnp.bfloat16), "wide", scatter_dimension=0, tiled=True
        ).astype(jnp.float32),
        lax.psum_scatter(
            key_weight_grad.astype(jnp.bfloat16), "wide", scatter_dimension=0, tiled=True
        ).astype(jnp.float32),
        lax.psum_scatter(
            value_weight_grad.astype(jnp.bfloat16), "wide", scatter_dimension=0, tiled=True
        ).astype(jnp.float32),
        lax.psum_scatter(
            out_weight_grad.astype(jnp.bfloat16), "wide", scatter_dimension=0, tiled=True
        ).astype(jnp.float32),
        lax.psum_scatter(
            up_weight_grad.astype(jnp.bfloat16), "wide", scatter_dimension=0, tiled=True
        ).astype(jnp.float32),
        lax.psum_scatter(
            down_weight_grad.astype(jnp.bfloat16), "wide", scatter_dimension=0, tiled=True
        ).astype(jnp.float32),
        lax.psum_scatter(
            query_bias_grad.astype(jnp.bfloat16), "wide", scatter_dimension=0, tiled=True
        ).astype(jnp.float32),
        lax.psum_scatter(
            value_bias_grad.astype(jnp.bfloat16), "wide", scatter_dimension=0, tiled=True
        ).astype(jnp.float32),
        lax.psum_scatter(
            out_bias_grad.astype(jnp.bfloat16), "wide", scatter_dimension=0, tiled=True
        ).astype(jnp.float32),
        lax.psum_scatter(
            up_bias_grad.astype(jnp.bfloat16), "wide", scatter_dimension=0, tiled=True
        ).astype(jnp.float32),
        lax.psum_scatter(
            down_bias_grad.astype(jnp.bfloat16), "wide", scatter_dimension=0, tiled=True
        ).astype(jnp.float32),
        lax.psum_scatter(
            first_gain_grad.astype(jnp.bfloat16), "wide", scatter_dimension=0, tiled=True
        ).astype(jnp.float32),
        lax.psum_scatter(
            first_shift_grad.astype(jnp.bfloat16), "wide", scatter_dimension=0, tiled=True
        ).astype(jnp.float32),
        lax.psum_scatter(
            second_gain_grad.astype(jnp.bfloat16), "wide", scatter_dimension=0, tiled=True
        ).astype(jnp.float32),
        lax.psum_scatter(
            second_shift_grad.astype(jnp.bfloat16), "wide", scatter_dimension=0, tiled=True
        ).astype(jnp.float32),
        lax.psum_scatter(
            bias_table_grad.astype(jnp.bfloat16), "wide", scatter_dimension=0, tiled=True
        ).astype(jnp.float32),
    )
    replica_sums = (
        lax.psum(shard_sums[0].astype(jnp.bfloat16), "narrow").astype(jnp.float32),
        lax.psum(shard_sums[1].astype(jnp.bfloat16), "narrow").astype(jnp.float32),
        lax.psum(shard_sums[2].astype(jnp.bfloat16), "narrow").astype(jnp.float32),
        lax.psum(shard_sums[3].astype(jnp.bfloat16), "narrow").astype(jnp.float32),
        lax.psum(shard_sums[4].astype(jnp.bfloat16), "narrow").astype(jnp.float32),
        lax.psum(shard_sums[5].astype(jnp.bfloat16), "narrow").astype(jnp.float32),
        lax.psum(shard_sums[6].astype(jnp.bfloat16), "narrow").astype(jnp.float32),
        lax.psum(shard_sums[7].astype(jnp.bfloat16), "narrow").astype(jnp.float32),
        lax.psum(shard_sums[8].astype(jnp.bfloat16), "narrow").astype(jnp.float32),
        lax.psum(shard_sums[9].astype(jnp.bfloat16), "narrow").astype(jnp.float32),
        lax.psum(shard_sums[10].astype(jnp.bfloat16), "narrow").astype(jnp.float32),
        lax.psum(shard_sums[11].astype(jnp.bfloat16), "narrow").astype(jnp.float32),
        lax.psum(shard_sums[12].astype(jnp.bfloat16), "narrow").astype(jnp.float32),
        lax.psum(shard_sums[13].astype(jnp.bfloat16), "narrow").astype(jnp.float32),
        lax.psum(shard_sums[14].astype(jnp.bfloat16), "narrow").astype(jnp.float32),
        lax.psum(shard_sums[15].astype(jnp.bfloat16), "narrow").astype(jnp.float32),
    )
    matrix_sums = (
        replica_sums[0],
        replica_sums[1],
        replica_sums[2],
        replica_sums[3],
        replica_sums[4],
        replica_sums[5],
        replica_sums[15],
    )
    vector_sums = replica_sums[6:15]
    gate_sums = lax.psum((gate_weight_grad, gate_bias_grad, gate_scale_grad), ("narrow", "wide"))
    return (
        output,
        tokens_grad,
        matrix_sums[0],
        matrix_sums[1],
        matrix_sums[2],
        matrix_sums[3],
        matrix_sums[4],
        matrix_sums[5],
        vector_sums[0],
        vector_sums[1],
        vector_sums[2],
        vector_sums[3],
        vector_sums[4],
        vector_sums[5],
        vector_sums[6],
        vector_sums[7],
        vector_sums[8],
        matrix_sums[6],
        gate_sums[0],
        gate_sums[1],
        gate_sums[2],
    )


def solution(mesh):
    in_specs = (
        P(("narrow", "wide"), None, None),
        P(("narrow", "wide"), None),
        P(("narrow", "wide")),
        P("wide", None),
        P("wide", None),
        P("wide", None),
        P("wide", None),
        P("wide", None),
        P("wide", None),
        P("wide"),
        P("wide"),
        P("wide"),
        P("wide"),
        P("wide"),
        P("wide"),
        P("wide"),
        P("wide"),
        P("wide"),
        P("wide", None),
        P(),
        P(),
        P(),
        P(("narrow", "wide"), None, None),
    )
    out_specs = (
        P(("narrow", "wide"), None, None),
        P(("narrow", "wide"), None, None),
        P("wide", None),
        P("wide", None),
        P("wide", None),
        P("wide", None),
        P("wide", None),
        P("wide", None),
        P("wide"),
        P("wide"),
        P("wide"),
        P("wide"),
        P("wide"),
        P("wide"),
        P("wide"),
        P("wide"),
        P("wide"),
        P("wide", None),
        P(),
        P(),
        P(),
    )
    return jax.shard_map(body, mesh=mesh, in_specs=in_specs, out_specs=out_specs, check_vma=False)
```

profile of v0, /device:TPU:0, one launch (start us, length us, event | category | flops | bytes accessed | tf_op | source)
XLA Modules:
  0.0 567.0 jit_solution(4958036519893541719)
XLA Ops:
  19.1 30.4 %all-reduce.20 = (bf16[768]{0:T(1024)(128)(2,1)S(1)}, bf16[768]{0:T(1024)(128)(2,1)S(1)}, bf16[768]{0:T(1024)(128)(2,1)S(1)}, bf16[768]{0:T(1024)(128)(2,1)S(1)}...) all-reduce(bf16[768]{0:T(1024)(128)(2,1)S(1)} %dynamic-update-slice, ...), channel_id=1, replica_groups=mesh['narrow'=4,'wide'=8] {'wide'}, use_global_device_ids=true, to_apply=%add.2 | all-reduce | flops 5376 | bytes 21504
  55.1 2.2 convert_reduce_fusion
  57.3 14.0 %all-gather = bf16[8,40,12]{1,2,0:T(8,128)(2,1)S(1)} all-gather(bf16[1,40,12]{1,2,0:T(8,128)(2,1)S(1)} %bitcast.223), channel_id=1, replica_groups=mesh['narrow'=4,'wide'=8] {'wide'}, dimensions={0}, use_global_device_ids=true | all-gather | bytes 8640 | tf_op jit(solution)/shard_map/all_gather | solution.py:104
  72.0 18.8 %while.22 = (s32[]{:T(128)}, f32[4,12,128,128]{2,3,1,0:T(8,128)}, s32[4,16384]{1,0:T(4,128)S(1)}, bf16[320,12]{0,1:T(8,128)(2,1)S(1)}, s32[]{:T(128)}) while((s32[]{:T(128)}, f32[4,12,128,128]{2,3,1,0:T(8,128)}, s32[4,16384]{1,0:T(4,128)S(1)}, bf16[320,12]{0,1:T(8,128)(2,1)S(1)}, s32[]{:T(128)}) %tuple.74), condition=%wide.region_4.5_spmd.clone, body=%wide.region_3.4_spmd.clone.sunk | while | flops 131072000 | bytes 7807041 | solution.py:163
  72.1 3.2 fusion.134
  76.8 3.2 fusion.134
  81.5 3.2 fusion.134
  86.2 3.2 fusion.134
  92.1 13.0 %all-gather.1 = bf16[8,1,384]{2,1,0:T(2,128)(2,1)S(1)} all-gather(bf16[1,1,384]{2,1,0:T(2,128)(2,1)S(1)} %reshape.303), channel_id=1, replica_groups=mesh['narrow'=4,'wide'=8] {'wide'}, dimensions={0}, use_global_device_ids=true | all-gather | bytes 6912 | tf_op jit(solution)/shard_map/all_gather | solution.py:98
  108.4 2.3 add_convert_fusion.2
  112.1 2.0 convolution_convert_fusion.8
  115.5 2.1 add_convert_fusion.3
  119.0 3.5 fusion.94
  125.9 2.7 fusion.95
  130.6 29.8 %all-gather.17.cloned.1.call-done = bf16[768,3072]{1,0:T(8,128)(2,1)} async-done(((bf16[96,3072]{1,0:T(8,128)(2,1)}), bf16[768,3072]{1,0:T(8,128)(2,1)}) %all-gather.17.cloned.1.call-update) | async-done | bytes 4718608 | tf_op jit(solution)/shard_map/all_gather | solution.py:93
  160.4 21.8 %multiply_convert_fusion = (bf16[512,3072]{1,0:T(8,128)(2,1)}, f32[512,3072]{1,0:T(8,128)}, f32[512,3072]{1,0:T(8,128)}) fusion(f32[3072]{0:T(1024)} %bitcast.221, bf16[768,3072]{1,0:T(8,128)(2,1)} %all-gather.17.cloned.1.call-done, f32[512,768]{1,0:T(8,128)} %copy-done.14, f32[768]{0:T(1024)} %convert_element_type.288, f32[768]{0:T(1024)S(1)} %convert_element_type.287, ...), kind=kOutput, calls=%fused_computation.21 | convolution fusion | flops 2521694208 | bytes 22042624 | tf_op jit(solution)/shard_map/dot_general | solution.py:52
  182.2 30.3 %all-gather.19.cloned.1.call-done = bf16[3072,768]{1,0:T(8,128)(2,1)} async-done(((bf16[384,768]{1,0:T(8,128)(2,1)}), bf16[3072,768]{1,0:T(8,128)(2,1)}) %all-gather.19.cloned.1.call-update) | async-done | bytes 4718608 | tf_op jit(solution)/shard_map/all_gather | solution.py:94
  212.4 6.6 %fusion.96 = (f32[512]{0:T(512)S(1)}, f32[512,768]{1,0:T(8,128)S(1)}) fusion(f32[768]{0:T(1024)} %convert_element_type.292, bf16[512,3072]{1,0:T(8,128)(2,1)} %get-tuple-element.190, bf16[3072,768]{1,0:T(8,128)(2,1)} %all-gather.19.cloned.1.call-done, f32[768]{0:T(1024)} %convert_element_type.288, f32[768]{0:T(1024)S(1)} %convert_element_type.287, ...), kind=kOutput, calls=%fused_computation.183 | convolution fusion | flops 2419064320 | bytes 11025408 | tf_op jit(solution)/shard_map/dot_general | solution.py:52
  221.9 10.0 %fusion.99 = (bf16[3072]{0:T(1024)(128)(2,1)}, bf16[512,3072]{1,0:T(8,128)(2,1)S(1)}) fusion(f32[512,3072]{1,0:T(8,128)} %get-tuple-element.191, bf16[3072,768]{1,0:T(8,128)(2,1)} %all-gather.19.cloned.1.call-done, f32[512,768]{1,0:T(8,128)S(1)} %get-tuple-element.187, f32[512,3072]{1,0:T(8,128)} %get-tuple-element.207, f32[3072]{0:T(1024)S(1)} %bitcast.222), kind=kOutput, calls=%fused_computation.186 | convolution fusion | flops 2441475072 | bytes 22038528 | tf_op jit(solution)/shard_map/re,de->rd/dot_general | solution.py:56
  231.9 3.7 multiply_reduce_fusion.2
  235.6 2.3 convert_reduce_fusion.1
  237.9 3.2 convolution_convert_fusion.3
  241.2 3.5 convolution_convert_fusion.7
  244.7 2.3 copy.213
  247.0 2.4 reshape.270
  249.4 2.5 multiply_reduce_fusion
  252.0 2.2 fusion.19
  259.0 3.1 fusion.98
  269.1 6.5 %convolution_convert_fusion.1 = bf16[768,3072]{1,0:T(8,128)(2,1)} fusion(bf16[512,3072]{1,0:T(8,128)(2,1)} %copy-done.76, f32[512,768]{1,0:T(8,128)S(1)} %copy-done.16, f32[768]{0:T(1024)S(1)} %copy-done.64, f32[768]{0:T(1024)S(1)} %copy-done.48, f32[512]{0:T(512)S(1)} %copy-done.53, f32[512]{0:T(512)S(1)} %copy-done.43), kind=kOutput, calls=%fused_computation.36 | convolution fusion | flops 2420244480 | bytes 9447424 | tf_op jit(solution)/shard_map/rd,re->de/dot_general | solution.py:60
  277.8 2.1 fusion.20
  280.0 2.4 copy.236
  282.4 2.4 reshape.325
  284.9 7.3 %convolution_convert_fusion = bf16[3072,768]{1,0:T(8,128)(2,1)} fusion(bf16[512,3072]{1,0:T(8,128)(2,1)} %get-tuple-element.190, f32[512,768]{1,0:T(8,128)} %copy-done.21), kind=kOutput, calls=%fused_computation.35 | convolution fusion | flops 2418671616 | bytes 9437184 | tf_op jit(solution)/shard_map/rd,re->de/dot_general | solution.py:60
  293.2 41.1 %while.23 = (s32[]{:T(128)}, f32[4,320,12]{1,2,0:T(8,128)S(1)}, s32[4,16384]{1,0:T(4,128)S(1)}, f32[4,16384,12]{1,2,0:T(8,128)}, s32[]{:T(128)}) while((s32[]{:T(128)}, f32[4,320,12]{1,2,0:T(8,128)S(1)}, s32[4,16384]{1,0:T(4,128)S(1)}, f32[4,16384,12]{1,2,0:T(8,128)}, s32[]{:T(128)}) %tuple.108), condition=%wide.region_57.58_spmd.clone, body=%wide.region_56.57_spmd.clone.sunk | while | flops 760217600 | bytes 1270849 | solution.py:305
  293.3 10.3 %fusion.136 = f32[4,320,12]{1,2,0:T(8,128)S(1)} fusion(f32[4,320,12]{1,2,0:T(8,128)S(1)} %get-tuple-element.292, s32[]{:T(128)} %get-tuple-element.291, s32[16384]{0:T(1024)S(1)} %bitcast.207, f32[4,16384,12]{1,2,0:T(8,128)} %get-tuple-element.299), kind=kOutput, calls=%fused_computation.12.clone.1 | convolution fusion | flops 760217600 | bytes 1139712 | tf_op jit(solution)/shard_map/while/body/eval_jaxpr/pb,ph->bh/dot_general | solution.py:303
  303.6 10.2 %fusion.136 = f32[4,320,12]{1,2,0:T(8,128)S(1)} fusion(f32[4,320,12]{1,2,0:T(8,128)S(1)} %get-tuple-element.292, s32[]{:T(128)} %get-tuple-element.291, s32[16384]{0:T(1024)S(1)} %bitcast.207, f32[4,16384,12]{1,2,0:T(8,128)} %get-tuple-element.299), kind=kOutput, calls=%fused_computation.12.clone.1 | convolution fusion | flops 760217600 | bytes 1139712 | tf_op jit(solution)/shard_map/while/body/eval_jaxpr/pb,ph->bh/dot_general | solution.py:303
  313.9 10.2 %fusion.136 = f32[4,320,12]{1,2,0:T(8,128)S(1)} fusion(f32[4,320,12]{1,2,0:T(8,128)S(1)} %get-tuple-element.292, s32[]{:T(128)} %get-tuple-element.291, s32[16384]{0:T(1024)S(1)} %bitcast.207, f32[4,16384,12]{1,2,0:T(8,128)} %get-tuple-element.299), kind=kOutput, calls=%fused_computation.12.clone.1 | convolution fusion | flops 760217600 | bytes 1139712 | tf_op jit(solution)/shard_map/while/body/eval_jaxpr/pb,ph->bh/dot_general | solution.py:303
  324.1 10.2 %fusion.136 = f32[4,320,12]{1,2,0:T(8,128)S(1)} fusion(f32[4,320,12]{1,2,0:T(8,128)S(1)} %get-tuple-element.292, s32[]{:T(128)} %get-tuple-element.291, s32[16384]{0:T(1024)S(1)} %bitcast.207, f32[4,16384,12]{1,2,0:T(8,128)} %get-tuple-element.299), kind=kOutput, calls=%fused_computation.12.clone.1 | convolution fusion | flops 760217600 | bytes 1139712 | tf_op jit(solution)/shard_map/while/body/eval_jaxpr/pb,ph->bh/dot_general | solution.py:303
  334.4 27.1 %all-reduce.19 = (bf16[768]{0:T(1024)(128)(2,1)S(1)}, bf16[768]{0:T(1024)(128)(2,1)S(1)}, bf16[768]{0:T(1024)(128)(2,1)S(1)}, bf16[768]{0:T(1024)(128)(2,1)S(1)}...) all-reduce(bf16[768]{0:T(1024)(128)(2,1)S(1)} %copy-done.58, ...), channel_id=1, replica_groups=mesh['narrow'=4,'wide'=8] {'wide'}, use_global_device_ids=true, to_apply=%add.7 | all-reduce | flops 13824 | bytes 55296
  364.1 10.3 %reduce-scatter.8.cloned.1.call-done = bf16[96,768]{1,0:T(8,128)(2,1)} async-done(((bf16[768,768]{1,0:T(8,128)(2,1)}), bf16[96,768]{1,0:T(8,128)(2,1)}) %reduce-scatter.8.cloned.1.call-update) | async-done | bytes 147472 | tf_op jit(solution)/shard_map/reduce_scatter | solution.py:340
  374.3 55.4 %reduce-scatter.16.cloned.1.call-done = bf16[96,3072]{1,0:T(8,128)(2,1)} async-done(((bf16[768,3072]{1,0:T(8,128)(2,1)}), bf16[96,3072]{1,0:T(8,128)(2,1)}) %reduce-scatter.16.cloned.1.call-update) | async-done | bytes 589840 | tf_op jit(solution)/shard_map/reduce_scatter | solution.py:352
  429.7 55.5 %reduce-scatter.18.cloned.1.call-done = bf16[384,768]{1,0:T(8,128)(2,1)} async-done(((bf16[3072,768]{1,0:T(8,128)(2,1)}), bf16[384,768]{1,0:T(8,128)(2,1)}) %reduce-scatter.18.cloned.1.call-update) | async-done | bytes 589840 | tf_op jit(solution)/shard_map/reduce_scatter | solution.py:355
  486.0 10.3 %all-reduce.21 = (bf16[96]{0:T(256)(128)(2,1)S(1)}, bf16[96]{0:T(256)(128)(2,1)S(1)}, bf16[96]{0:T(256)(128)(2,1)S(1)}, bf16[384]{0:T(512)(128)(2,1)S(1)}, bf16[...) all-reduce(bf16[96]{0:T(256)(128)(2,1)S(1)} %dynamic-slice.9, ...), channel_id=1, replica_groups=mesh['narrow'=4,'wide'=8] {'narrow'}, use_global_device_ids=true, to_apply=%region_31.32 | all-reduce | flops 1632 | bytes 6528 | tf_op jit(solution)/shard_map/psum | solution.py:396
  504.5 37.3 %all-reduce.18 = (f32[64,8]{0,1:T(8,128)}, f32[8]{0:T(128)}, f32[12]{0:T(128)}) all-reduce(f32[64,8]{0,1:T(8,128)S(1)} %convolution_bitcast_fusion, f32[8]{0:T(128)S(1)} %fusion.68, f32[12]{0:T(128)S(1)} %get-tuple-element.194), channel_id=1, replica_groups=mesh['narrow'=4,'wide'=8] {'narrow','wide'}, use_global_device_ids=true, to_apply=%region_61.62 | all-reduce | flops 532 | bytes 4256 | tf_op jit(solution)/shard_map/psum | solution.py:417
  546.8 2.4 add_convert_fusion.1
  549.2 2.6 convolution_convert_fusion.2
  552.8 2.3 convert_element_type.326
  555.2 2.2 convert_element_type.328
  (327 shorter events, 73.7 us)
Async XLA Ops:
  7.2 44.7 %copy-start = (bf16[4,496,768]{2,1,0:T(8,128)(2,1)S(1)}, bf16[4,496,768]{2,1,0:T(8,128)(2,1)}, u32[]{:S(2)}) copy-start(bf16[4,496,768]{2,1,0:T(8,128)(2,1)} %param.28) | copy-start | bytes 9142276
  7.2 101.2 %all-gather.11.cloned.1.call-start = ((), (), s32[]{:S(2)}) async-start(), calls=%async_computation.7 | async-start | bytes 1327104 | tf_op jit(solution)/shard_map/all_gather | solution.py:89
  7.9 104.2 %all-gather.13.cloned.1.call-start = ((), (), s32[]{:S(2)}) async-start(), calls=%async_computation.8 | async-start | bytes 1327104 | tf_op jit(solution)/shard_map/all_gather | solution.py:90
  8.7 106.8 %all-gather.9.cloned.1.call-start = ((), (), s32[]{:S(2)}) async-start(), calls=%async_computation.6 | async-start | bytes 1327104 | tf_op jit(solution)/shard_map/all_gather | solution.py:91
  9.4 116.4 %all-gather.15.cloned.1.call-start = ((), (), s32[]{:S(2)}) async-start(), calls=%async_computation.9 | async-start | bytes 1327104 | tf_op jit(solution)/shard_map/all_gather | solution.py:92
  10.0 150.4 %all-gather.17.cloned.1.call-start = ((), (), s32[]{:S(2)}) async-start(), calls=%async_computation.10 | async-start | bytes 5308416 | tf_op jit(solution)/shard_map/all_gather | solution.py:93
  10.6 201.8 %all-gather.19.cloned.1.call-start = ((), (), s32[]{:S(2)}) async-start(), calls=%async_computation.11 | async-start | bytes 5308416 | tf_op jit(solution)/shard_map/all_gather | solution.py:94
  11.2 352.8 %reduce-scatter.14.cloned.1.call-start = ((), (), s32[]{:S(2)}) async-start(), calls=%async_computation.15 | async-start | bytes 1327104 | tf_op jit(solution)/shard_map/reduce_scatter | solution.py:349
  50.3 68.7 %copy-start.61 = (pred[4,128]{1,0:T(4,128)(4,1)}, pred[4,128]{1,0:T(4,128)(4,1)S(1)}, u32[]{:S(2)}) copy-start(pred[4,128]{1,0:T(4,128)(4,1)S(1)} %get-tuple-element.202) | copy-start | bytes 1540
  53.5 18.0 %copy-start.23 = (s32[1,4,128,128]{3,2,1,0:T(8,128)S(1)}, s32[1,4,128,128]{3,2,1,0:T(8,128)}, u32[]{:S(2)}) copy-start(s32[1,4,128,128]{3,2,1,0:T(8,128)} %get-tuple-element.195) | copy-start | bytes 786436
  53.5 18.0 %copy-start.24 = (s32[1,4,128,128]{3,2,1,0:T(8,128)S(1)}, s32[1,4,128,128]{3,2,1,0:T(8,128)}, u32[]{:S(2)}) copy-start(s32[1,4,128,128]{3,2,1,0:T(8,128)} %get-tuple-element.196) | copy-start | bytes 786436
  55.0 51.2 %copy-start.7 = (bf16[4,128,768]{1,2,0:T(8,128)(2,1)}, bf16[4,128,768]{1,2,0:T(8,128)(2,1)S(1)}, u32[]{:S(2)}) copy-start(bf16[4,128,768]{1,2,0:T(8,128)(2,1)S(1)} %copy.207) | copy-start | bytes 2359300
  72.0 20.1 %copy-start.70 = (bf16[384]{0:T(512)(128)(2,1)S(1)}, bf16[384]{0:T(512)(128)(2,1)}, u32[]{:S(2)}) copy-start(bf16[384]{0:T(512)(128)(2,1)} %param.40) | copy-start | bytes 2308
  72.0 34.3 %copy-start.44 = (f32[64,8]{0,1:T(8,128)S(1)}, f32[64,8]{0,1:T(8,128)}, u32[]{:S(2)}) copy-start(f32[64,8]{0,1:T(8,128)} %param.47) | copy-start | bytes 6148
  72.0 34.3 %copy-start.71 = (f32[8]{0:T(128)S(1)}, f32[8]{0:T(128)}, u32[]{:S(2)}) copy-start(f32[8]{0:T(128)} %param.48) | copy-start | bytes 100
  72.0 34.8 %copy-start.9 = (bf16[4,128,768]{2,1,0:T(8,128)(2,1)S(1)}, bf16[4,128,768]{2,1,0:T(8,128)(2,1)}, u32[]{:S(2)}) copy-start(bf16[4,128,768]{2,1,0:T(8,128)(2,1)} %param.50) | copy-start | bytes 2359300
  72.0 36.3 %copy-start.66 = (f32[12]{0:T(128)S(1)}, f32[12]{0:T(128)}, u32[]{:S(2)}) copy-start(f32[12]{0:T(128)} %param.49) | copy-start | bytes 148
  91.5 121.0 %copy-start.46 = (f32[768]{0:T(1024)}, f32[768]{0:T(1024)S(1)}, u32[]{:S(2)}) copy-start(f32[768]{0:T(1024)S(1)} %convert_element_type.287) | copy-start | bytes 9220
  128.6 83.9 %copy-start.41 = (f32[512]{0:T(512)}, f32[512]{0:T(512)S(1)}, u32[]{:S(2)}) copy-start(f32[512]{0:T(512)S(1)} %broadcast_multiply_fusion.4) | copy-start | bytes 6148
  212.4 7.0 %copy-start.10 = (bf16[4,128,768]{2,1,0:T(8,128)(2,1)S(1)}, bf16[4,128,768]{2,1,0:T(8,128)(2,1)}, u32[]{:S(2)}) copy-start(bf16[4,128,768]{2,1,0:T(8,128)(2,1)} %param.50) | copy-start | bytes 2359300
  220.6 11.2 %slice-start = ((s8[4718592]{0:T(1024)(128)(4,1)}), s8[4194304]{0:T(1024)(128)(4,1)S(1)}, s32[]{:S(2)}) async-start(s8[4718592]{0:T(1024)(128)(4,1)} %bitcast.224), calls=%async_computation.19 | async-start | bytes 8388608
  221.8 10.0 %copy-start.21 = (f32[512,768]{1,0:T(8,128)}, f32[512,768]{1,0:T(8,128)S(1)}, u32[]{:S(2)}) copy-start(f32[512,768]{1,0:T(8,128)S(1)} %get-tuple-element.187) | copy-start | bytes 4718596
  221.8 10.0 %copy-start.15 = (f32[512,768]{1,0:T(8,128)S(1)}, f32[512,768]{1,0:T(8,128)}, u32[]{:S(2)}) copy-start(f32[512,768]{1,0:T(8,128)} %copy-done.14) | copy-start | bytes 4718596
  221.8 10.0 %copy-start.42 = (f32[512]{0:T(512)S(1)}, f32[512]{0:T(512)}, u32[]{:S(2)}) copy-start(f32[512]{0:T(512)} %copy-done.41) | copy-start | bytes 6148
  221.8 10.0 %copy-start.47 = (f32[768]{0:T(1024)S(1)}, f32[768]{0:T(1024)}, u32[]{:S(2)}) copy-start(f32[768]{0:T(1024)} %copy-done.46) | copy-start | bytes 9220
  221.9 10.0 %copy-start.52 = (f32[512]{0:T(512)S(1)}, f32[512]{0:T(512)}, u32[]{:S(2)}) copy-start(f32[512]{0:T(512)} %add_rsqrt_fusion.1) | copy-start | bytes 6148
  221.9 10.0 %slice-start.1 = ((s8[4718592]{0:T(1024)(128)(4,1)}), s8[524288]{0:T(1024)(128)(4,1)S(1)}, s32[]{:S(2)}) async-start(s8[4718592]{0:T(1024)(128)(4,1)} %bitcast.224), calls=%async_computation.20 | async-start | bytes 1048576
  241.1 122.9 %reduce-scatter.10.cloned.1.call-start = ((), (), s32[]{:S(2)}) async-start(), calls=%async_computation.13 | async-start | bytes 1327104 | tf_op jit(solution)/shard_map/reduce_scatter | solution.py:343
  258.7 105.3 %reduce-scatter.12.cloned.1.call-start = ((), (), s32[]{:S(2)}) async-start(), calls=%async_computation.14 | async-start | bytes 1327104 | tf_op jit(solution)/shard_map/reduce_scatter | solution.py:346
  264.6 109.7 %reduce-scatter.8.cloned.1.call-start = ((), (), s32[]{:S(2)}) async-start(), calls=%async_computation.12 | async-start | bytes 1327104 | tf_op jit(solution)/shard_map/reduce_scatter | solution.py:340
  269.0 160.7 %reduce-scatter.16.cloned.1.call-start = ((), (), s32[]{:S(2)}) async-start(), calls=%async_computation.16 | async-start | bytes 5308416 | tf_op jit(solution)/shard_map/reduce_scatter | solution.py:352
  275.6 209.7 %reduce-scatter.18.cloned.1.call-start = ((), (), s32[]{:S(2)}) async-start(), calls=%async_computation.17 | async-start | bytes 5308416 | tf_op jit(solution)/shard_map/reduce_scatter | solution.py:355
  292.2 260.6 %all-reduce.25.cloned.1.call-start = ((), (), s32[]{:S(2)}) async-start(), calls=%async_computation.18 | async-start | bytes 3538944 | tf_op jit(solution)/shard_map/psum | solution.py:390
  293.1 41.3 %copy-start.51 = (bf16[768]{0:T(1024)(128)(2,1)S(1)}, bf16[768]{0:T(1024)(128)(2,1)}, u32[]{:S(2)}) copy-start(bf16[768]{0:T(1024)(128)(2,1)} %get-tuple-element.188) | copy-start | bytes 4612
  293.1 41.3 %copy-start.54 = (bf16[768]{0:T(1024)(128)(2,1)S(1)}, bf16[768]{0:T(1024)(128)(2,1)}, u32[]{:S(2)}) copy-start(bf16[768]{0:T(1024)(128)(2,1)} %get-tuple-element.127) | copy-start | bytes 4612
  293.1 41.3 %copy-start.55 = (bf16[768]{0:T(1024)(128)(2,1)S(1)}, bf16[768]{0:T(1024)(128)(2,1)}, u32[]{:S(2)}) copy-start(bf16[768]{0:T(1024)(128)(2,1)} %get-tuple-element.186) | copy-start | bytes 4612
  293.1 41.3 %copy-start.58 = (bf16[768]{0:T(1024)(128)(2,1)S(1)}, bf16[768]{0:T(1024)(128)(2,1)}, u32[]{:S(2)}) copy-start(bf16[768]{0:T(1024)(128)(2,1)} %copy-done.57) | copy-start | bytes 4612
  293.1 41.3 %copy-start.59 = (bf16[768]{0:T(1024)(128)(2,1)S(1)}, bf16[768]{0:T(1024)(128)(2,1)}, u32[]{:S(2)}) copy-start(bf16[768]{0:T(1024)(128)(2,1)} %get-tuple-element.123) | copy-start | bytes 4612
  293.1 41.3 %copy-start.60 = (bf16[3072]{0:T(1024)(128)(2,1)S(1)}, bf16[3072]{0:T(1024)(128)(2,1)}, u32[]{:S(2)}) copy-start(bf16[3072]{0:T(1024)(128)(2,1)} %get-tuple-element.217) | copy-start | bytes 18436
  293.1 41.3 %copy-start.68 = (bf16[768]{0:T(1024)(128)(2,1)S(1)}, bf16[768]{0:T(1024)(128)(2,1)}, u32[]{:S(2)}) copy-start(bf16[768]{0:T(1024)(128)(2,1)} %get-tuple-element.121) | copy-start | bytes 4612
  293.1 41.3 %copy-start.69 = (bf16[768]{0:T(1024)(128)(2,1)S(1)}, bf16[768]{0:T(1024)(128)(2,1)}, u32[]{:S(2)}) copy-start(bf16[768]{0:T(1024)(128)(2,1)} %get-tuple-element.126) | copy-start | bytes 4612
  293.1 68.5 %copy-start.37 = (f32[4,12,128]{2,1,0:T(8,128)S(1)}, f32[4,12,128]{2,1,0:T(8,128)}, u32[]{:S(2)}) copy-start(f32[4,12,128]{2,1,0:T(8,128)} %get-tuple-element.184) | copy-start | bytes 73732
  293.2 68.4 %copy-start.67 = (f32[12]{0:T(128)S(1)}, f32[12]{0:T(128)}, u32[]{:S(2)}) copy-start(f32[12]{0:T(128)} %param.49) | copy-start | bytes 148
  293.2 68.6 %copy-start.8 = (bf16[4,128,768]{1,2,0:T(8,128)(2,1)S(1)}, bf16[4,128,768]{1,2,0:T(8,128)(2,1)}, u32[]{:S(2)}) copy-start(bf16[4,128,768]{1,2,0:T(8,128)(2,1)} %copy-done.7) | copy-start | bytes 2359300
  293.2 69.3 %copy-start.45 = (f32[64,8]{0,1:T(8,128)S(1)}, f32[64,8]{0,1:T(8,128)}, u32[]{:S(2)}) copy-start(f32[64,8]{0,1:T(8,128)} %param.47) | copy-start | bytes 6148
  502.7 39.1 %copy-start.3 = (f32[512,768]{1,0:T(8,128)S(1)}, f32[512,768]{1,0:T(8,128)}, u32[]{:S(2)}) copy-start(f32[512,768]{1,0:T(8,128)} %copy-done.2) | copy-start | bytes 4718596
  504.4 38.7 %copy-start.26 = (bf16[4,128,12,64]{1,0,3,2:T(4,128)(2,1)S(1)}, bf16[4,128,12,64]{1,0,3,2:T(4,128)(2,1)}, u32[]{:S(2)}) copy-start(bf16[4,128,12,64]{1,0,3,2:T(4,128)(2,1)} %copy-done.25) | copy-start | bytes 2359300
  552.8 7.5 %copy-start.1 = (bf16[4,496,768]{2,1,0:T(8,128)(2,1)S(1)}, bf16[4,496,768]{2,1,0:T(8,128)(2,1)}, u32[]{:S(2)}) copy-start(bf16[4,496,768]{2,1,0:T(8,128)(2,1)} %param.28) | copy-start | bytes 9142276
  (44 other events, 109.0 us)
Sparse Core Ops, SparseCore 0:
  9.7 25.5 all-gather.10
  36.9 22.5 all-gather.12
  61.1 22.3 all-gather.8
  85.0 22.4 all-gather.14
  109.0 51.3 all-gather.16
  161.9 50.5 all-gather.18
  241.3 31.6 reduce-scatter.13
  275.9 30.9 reduce-scatter.9
  309.1 31.0 reduce-scatter.11
  342.9 31.3 reduce-scatter.7
  376.6 53.0 reduce-scatter.15
  431.9 53.3 reduce-scatter.17
  489.1 63.7 all-reduce.24
where the time goes:
time: 576 us; the launch traced here: 567 us
  waiting for transfers between devices  186 us (32%)
  matrix products  153 us (27%)
  blocking collectives  132 us (23%)
  local copies, waits for them, and re-layouts  43 us (7%)
  other arithmetic  33.7 us (6%)
  between operations  17.7 us (3%)
    unnamed x2, blocking collectives  57.6 us
    reduce_scatter x1, waiting for transfers between devices, body(): lax.psum_scatter(down_weight_grad.astype(jnp.bfloat16), 'wide', scatter_d...  55.5 us
    reduce_scatter x1, waiting for transfers between devices, body(): lax.psum_scatter(up_weight_grad.astype(jnp.bfloat16), 'wide', scatter_dim...  55.4 us
    dot_general x4, matrix products, clip_table_grad(): return jnp.einsum('pb,ph->bh', onehot, clip_grad, precision=highest)  40.8 us
    dot_general x6, matrix products, project(): return jnp.dot(inputs, matrix, preferred_element_type=jnp.float32)  37.5 us
    psum x1, blocking collectives, body(): lax.psum((gate_weight_grad, gate_bias_grad, gate_scale_grad), ('narrow',...  37.3 us
    all_gather x1, waiting for transfers between devices, body(): lax.all_gather(down_weight, 'wide', axis=0, tiled=True)  30.3 us
    all_gather x1, waiting for transfers between devices, body(): lax.all_gather(up_weight, 'wide', axis=0, tiled=True)  29.8 us
  transfers between devices with their start and end apart: 13, of which 6 were waited for; matrix products, arithmetic and copies ran while one was open for 33% of the time, Pallas kernels for 0%

commit v1 on v0

v1 whole, which is shorter than its diff:
```python
from functools import partial
import math

import jax
import jax.numpy as jnp
import numpy as np
from jax import lax
from jax.experimental import pallas as pl
from jax.experimental.pallas import tpu as pltpu
from jax.sharding import PartitionSpec as P

NUM_BUCKETS = 320
SPAN = 512
SPARE = 4
MOST = 51
HIGHEST = lax.Precision.HIGHEST
ALPHA = math.pow(24.0, 0.25)
EPS = 1e-05
F32 = jnp.float32
BF16 = jnp.bfloat16
NN = (((1,), (0,)), ((), ()))
NT = (((1,), (1,)), ((), ()))
TN = (((0,), (0,)), ((), ()))


def dot(a, b, dims=NN, precision=None):
    return lax.dot_general(a, b, dims, precision=precision, preferred_element_type=F32)


def params(need=0, *semantics):
    extra = dict(dimension_semantics=semantics) if semantics else {}
    need = need if need > 50 else min(need + SPARE, MOST) if need else MOST
    return pltpu.CompilerParams(vmem_limit_bytes=need * 1024 * 1024, **extra)


def size_of(x):
    shape = list(x.shape)
    shape[-1] = -(-shape[-1] // 128) * 128
    if len(shape) > 1:
        shape[-2] = -(-shape[-2] // 8) * 8
    return math.prod(shape) * jnp.dtype(x.dtype).itemsize


def cost(us):
    return pl.CostEstimate(
        flops=int(us * 1e10), bytes_accessed=int(us * 3.5e7), transcendentals=0
    )


def sds(shape, dtype):
    return jax.ShapeDtypeStruct(shape, dtype)


def relative_buckets():
    place = np.arange(2 * SPAN)
    relative = np.where(place < SPAN, -place, 2 * SPAN - place)
    distance = np.abs(relative)
    ratio = np.log(np.maximum(distance, 1) / 80.0) / math.log(10.0)
    beyond = np.minimum(80 + np.floor(ratio * 80.0).astype(np.int64), 159)
    bucket = np.where(relative > 0, 160, 0) + np.where(distance < 80, distance, beyond)
    return bucket.astype(np.int32)


SMEM = pl.BlockSpec(memory_space=pltpu.SMEM)
VMEM = pl.BlockSpec(memory_space=pltpu.VMEM)
ANY = pl.BlockSpec(memory_space=pl.ANY)


def call(kernel, name, us, out_shape, args, kinds, scratch=(), after=(), out_kinds=None, large=None):
    count = len(args)
    spaces = dict(s=SMEM, v=VMEM, a=ANY, p=VMEM)
    args = [pinned(x) if kind == "p" else x for x, kind in zip(args, kinds)]

    def run(*refs):
        kernel(*refs[:count], *refs[count + len(after) :])

    extra = {}
    outs = jax.tree.leaves(out_shape)
    if out_kinds:
        extra["out_specs"] = [spaces[k] for k in out_kinds]
    else:
        out_kinds = "v" * len(outs)
    held = [x for x, kind in zip([*args, *outs], kinds + out_kinds) if kind == "v"]
    held += [x for x in scratch if hasattr(x, "shape") and hasattr(x, "dtype")]
    held = [x for x in held if "sem" not in str(x.dtype)]
    return pl.pallas_call(
        run,
        in_specs=[spaces[k] for k in kinds] + [ANY] * len(after),
        out_shape=out_shape,
        scratch_shapes=list(scratch),
        compiler_params=params(large or sum(map(size_of, held)) >> 20),
        name=name,
        cost_estimate=cost(us),
        **extra,
    )(*args, *after)


def pinned(x):
    return pltpu.with_memory_space_constraint(x, pltpu.VMEM)


def hold(x, after, pin=False):
    def nothing(*refs):
        pass

    space = VMEM if pin else ANY
    return pl.pallas_call(
        nothing,
        in_specs=[space] + [ANY] * len(after),
        out_specs=space,
        out_shape=sds(x.shape, x.dtype),
        input_output_aliases={0: 0},
        name="hold",
        cost_estimate=cost(0.1),
    )(pinned(x) if pin else x, *after)


def lanes_of(shape):
    return lax.broadcasted_iota(jnp.int32, shape, len(shape) - 1)


def lines_of(shape):
    return lax.broadcasted_iota(jnp.int32, shape, len(shape) - 2)


def chosen_rows(order, visible, c, rows):
    slots = order[:, :rows]
    slots = jnp.sum(jnp.where(lines_of(slots.shape) == c, slots, 0), 0, keepdims=True)
    return jnp.where(lanes_of((1, rows)) < visible[c], slots, -1)


def one_hot(order, visible, c, rows, patches):
    slots = chosen_rows(order, visible, c, rows)
    return jnp.where(lines_of((patches, rows)) == slots, 1.0, 0.0).astype(BF16)


def widen(block, width):
    lines, lanes = block.shape
    return jnp.concatenate([block, jnp.zeros((lines, width - lanes), block.dtype)], 1)


def small_block(lines, table, width):
    heads = table.shape[0]
    table = jnp.concatenate([widen(table, 128), jnp.zeros((16 - heads, 128), F32)], 0)
    block = jnp.concatenate([lines, table], 1)
    return widen(block, width) if width > 256 else block


def first_kernel(where, query, key, value, out, *refs):
    vectors, up_b, table = refs[:8], refs[8], refs[9]
    own, quarter = refs[10:]
    share, width = query.shape
    for j, weight in enumerate((query, key, value, out)):
        own[j] = weight[...]
    quarter[:share, :] = own[where[0]]
    lines = [widen(v[...].astype(F32), 128) for v in vectors]
    for j in range(4):
        lines.append(widen(up_b[...].astype(F32)[:, j * share : (j + 1) * share], 128))
    lines.append(jnp.zeros((4, 128), F32))
    small = small_block(jnp.concatenate(lines, 0), table[...].astype(F32), width)
    quarter[share:, :] = small.astype(BF16)


def first_blocks(where, weights, vectors, up_b, table):
    share, width = weights[0].shape
    return call(
        first_kernel,
        "first_blocks",
        3,
        [sds((4, share, width), BF16), sds((share + 16, width), BF16)],
        [where, *weights, *vectors, up_b, table],
        "s" + "v" * 14,
        large=56,
    )


def up_blocks_kernel(where, up, own, quarter):
    width = quarter.shape[1]
    for j in range(4):
        own[j] = up[:, j * width : (j + 1) * width]
    quarter[...] = own[where[0]]


def up_blocks(where, up, width, after=()):
    share = up.shape[0]
    return call(
        up_blocks_kernel,
        "up_blocks",
        2,
        [sds((4, share, width), BF16), sds((share, width), BF16)],
        [where, up],
        "sv",
        after=after,
    )


def first_column_kernel(own, one, two, three, down, blocks, smalls, down_out, sem):
    share = blocks.shape[2]
    copy = pltpu.make_async_copy(down, down_out, sem)
    copy.start()
    for k, quarter in enumerate((own, one, two, three)):
        smalls[k] = quarter[share:, :]
        if k:
            for place in range(4):
                blocks[place, k - 1] = quarter[:share, :]
    copy.wait()


def first_column(own, arrived, down, after=()):
    share, width = own.shape[0] - 16, own.shape[1]
    return call(
        first_column_kernel,
        "first_column",
        2,
        [sds((4, 3, share, width), BF16), sds((4, 16, width), BF16), sds(down.shape, BF16)],
        [own, *arrived, down],
        "vvvva",
        [pltpu.SemaphoreType.DMA],
        after,
        "vva",
    )


def up_column_kernel(one, two, three, blocks):
    for k, quarter in enumerate((one, two, three)):
        for copy in range(4):
            blocks[copy, k] = quarter[...]


def up_column(arrived, after=()):
    return call(
        up_column_kernel,
        "up_column",
        2,
        sds((4, 3) + arrived[0].shape, BF16),
        arrived,
        "vvv",
        after=after,
    )


def gate_spread(gate_weight, width):
    half = gate_weight.shape[0] // 2
    size = gate_weight.shape[1]
    values = gate_weight[...]
    own = lanes_of((16, width)) // size == lines_of((16, width))
    spread = []
    for i in range(2):
        line = jnp.sum(values[i * half : (i + 1) * half], 0, keepdims=True)
        line = widen(line, 128)
        line = line + pltpu.roll(line, size, 1)
        line = jnp.concatenate([line] * (width // 128), 1)
        spread.append(jnp.where(own, line, 0.0))
    return jnp.concatenate(spread, 0)


def scale_lines(gate_scale, lanes):
    line = lines_of((16, lanes))
    scale = jnp.zeros((16, lanes), F32)
    for h in range(gate_scale.shape[0]):
        scale = jnp.where(line == h, gate_scale[h], scale)
    return scale


def pick_kernel(
    order, visible, gate_bias, gate_scale, tokens, gate_weight, token, picked, first, second, value,
    spread
):
    clip = pl.program_id(0)
    patches, width = tokens.shape[1:]
    rows = picked.shape[0]

    @pl.when(clip == 0)
    def _():
        spread[...] = gate_spread(gate_weight, width)

    chosen = dot(one_hot(order, visible, clip, rows, patches), tokens[0], TN)
    picked[...] = chosen.astype(BF16)
    logits = dot(spread[...], chosen, NT, HIGHEST)
    half = gate_bias.shape[0] // 2
    one = jax.nn.sigmoid(logits[:16] + sum(gate_bias[f] for f in range(half)))
    two = jax.nn.sigmoid(logits[16:] + sum(gate_bias[f + half] for f in range(half)))
    first[0] = one
    second[0] = two
    value[0] = one * (two * scale_lines(gate_scale, rows) - 1.0) + 2.0


def pick(order, visible, gate_bias, gate_scale, tokens, gate_weight, rows, after):
    clips, patches, width = tokens.shape
    whole = lambda *s: pl.BlockSpec(s, lambda c: (0,) * len(s))
    gate = pl.BlockSpec((1, 16, rows), lambda c: (c, 0, 0))
    return pl.pallas_call(
        pick_kernel,
        grid=(clips,),
        in_specs=[
            whole(*order.shape),
            SMEM,
            SMEM,
            SMEM,
            pl.BlockSpec((1, patches, width), lambda c: (c, 0, 0)),
            whole(*gate_weight.shape),
            ANY,
        ],
        out_specs=[pl.BlockSpec((rows, width), lambda c: (c, 0)), gate, gate, gate],
        out_shape=[sds((clips * rows, width), BF16)] + [sds((clips, 16, rows), F32)] * 3,
        scratch_shapes=[pltpu.VMEM((32, width), F32)],
        compiler_params=params(0, "arbitrary"),
        name="pick",
        cost_estimate=cost(6),
    )(order, visible, gate_bias, gate_scale, tokens, gate_weight, after)


def position_kernel(
    where, order, visible, buckets, *refs
):
    mine, other, out, vectors, held, levels, toeplitz, select = refs
    clips, pairs, rows = out.shape[:3]
    heads = 2 * pairs
    width = vectors.shape[1]
    share = width // 8
    held[0] = mine[...]
    held[1] = other[...]
    shards = [
        held[where[2] ^ (w % 2), where[1] ^ (w // 2)].astype(F32) for w in range(8)
    ]
    lane = lanes_of((16, 128))
    rows_of = [widen(jnp.where(lane < share, shard[:, :128], 0.0), width) for shard in shards]
    total = rows_of[0]
    for w in range(1, 8):
        total += pltpu.roll(rows_of[w], share * w, 1)
    vectors[0:8, :] = total[:8]
    chunk = []
    for k in range(4):
        line = jnp.zeros((1, width), F32)
        for half in range(2):
            for j in range(4):
                turn = 4 * share * half + share * j
                piece = rows_of[2 * k + half][8 + j : 9 + j]
                line += pltpu.roll(piece, turn, 1) if turn else piece
        chunk.append(line)
    vectors[8:16, :] = jnp.concatenate(chunk + [jnp.zeros((4, width), F32)], 0)
    count = NUM_BUCKETS // 8
    table = jnp.zeros((16, 384), F32)
    for w, shard in enumerate(shards):
        piece = widen(jnp.where(lane < count, shard[:, 128:256], 0.0), 384)
        table += pltpu.roll(piece, count * w, 1) if w else piece
    ids = lines_of((384, 2 * SPAN))
    onehot = jnp.where(ids == buckets[...], 1.0, 0.0).astype(BF16)
    levels[...] = dot(table.astype(BF16), onehot)
    for c in range(clips):
        select[:, c * rows : (c + 1) * rows] = one_hot(order, visible, c, rows, SPAN)

    def pair_step(pair, carry):
        for half in range(2):
            level = levels[pl.ds(2 * pair + half, 1), :]
            base = pltpu.roll(
                jnp.broadcast_to(level, (8, 2 * SPAN)), 0, 1, stride=1, stride_axis=0
            )
            for k in range(0, 16, 2):
                low = pltpu.roll(base, 8 * k, 1) if k else base
                block = jnp.concatenate([low, pltpu.roll(base, 8 * k + 8, 1)], 0).astype(BF16)
                for m in range(SPAN // 128):
                    for t in range(SPAN // 128):
                        source = ((t - m) % (SPAN // 64)) * 128
                        toeplitz[pl.ds(128 * m + 8 * k, 16), pl.ds(128 * t, 128)] = block[
                            :, source : source + 128
                        ]
            lines = dot(select[...], toeplitz[...], TN).astype(BF16)
            for c in range(clips):
                cut = slice(c * rows, (c + 1) * rows)
                out[c, pair, :, half * rows : (half + 1) * rows] = dot(
                    lines[cut], select[:, cut]
                ).astype(BF16)
        return carry

    lax.fori_loop(0, pairs, pair_step, 0)


def positions(where, order, visible, smalls, clips, rows, pairs, width):
    buckets = jnp.asarray(relative_buckets()[None, :])
    return call(
        position_kernel,
        "position",
        11,
        [sds((clips, pairs, rows, 2 * rows), BF16), sds((16, width), F32)],
        [where, order, visible, buckets, *smalls],
        "svsv" + "v" * 2,
        [
            pltpu.VMEM((2, 4, 16, width), BF16),
            pltpu.VMEM((16, 2 * SPAN), F32),
            pltpu.VMEM((SPAN, SPAN), BF16),
            pltpu.VMEM((SPAN, clips * rows), BF16),
        ],
        large=MOST,
    )


def two_heads(block):
    lane = lax.broadcasted_iota(jnp.int32, block.shape, 1)
    zero = jnp.zeros_like(block)
    half = block.shape[1] // 2
    return jnp.concatenate(
        [jnp.where(lane < half, block, zero), jnp.where(lane < half, zero, block)], 0
    )


def one_block(stacked):
    rows = stacked.shape[0] // 2
    lane = lax.broadcasted_iota(jnp.int32, (rows, stacked.shape[1]), 1)
    return jnp.where(lane < stacked.shape[1] // 2, stacked[:rows], stacked[rows:])


def unit_norm(values):
    center = values - jnp.mean(values, -1, keepdims=True)
    inverse = lax.rsqrt(jnp.mean(center * center, -1, keepdims=True) + EPS)
    return center * inverse, inverse


def load_squares(where, mine, other, weights, sem):
    share = weights.shape[1] // 8
    started = []

    def start(source, quarter, shard):
        line = pl.ds(pl.multiple_of(shard * share, share), share)
        copy = pltpu.make_async_copy(source, weights.at[quarter, line, :], sem)
        copy.start()
        started.append(copy)

    for side, (own, plane) in enumerate((mine, other)):
        core = where[2] ^ side
        for j in range(4):
            start(own.at[j], j, where[1] * 2 + core)
            for k in range(1, 4):
                start(plane.at[j, k - 1], j, (where[1] ^ k) * 2 + core)
    return started


def finish(copies):
    for copy in copies:
        copy.wait()


def attend_kernel(where, visible, picked, gates, position, vectors, *refs):
    mine, other = refs[:2], refs[2:4]
    query, key, value, soft, mixed, unit, inverse, normed, normed_low, weights, sem = refs[4:]
    clips, pairs, rows = position.shape[:3]
    finish(load_squares(where, mine, other, weights, sem))
    query_b, value_b, out_b = vectors[0:1, :], vectors[1:2, :], vectors[2:3, :]
    gain, shift = vectors[4:5, :], vectors[5:6, :]
    x = picked[...]
    query[...] = ((dot(x, weights[0]) + query_b).astype(BF16).astype(F32) * 0.125).astype(BF16)
    key[...] = dot(x, weights[1]).astype(BF16)
    value[...] = (dot(x, weights[2]) + value_b).astype(BF16)

    def clip_step(c, carry):
        cut = pl.ds(pl.multiple_of(c * rows, rows), rows)
        live = lines_of((rows, 2 * rows)) < visible[c]
        for pair in range(pairs):
            lanes = pl.ds(128 * pair, 128)
            scores = dot(key[cut, lanes], two_heads(query[cut, lanes]), NT)
            gate = jnp.concatenate(
                [gates[c, 2 * pair : 2 * pair + 1, :], gates[c, 2 * pair + 1 : 2 * pair + 2, :]], 1
            )
            scores = scores + gate * position[c, pair].astype(F32)
            scores = jnp.where(live, scores, -1000000000.0)
            exps = jnp.exp(scores - jnp.max(scores, 0, keepdims=True))
            exps = exps * (1.0 / jnp.sum(exps, 0, keepdims=True))
            low = exps.astype(BF16)
            soft[c, pair] = exps
            mixed[cut, lanes] = one_block(dot(low, value[cut, lanes], TN)).astype(BF16)
        return carry

    lax.fori_loop(0, clips, clip_step, 0)
    attended = dot(mixed[...], weights[3]) + out_b
    units, inv = unit_norm(ALPHA * x.astype(F32) + attended)
    unit[...] = units
    inverse[...] = inv
    result = units * gain + shift
    normed[...] = result
    normed_low[...] = result.astype(BF16)


def attend(where, visible, picked, gates, position, vectors, mine, other, after=()):
    clips, pairs, rows = position.shape[:3]
    total, width = picked.shape
    flat = sds((total, width), BF16)
    wide = sds((total, width), F32)
    return call(
        attend_kernel,
        "attend",
        14,
        [
            flat,
            flat,
            flat,
            sds((clips, pairs, rows, 2 * rows), F32),
            flat,
            wide,
            sds((total, 1), F32),
            wide,
            flat,
            sds((4, width, width), BF16),
        ],
        [where, visible, picked, gates, position, vectors, *mine, *other],
        "ssvvvv" + "a" * 4,
        [pltpu.SemaphoreType.DMA],
        after,
        large=MOST,
    )


def gelu_parts(x):
    size = jnp.abs(x) * (1.0 / math.sqrt(2.0))
    t = 1.0 / (1.0 + 0.3275911 * size)
    fall = jnp.exp(-0.5 * x * x)
    series = t * (
        0.5 * 0.254829592
        + t
        * (
            0.5 * -0.284496736
            + t * (0.5 * 1.421413741 + t * (0.5 * -1.453152027 + t * (0.5 * 1.061405429)))
        )
    )
    tail = series * fall
    below = jnp.where(x >= 0.0, 1.0 - tail, tail)
    return x * below, below + x * fall * (1.0 / math.sqrt(2.0 * math.pi))


def norm_back(grad, unit, inverse, gain):
    scaled = grad * gain
    return inverse * (
        scaled
        - jnp.mean(scaled, -1, keepdims=True)
        - unit * jnp.mean(scaled * unit, -1, keepdims=True)
    )


UPROWS = 256


def feed_kernel(where, visible, normed_low, normed, vectors, cotangent, *refs):
    ups, down = (refs[0:2], refs[2:4]), refs[4]
    down_keep, down_send, up_out, output, grad_normed, up_b_grad, sums = refs[5:12]
    (
        up_w, down_w, active, slope, branch, grad_branch, down_parts, up_parts, up_sem, down_sem,
        down_done, up_done,
    ) = refs[12:]
    chunks, rows, width = slope.shape
    share = width // 8
    clips = visible.shape[0]
    block = rows // clips
    depth, core = where[1], where[2]
    up_copies = load_squares(where, *ups, up_w, up_sem)
    down_copies = [pltpu.make_async_copy(down, down_w, down_sem)]
    down_copies[0].start()
    finish(up_copies)

    def up_step(k, carry):
        bias = vectors[pl.ds(8 + k, 1), :]
        parts = [
            dot(normed_low[r : r + UPROWS, :], up_w[k]) for r in range(0, rows, UPROWS)
        ]
        for i, part in enumerate(parts):
            activated, derivative = gelu_parts(part + bias)
            active[k, i * UPROWS : (i + 1) * UPROWS, :] = activated.astype(BF16)
            slope[k, i * UPROWS : (i + 1) * UPROWS, :] = derivative
        return carry

    lax.fori_loop(0, chunks, up_step, 0)
    finish(down_copies)
    total = dot(active[0], down_w[0])
    for k in range(1, chunks):
        total += dot(active[k], down_w[k])
    branch[...] = total
    gain, shift = vectors[6:7, :], vectors[7:8, :]
    sums[...] = jnp.zeros_like(sums)

    def norm_step(c, carry):
        cut = pl.ds(pl.multiple_of(c * block, block), block)
        units, inv = unit_norm(ALPHA * normed[cut, :] + branch[cut, :] + vectors[3:4, :])
        alive = jnp.where(lines_of((block, width)) < visible[c], 1.0, 0.0)
        output[cut, :] = ((units * gain + shift) * alive).astype(BF16)
        grad = cotangent[cut, :].astype(F32) * alive
        pre = norm_back(grad, units, inv, gain)
        grad_normed[cut, :] = ALPHA * pre
        low = pre.astype(BF16)
        grad_branch[cut, :] = low
        sums[0:1, :] += jnp.sum(grad * units, 0, keepdims=True)
        sums[1:2, :] += jnp.sum(grad, 0, keepdims=True)
        sums[2:3, :] += jnp.sum(low.astype(F32), 0, keepdims=True)
        return carry

    lax.fori_loop(0, clips, norm_step, 0)
    up_b_grad[...] = jnp.zeros_like(up_b_grad)
    down_out = lambda k: [
        pltpu.make_async_copy(down_parts.at[0, :, k], down_keep.at[:, k], down_done),
        pltpu.make_async_copy(down_parts.at[1, :, k], down_send.at[:, k], down_done),
    ]
    up_copy = lambda k: [
        pltpu.make_async_copy(
            up_parts.at[k], up_out.at[:, pl.ds(pl.multiple_of(k * width, width), width)], up_done
        )
    ]

    def down_step(k, carry):
        grad = dot(active[k], grad_branch[...], TN).astype(BF16)
        place = depth ^ k
        for side in range(2):
            for j in range(4):
                line = 4 * share * side + share * j
                down_parts[core ^ side, j, place] = grad[line : line + share]
        for copy in down_out(place):
            copy.start()
        return carry

    lax.fori_loop(0, chunks, down_step, 0)

    def up_back_step(k, carry):
        grad_hidden = dot(grad_branch[...], down_w[k], NT) * slope[k]
        grad_hidden = grad_hidden.astype(BF16)
        up_b_grad[pl.ds(k, 1), :] = jnp.sum(grad_hidden.astype(F32), 0, keepdims=True)
        up_parts[k] = dot(normed_low[...], grad_hidden, TN).astype(BF16)
        for copy in up_copy(k):
            copy.start()
        grad_normed[...] += dot(grad_hidden, up_w[k], NT)
        return carry

    lax.fori_loop(0, chunks, up_back_step, 0)
    for k in range(4):
        finish(down_out(k))
        finish(up_copy(k))


def feed(where, visible, normed_low, normed, vectors, cotangent, ups, down, after=()):
    rows, width = normed.shape
    chunks = 4
    part = sds((4, 4, width // 8, width), BF16)
    deep = pltpu.VMEM((chunks, width, width), BF16)
    long = pltpu.VMEM((chunks, rows, width), BF16)
    parts = pltpu.VMEM((2,) + part.shape, BF16)
    args = [where, visible, normed_low, normed, vectors, cotangent, *ups[0], *ups[1], down]
    return call(
        feed_kernel,
        "feed",
        32,
        [
            part,
            part,
            sds((width, chunks * width), BF16),
            sds((rows, width), BF16),
            sds((rows, width), F32),
            sds((8, width), F32),
            sds((8, width), F32),
        ],
        args,
        "ssvvvv" + "a" * 5,
        [
            deep,
            deep,
            long,
            pltpu.VMEM((chunks, rows, width), F32),
            pltpu.VMEM((rows, width), F32),
            pltpu.VMEM((rows, width), BF16),
            parts,
            deep,
        ]
        + [pltpu.SemaphoreType.DMA] * 4,
        after,
        "aaavvvv",
        large=MOST,
    )


def place_square(where, j, block, keep, send):
    share = block.shape[0] // 8
    core = where[2]
    for z in range(4):
        for side, target in ((core, keep), (1 - core, send)):
            line = pl.multiple_of(share * (2 * z + side), share)
            target[j, where[1] ^ z] = block[pl.ds(line, share), :]


def mix_back_kernel(
    grad_normed, unit, inverse, vectors, mixed, weights, grad_pre, out_grad, grad_mixed, sums
):
    width = grad_normed.shape[1]
    grad = grad_normed[...]
    units = unit[...]
    pre = norm_back(grad, units, inverse[...], vectors[4:5, :])
    grad_pre[...] = ALPHA * pre
    low = pre.astype(BF16)
    sums[0:1, :] = jnp.sum(grad * units, 0, keepdims=True)
    sums[1:2, :] = jnp.sum(grad, 0, keepdims=True)
    sums[2:3, :] = jnp.sum(low.astype(F32), 0, keepdims=True)
    sums[3:8, :] = jnp.zeros((5, width), F32)
    out_grad[...] = dot(mixed[...], low, TN).astype(BF16)
    grad_mixed[...] = dot(low, weights[0], NT).astype(BF16)


def mix_back(grad_normed, unit, inverse, vectors, mixed, weights, after=()):
    total, width = grad_normed.shape

    def run(*refs):
        mix_back_kernel(*refs[:6], *refs[6 + len(after) :])

    whole = lambda x: pl.BlockSpec(x.shape, lambda i: (0,) * len(x.shape))
    outs = [
        sds((total, width), F32),
        sds((width, width), BF16),
        sds((total, width), BF16),
        sds((8, width), F32),
    ]
    return pl.pallas_call(
        run,
        grid=(1,),
        in_specs=[whole(x) for x in (grad_normed, unit, inverse, vectors, mixed)]
        + [pl.BlockSpec((1, width, width), lambda i: (3, 0, 0))]
        + [ANY] * len(after),
        out_specs=[whole(x) for x in outs],
        out_shape=outs,
        compiler_params=params(),
        name="mix_back",
        cost_estimate=cost(6),
    )(grad_normed, unit, inverse, vectors, mixed, weights, *after)


def attend_back_kernel(
    where, grad_mixed, out_grad, picked, query, key, value, soft, position, gates, *refs
):
    keep, send, grad_query, grad_key, grad_value, grad_gate, gated_scores, sums = refs[-12:-4]
    queries, keys, values, block = refs[-4:]
    pairs, rows = position.shape[1:3]
    width = picked.shape[1]
    clip = pl.program_id(0)
    cut = pl.ds(pl.multiple_of(clip * rows, rows), rows)
    for pair in range(pairs):
        lanes = pl.ds(128 * pair, 128)
        weights = soft[0, pair]
        weights_low = weights.astype(BF16)
        back = two_heads(grad_mixed[:, lanes])
        grad_soft = dot(value[:, lanes], back, NT)
        grad_value[:, lanes] = dot(weights_low, back).astype(BF16)
        carried = jnp.sum(grad_soft * weights, 0, keepdims=True)
        low_scores = (weights * (grad_soft - carried)).astype(BF16)
        scores = low_scores.astype(F32)
        grad_key[:, lanes] = dot(low_scores, two_heads(query[:, lanes])).astype(BF16)
        grad_query[:, lanes] = (one_block(dot(low_scores, key[:, lanes], TN)) * 0.125).astype(BF16)
        gate = jnp.concatenate(
            [gates[0, 2 * pair : 2 * pair + 1, :], gates[0, 2 * pair + 1 : 2 * pair + 2, :]], 1
        )
        by_gate = jnp.sum(scores * position[0, pair].astype(F32), 0, keepdims=True)
        grad_gate[0, 2 * pair : 2 * pair + 1, :] = by_gate[:, :rows]
        grad_gate[0, 2 * pair + 1 : 2 * pair + 2, :] = by_gate[:, rows:]
        gated_scores[0, pair] = (scores * gate).astype(BF16)
    grad_gate[0, 2 * pairs :, :] = jnp.zeros((16 - 2 * pairs, rows), F32)
    queries[cut, :] = grad_query[...]
    keys[cut, :] = grad_key[...]
    values[cut, :] = grad_value[...]

    @pl.when(clip == pl.num_programs(0) - 1)
    def _():
        sums[0:1, :] = jnp.sum(queries[...].astype(F32), 0, keepdims=True)
        sums[1:2, :] = jnp.sum(values[...].astype(F32), 0, keepdims=True)
        sums[2:8, :] = jnp.zeros((6, width), F32)
        x = picked[...]
        for j, grad in enumerate((queries, keys, values)):
            block[...] = dot(x, grad[...], TN).astype(BF16)
            place_square(where, j, block, keep, send)
        place_square(where, 3, out_grad, keep, send)


def attend_back(
    where, grad_mixed, out_grad, picked, query, key, value, soft, position, gates, after=()
):
    clips, pairs, rows = position.shape[:3]
    total, width = picked.shape
    flat = sds((total, width), BF16)
    part = sds((4, 4, width // 8, width), BF16)
    whole = lambda *s: pl.BlockSpec(s, lambda c: (0,) * len(s))
    lines = pl.BlockSpec((rows, width), lambda c: (c, 0))
    square = pl.BlockSpec((1, pairs, rows, 2 * rows), lambda c: (c, 0, 0, 0))
    gate = pl.BlockSpec((1, 16, rows), lambda c: (c, 0, 0))
    return pl.pallas_call(
        attend_back_kernel,
        grid=(clips,),
        in_specs=[
            SMEM,
            lines,
            whole(width, width),
            whole(total, width),
            lines,
            lines,
            lines,
            square,
            square,
            gate,
        ]
        + [ANY] * len(after),
        out_specs=[
            whole(*part.shape),
            whole(*part.shape),
            lines,
            lines,
            lines,
            gate,
            square,
            whole(8, width),
        ],
        out_shape=[
            part,
            part,
            flat,
            flat,
            flat,
            sds((clips, 16, rows), F32),
            sds(position.shape, BF16),
            sds((8, width), F32),
        ],
        scratch_shapes=[pltpu.VMEM((total, width), BF16)] * 3
        + [pltpu.VMEM((width, width), BF16)],
        compiler_params=params(0, "arbitrary"),
        name="attend_back",
        cost_estimate=cost(15),
    )(
        where, grad_mixed, out_grad, picked, query, key, value, soft, position, gates, *after
    )


def table_kernel(order, visible, gated, out, select, picks):
    clips, pairs, rows = gated.shape[:3]
    heads, total = 2 * pairs, clips * rows
    for c in range(clips):
        select[:, c * rows : (c + 1) * rows] = one_hot(order, visible, c, rows, SPAN)
    out[...] = jnp.zeros_like(out)

    def pair_step(pair, carry):
        for half in range(2):
            for c in range(clips):
                cut = slice(c * rows, (c + 1) * rows)
                block = gated[c, pair, :, half * rows : (half + 1) * rows]
                picks[cut, :] = dot(block, select[:, cut], NT).astype(BF16)
            sums = dot(select[...], picks[...])
            base = None
            for k in range(16):
                parts = []
                for t in range(SPAN // 64):
                    part = None
                    for m in range(SPAN // 128):
                        column = (t + m) % (SPAN // 64)
                        if column < SPAN // 128:
                            line = 128 * m + 8 * k
                            block = sums[line : line + 8, 128 * column : 128 * column + 128]
                            part = block if part is None else part + block
                    parts.append(jnp.zeros((8, 128), F32) if part is None else part)
                line = jnp.concatenate(parts, 1)
                line = pltpu.roll(line, 2 * SPAN - 8 * k, 1) if k else line
                base = line if base is None else base + line
            level = base[0:1, :]
            for r in range(1, 8):
                level = level + pltpu.roll(base[r : r + 1, :], 2 * SPAN - r, 1)
            out[pl.ds(2 * pair + half, 1), :] = level
        return carry

    lax.fori_loop(0, pairs, pair_step, 0)


def table_levels(order, visible, gated, after=()):
    total = gated.shape[0] * gated.shape[2]
    return call(
        table_kernel,
        "table_back",
        12,
        sds((16, 2 * SPAN), F32),
        [order, visible, gated],
        "vsv",
        [pltpu.VMEM((SPAN, total), BF16), pltpu.VMEM((total, SPAN), BF16)],
        after,
        large=MOST,
    )


def tokens_kernel(
    order, visible, gate_scale, grad_pre, grad_query, grad_key, grad_value, weights, picked, first,
    second, grad_gate, gate_weight, tokens_grad, gate_sums, gate_mix, grad_picked
):
    clips, patches = tokens_grad.shape[:2]
    total, width = picked.shape
    rows = total // clips
    spread = gate_spread(gate_weight, width)
    scale = scale_lines(gate_scale, rows)
    logits = []
    by_scale = jnp.zeros((16, rows), F32)
    for c in range(clips):
        one, two, grad = first[c], second[c], grad_gate[c]
        by_scale += grad * one * two
        logits.append(
            jnp.concatenate(
                [
                    grad * (two * scale - 1.0) * one * (1.0 - one),
                    grad * one * scale * two * (1.0 - two),
                ],
                0,
            )
        )
    logits = jnp.concatenate(logits, 1)
    gate_sums[...] = jnp.zeros_like(gate_sums)
    gate_sums[0:8, 0:32] = dot(jnp.ones((8, total), F32), logits, NT, HIGHEST)
    gate_sums[0:8, 32:48] = dot(jnp.ones((8, rows), F32), by_scale, NT, HIGHEST)
    gate_mix[...] = dot(logits, picked[...].astype(F32), NN, HIGHEST)
    grad = (
        grad_pre[...]
        + dot(grad_query[...], weights[0], NT)
        + dot(grad_key[...], weights[1], NT)
        + dot(grad_value[...], weights[2], NT)
        + dot(logits, spread, TN, HIGHEST)
    )
    grad_picked[...] = grad.astype(BF16)
    for c in range(clips):
        tokens_grad[c] = dot(
            one_hot(order, visible, c, rows, patches), grad_picked[c * rows : (c + 1) * rows, :]
        ).astype(BF16)


def tokens_back(patches, args, after=()):
    order, visible, picked = args[0], args[1], args[8]
    clips = visible.shape[0]
    total, width = picked.shape
    return call(
        tokens_kernel,
        "tokens_back",
        11,
        [
            sds((clips, patches, width), BF16),
            sds((8, 128), F32),
            sds((32, width), F32),
        ],
        args,
        "vss" + "v" * 10,
        [pltpu.VMEM((total, width), BF16)],
        after,
        large=MOST,
    )


def small_grads_kernel(
    where, sums_feed, up_b_grad, sums_mix, sums_attend, levels, buckets, gate_sums, gate_mix,
    keep, send, blocks
):
    width = sums_feed.shape[1]
    share = width // 8
    vectors = jnp.concatenate(
        [
            sums_attend[0:2, :],
            sums_mix[2:3, :],
            sums_feed[2:3, :],
            sums_mix[0:2, :],
            sums_feed[0:2, :],
        ],
        0,
    )
    ids = lines_of((384, 2 * SPAN))
    onehot = jnp.where(ids == buckets[...], 1.0, 0.0)
    table = dot(levels[...], onehot, NT, HIGHEST)
    count = NUM_BUCKETS // 8
    mix = gate_mix[...]
    own = lanes_of((16, width)) // 64 == lines_of((16, width))
    gates = []
    for half in range(2):
        line = jnp.sum(jnp.where(own, mix[16 * half : 16 * half + 16], 0.0), 0, keepdims=True)
        total = line[:, 0:128]
        for t in range(1, width // 128):
            total += line[:, 128 * t : 128 * t + 128]
        total += pltpu.roll(total, 64, 1)
        gates.append(total)
    gates.append(gate_sums[0:1, :])
    gates.append(jnp.zeros((1, 128), F32))
    gates = jnp.concatenate(gates, 0)
    for w in range(8):
        turned = pltpu.roll(vectors, width - share * w, 1) if w else vectors
        chunk = up_b_grad[w // 2 : w // 2 + 1, :]
        lines = [turned[:, :128]]
        for j in range(4):
            turn = 4 * share * (w % 2) + share * j
            lines.append((pltpu.roll(chunk, width - turn, 1) if turn else chunk)[:, :128])
        lines.append(gates)
        turned = pltpu.roll(table, 384 - count * w, 1) if w else table
        blocks[w] = jnp.concatenate([jnp.concatenate(lines, 0), turned[:, :128]], 1)
    for z in range(4):
        keep[where[1] ^ z] = blocks[2 * z + where[2]]
        send[where[1] ^ z] = blocks[2 * z + 1 - where[2]]


def small_grads(where, sums_feed, up_b_grad, sums_mix, sums_attend, levels, gate_sums, gate_mix):
    buckets = jnp.asarray(relative_buckets()[None, :])
    part = sds((4, 16, 256), F32)
    return call(
        small_grads_kernel,
        "small_grads",
        4,
        [part, part],
        [where, sums_feed, up_b_grad, sums_mix, sums_attend, levels, buckets, gate_sums, gate_mix],
        "s" + "v" * 8,
        [pltpu.VMEM((8, 16, 256), F32)],
    )


def swap_wide(x, flip):
    size = lax.axis_size("wide")
    return lax.ppermute(x, "wide", [(i, i ^ flip) for i in range(size)])


def swap_narrow(x, flip):
    size = lax.axis_size("narrow")
    return lax.ppermute(x, "narrow", [(i, i ^ flip) for i in range(size)])


def column_of(quarter):
    return [swap_wide(quarter, 2 * k) for k in range(1, 4)]


def trade(parts):
    return lax.all_to_all(parts, "narrow", 0, 0)


def both_cores(own, plane):
    return (own, plane), (swap_wide(own, 1), swap_wide(plane, 1))


def core_sum_kernel(keep, came, *refs):
    refs[-1][...] = (keep[...].astype(F32) + came[...].astype(F32)).astype(BF16)


def core_sum(keep, came, after=()):
    return call(
        core_sum_kernel, "core_sum", 4, sds(keep.shape, BF16), [keep, came], "vv", after=after
    )


def sum_four(a, b, c, d):
    return (a.astype(F32) + b.astype(F32)) + (c.astype(F32) + d.astype(F32))


def plane_sum_kernel(parts, *refs):
    smalls, outs = refs[:-4], refs[-4:]
    share = parts.shape[2]
    for k, out in enumerate(outs):
        out[:share, :] = sum_four(*(parts[j, k] for j in range(4))).astype(BF16)
        if smalls:
            small = sum_four(*(small[k] for small in smalls))
            high = small.astype(BF16).astype(F32)
            split = jnp.concatenate([high, small - high], 1)
            out[share:, :] = widen(split, out.shape[1]).astype(BF16)


def plane_sum(parts, smalls=(), after=()):
    share, width = parts.shape[2:]
    share += sum(s.shape[1] for s in smalls[:1])
    out = [sds((share, width), BF16)] * 4
    args = [parts, *smalls]
    return call(plane_sum_kernel, "plane_sum", 30, out, args, "v" * len(args), after=after)


def up_parts_kernel(up, out):
    width = out.shape[2]
    for j in range(4):
        out[j] = up[:, j * width : (j + 1) * width]


def up_parts(up, width, after=()):
    share = up.shape[0]
    return call(
        up_parts_kernel, "up_parts", 0.01, sds((4, share, width), BF16), [up], "v", after=after
    )


def column_sum_kernel(a, b, c, d, out):
    total = sum_four(a[...], b[...], c[...], d[...]).astype(BF16)
    for j in range(4):
        out[j] = total


def column_sum(parts, after=()):
    out = sds((4,) + parts[0].shape, BF16)
    return call(column_sum_kernel, "column_sum", 20, out, parts, "vvvv", after=after)


def square_sum_kernel(a, b, c, d, out, small):
    share = out.shape[0]
    total = sum_four(a[...], b[...], c[...], d[...])
    out[...] = total[:share].astype(BF16)
    lanes = small.shape[1]
    small[...] = total[share:, :lanes] + total[share:, lanes : 2 * lanes]


def square_sum(parts, share, after=()):
    lines, width = parts[0].shape
    out = [sds((share, width), BF16), sds((lines - share, 256), F32)]
    return call(square_sum_kernel, "square_sum", 20, out, parts, "vvvv", after=after)


def end_sum_kernel(ups, square, out):
    up = sum_four(*(ups[j] for j in range(4))).astype(BF16)
    for j in range(4):
        out[j, 0] = up
        out[j, 1] = square[...]


def end_sum(ups, square, after=()):
    out = sds((4, 2) + square.shape, BF16)
    return call(end_sum_kernel, "end_sum", 2, out, [ups, square], "vv", after=after)


def last_kernel(*refs):
    ends, small, downs = refs[:3]
    query, key, value, out, up, down = refs[3:9]
    vectors = refs[9:18]
    table, gate_weight, gate_bias, gate_scale = refs[18:]
    share, width = query.shape
    for j, target in enumerate((query, key, value, out)):
        up[:, j * width : (j + 1) * width] = ends[j, 0].astype(F32)
        target[...] = ends[j, 1].astype(F32)
        down[j * share : (j + 1) * share, :] = downs[j].astype(F32)
    sums = small[:, :128]
    heads, count = table.shape
    table[...] = small[:heads, 128 : 128 + count]
    lines = [sums[i : i + 1, :share] for i in range(8)]
    up_b = jnp.concatenate(
        [sums[8 + j : 9 + j, :share] for j in range(4)], 1
    )
    query_b, value_b, out_b, down_b, gain1, shift1, gain2, shift2 = lines
    for target, line in zip(
        vectors, (query_b, value_b, out_b, up_b, down_b, gain1, shift1, gain2, shift2)
    ):
        target[...] = line
    logits, size = gate_weight.shape
    half = logits // 2
    gate_weight[...] = jnp.where(
        lines_of((logits, 128)) < half, sums[12:13, :], sums[13:14, :]
    )[:, :size]
    line = sums[14:15, :]
    at = lanes_of((1, 128))
    one = jnp.sum(jnp.where(at < 16, line, 0.0), 1, keepdims=True)
    two = jnp.sum(jnp.where((at >= 16) & (at < 32), line, 0.0), 1, keepdims=True)
    gate_bias[...] = jnp.where(at < half, one, two)[:, : 2 * half]
    gate_scale[...] = pltpu.roll(line, 96, 1)[:, :heads]


def last(ends, small, downs, heads, logits):
    share, width = ends.shape[2:]
    line = sds((1, share), F32)
    return call(
        last_kernel,
        "last",
        5,
        [sds((share, width), F32)] * 4
        + [sds((share, 4 * width), F32), sds((4 * share, width), F32)]
        + [line] * 3
        + [sds((1, 4 * share), F32)]
        + [line] * 5
        + [
            sds((heads, NUM_BUCKETS // 8), F32),
            sds((logits, width // heads), F32),
            sds((1, logits), F32),
            sds((1, heads), F32),
        ],
        [ends, small, downs],
        "vvv",
    )


def body(
    tokens,
    patch_order,
    visible,
    query_weight,
    key_weight,
    value_weight,
    out_weight,
    up_weight,
    down_weight,
    query_bias,
    value_bias,
    out_bias,
    up_bias,
    down_bias,
    first_gain,
    first_shift,
    second_gain,
    second_shift,
    bias_table,
    gate_weight,
    gate_bias,
    gate_scale,
    cotangent,
):
    clips, patches, width = tokens.shape
    rows = cotangent.shape[1]
    heads = bias_table.shape[1]
    pairs = heads // 2
    total = clips * rows
    hidden = up_weight.shape[1]
    share = width // 8
    n_wide, n_narrow = lax.axis_size("wide"), lax.axis_size("narrow")
    fast = n_wide == 8 and n_narrow == 4
    me_wide, me_narrow = lax.axis_index("wide"), lax.axis_index("narrow")
    vectors = [
        query_bias, value_bias, out_bias, down_bias,
        first_gain, first_shift, second_gain, second_shift,
    ]
    squares = [query_weight, key_weight, value_weight, out_weight]
    gate_lines = gate_weight.T
    gather = lambda x: lax.all_gather(x, "wide", axis=0, tiled=True)

    if fast:
        where = jnp.stack([me_narrow, me_wide // 2, me_wide % 2]).astype(jnp.int32)
        own_square, square_quarter = first_blocks(
            where, squares, [v[None, :] for v in vectors], up_bias[None, :], bias_table.T
        )
        picked, first, second, gates = pick(
            patch_order, visible, gate_bias, gate_scale, tokens, gate_lines, rows, square_quarter
        )
        own_up, up_quarter = up_blocks(where, up_weight, width, (picked,))
        column, small, down_copy = first_column(
            square_quarter, column_of(square_quarter), down_weight, (own_up,)
        )
        down_w = gather(down_copy)
        smalls = (small, swap_wide(small, 1))
        up_arrived = column_of(up_quarter)
        square_plane = trade(column)
    else:
        where = jnp.zeros((3,), jnp.int32)
        picked, first, second, gates = pick(
            patch_order, visible, gate_bias, gate_scale, tokens, gate_lines, rows, tokens
        )
        fold = lambda x: x.reshape(4, 2, share, width).transpose(1, 0, 2, 3)
        pack = lambda x: [(c[0], jnp.swapaxes(c[1:], 0, 1)) for c in (x[0], x[1])]
        square_blocks = pack(jnp.stack([fold(gather(w)) for w in squares], 2))
        ups = jnp.split(gather(up_weight), 4, 1)
        up_pieces = pack(jnp.stack([fold(u) for u in ups], 2))
        down_w = gather(down_weight)
        lines = [gather(v).reshape(8, 1, share) for v in vectors]
        lines += [gather(up_bias).reshape(8, 4, share), jnp.zeros((8, 4, share), BF16)]
        lines = jnp.pad(jnp.concatenate(lines, 1), ((0, 0), (0, 0), (0, 128 - share)))
        table = gather(bias_table).reshape(8, -1, heads).transpose(0, 2, 1)
        table = jnp.pad(table, ((0, 0), (0, 16 - heads), (0, 128 - table.shape[2])))
        small = jnp.concatenate([lines, table], 2)
        small = jnp.pad(small, ((0, 0), (0, 0), (0, width - 256))).reshape(4, 2, 16, width)
        smalls = (small[:, 0], small[:, 1])

    position, lines = positions(
        where, patch_order, visible, smalls, clips, rows, pairs, width
    )
    if fast:
        square_plane = hold(square_plane, (lines,))
        square_blocks = both_cores(own_square, square_plane)
        column = up_column(up_arrived, (lines,))
        up_plane = trade(hold(column, (square_plane,)))
    query, key, value, soft, mixed, unit, inverse, normed, normed_low, weights = attend(
        where, visible, picked, gates, position, lines, *square_blocks
    )
    if fast:
        up_pieces = both_cores(own_up, hold(up_plane, (normed_low,)))
    down_keep, down_send, up_grad, output, grad_normed, up_b_grad, sums_feed = feed(
        where, visible, normed_low, normed, lines, cotangent.reshape(total, width),
        up_pieces, down_w.reshape(4, width, width),
    )
    grad_pre1, out_grad, grad_mixed, sums_mix = mix_back(
        grad_normed, unit, inverse, lines, mixed, weights
    )
    later = ()
    if fast:
        up_sum = lax.psum_scatter(up_grad, "wide", scatter_dimension=0, tiled=True)
        down_parts = core_sum(down_keep, swap_wide(down_send, 1), after=(grad_mixed,))
        later = (down_parts,)
    (
        square_keep, square_send, grad_query, grad_key, grad_value, grad_gate, gated, sums_attend,
    ) = attend_back(
        where, grad_mixed, out_grad, picked, query, key, value, soft, position, gates, later
    )
    levels = table_levels(patch_order, visible, gated)
    later = (levels,)
    if fast:
        square_parts = core_sum(square_keep, swap_wide(square_send, 1), after=(levels,))
        down_parts = plane_sum(trade(down_parts), after=(square_parts,))
        later = (down_parts[0],)
    tokens_grad, gate_sums, gate_mix = tokens_back(
        patches,
        [
            patch_order, visible, gate_scale, grad_pre1, grad_query, grad_key, grad_value, weights,
            picked, first, second, grad_gate, gate_lines,
        ],
        later,
    )
    small_keep, small_send = small_grads(
        where, sums_feed, up_b_grad, sums_mix, sums_attend, levels, gate_sums, gate_mix
    )

    if fast:
        spread = lambda parts: [parts[0]] + [swap_wide(parts[k], 2 * k) for k in range(1, 4)]
        up_part = up_parts(up_sum, width, (small_keep,))
        down_part = column_sum(spread(down_parts), (up_part,))
        small = small_keep + hold(swap_wide(small_send, 1), (down_part,))
        smalls = [small] + [swap_narrow(small, m) for m in range(1, 4)]
        square_plane = trade(square_parts)
        square_parts = plane_sum(square_plane, smalls)
        downs = trade(hold(down_part, (square_plane,)))
        ups = trade(hold(up_part, (downs,)))
        square, small = square_sum(spread(square_parts), share)
        ends = trade(end_sum(ups, square))
        ends = last(ends, small, downs, heads, gate_lines.shape[0])
        weight_grads, ends = ends[:6], ends[6:]
        vector_grads = [v.reshape(-1) for v in ends[:9]]
        table_grad, gate_weight_grad = ends[9].T, ends[10].T
        gate_bias_grad, gate_scale_grad = ends[11].reshape(-1), ends[12].reshape(-1)
    else:
        def reduce(x):
            x = lax.psum_scatter(x, "wide", scatter_dimension=0, tiled=True)
            return lax.psum(x, "narrow").astype(F32)

        def mine(x):
            part = x.shape[0] // n_wide
            return lax.dynamic_slice_in_dim(x, me_wide * part, part, 0)

        square = jnp.stack([square_keep, square_send], 2).reshape(4, width, width)
        down = jnp.stack([down_keep, down_send]).transpose(2, 0, 1, 3, 4).reshape(hidden, width)
        weight_grads = [reduce(square[j]) for j in range(4)]
        weight_grads += [reduce(up_grad), reduce(down)]
        small = jnp.stack([small_keep, small_send], 1).reshape(8, 16, 256)
        small = lax.psum(small, ("narrow", "wide"))
        lines = small[:, :8, :share].transpose(1, 0, 2).reshape(8, width)
        up_b_grad = small[:, 8:12, :share].reshape(-1)
        query_b, value_b, out_b, down_b, gain1, shift1, gain2, shift2 = lines
        vector_grads = [
            mine(v)
            for v in (query_b, value_b, out_b, up_b_grad, down_b, gain1, shift1, gain2, shift2)
        ]
        table = small[:, :heads, 128 : 128 + NUM_BUCKETS // 8].transpose(0, 2, 1)
        table_grad = mine(table.reshape(-1, heads))
        size, half = gate_weight.shape[0], gate_weight.shape[1] // 2
        gate_weight_grad = jnp.repeat(small[0, 12:14, :size].T, half, 1)
        gate_bias_grad = jnp.repeat(jnp.sum(small[0, 14, :32].reshape(2, 16), 1), half)
        gate_scale_grad = small[0, 14, 32 : 32 + heads]
    return (
        output.reshape(clips, rows, width),
        tokens_grad,
        *weight_grads,
        *vector_grads,
        table_grad,
        gate_weight_grad,
        gate_bias_grad,
        gate_scale_grad,
    )


def solution(mesh):
    split = P(("narrow", "wide"))
    shard = P("wide")
    in_specs = (split,) * 3 + (shard,) * 16 + (P(),) * 3 + (split,)
    out_specs = (split,) * 2 + (shard,) * 16 + (P(),) * 3
    return jax.shard_map(body, mesh=mesh, in_specs=in_specs, out_specs=out_specs, check_vma=False)
```

time: 576 us -> 257 us (0.45); the launches traced: 567 us -> 255 us
  matrix products: 153 us -> 0 us
  waiting for transfers between devices: 186 us -> 41.6 us
  Pallas kernels: 0 us -> 117 us
  blocking collectives: 132 us -> 16.3 us
  starting transfers between devices: 1.13 us -> 49.8 us
  other arithmetic: 33.7 us -> 2.03 us
  local copies, waits for them, and re-layouts: 43 us -> 14.3 us
    dot_general x37 -> x0, matrix products: 153 us -> none  [the longest x4 40.8 us: clip_table_grad(): return jnp.einsum('pb,ph->bh', onehot, clip_grad, precision=highest)]
    reduce_scatter x6 -> x1, waiting for transfers between devices: 121 us -> 0.01 us  [body(): up_sum = lax.psum_scatter(up_grad, 'wide', scatter_dimension=0, tiled=True)]
    pallas_call x0 -> x28, Pallas kernels: none -> 117 us  [the longest x19 93.3 us: call(): pl.pallas_call(run, in_specs=[spaces[k] for k in kinds] + [ANY] * len(aft...]
    all_gather x6 -> x1, waiting for transfers between devices: 60.1 us -> 0.01 us  [body(): gather = lambda x: lax.all_gather(x, 'wide', axis=0, tiled=True)]
    unnamed x2 -> x0, blocking collectives: 57.6 us -> none
    psum x2 -> x0, blocking collectives: 47.5 us -> none  [the longest x1 37.3 us: body(): lax.psum((gate_weight_grad, gate_bias_grad, gate_scale_grad), ('narrow',...]
    all_gather x2 -> x0, blocking collectives: 27 us -> none  [the longest x1 14 us: body(): lax.all_gather(bias_table, 'wide', axis=0, tiled=True)]
    all_to_all x0 -> x6, starting transfers between devices: none -> 26.5 us  [trade(): return lax.all_to_all(parts, 'narrow', 0, 0)]
  transfers between devices with their start and end apart: 13 -> 31, of which waited for: 6 -> 9; matrix products, arithmetic and copies ran while one was open for 33% -> 0% of each run, Pallas kernels for 0% -> 30%
where the time goes in v1:
time: 257 us; the launch traced here: 255 us
  Pallas kernels  117 us (46%)
  starting transfers between devices  49.8 us (19%)
  waiting for transfers between devices  41.6 us (16%)
  blocking collectives  16.3 us (6%)
  between operations  14.7 us (6%)
  local copies, waits for them, and re-layouts  14.3 us (6%)
    pallas_call x19, Pallas kernels, call(): pl.pallas_call(run, in_specs=[spaces[k] for k in kinds] + [ANY] * len(aft...  93.3 us
    all_to_all x6, starting transfers between devices, trade(): return lax.all_to_all(parts, 'narrow', 0, 0)  26.5 us
    all_to_all x6, waiting for transfers between devices, trade(): return lax.all_to_all(parts, 'narrow', 0, 0)  25.4 us
    ppermute x20, starting transfers between devices, swap_wide(): return lax.ppermute(x, 'wide', [(i, i ^ flip) for i in range(size)])  19.5 us
    all_to_all x1, blocking collectives, trade(): return lax.all_to_all(parts, 'narrow', 0, 0)  16.3 us
    ppermute x20, waiting for transfers between devices, swap_wide(): return lax.ppermute(x, 'wide', [(i, i ^ flip) for i in range(size)])  16.2 us
    pallas_call x1, Pallas kernels, attend_back(): pl.pallas_call(attend_back_kernel, grid=(clips,), in_specs=[SMEM, lines,...  13.5 us
    unnamed x92, local copies, waits for them, and re-layouts  13 us
  transfers between devices with their start and end apart: 31, of which 9 were waited for; matrix products, arithmetic and copies ran while one was open for 0% of the time, Pallas kernels for 30%

profile of v1, /device:TPU:0, one launch (start us, length us, event | category | flops | bytes accessed | tf_op | source)
XLA Modules:
  0.0 255.4 jit_solution(4586285934099299305)
XLA Ops:
  7.3 1.2 broadcast_in_dim.35.refs_13_
  9.1 2.2 first_blocks.1
  11.3 5.0 %collective-permute-start.2 = (bf16[112,768]{1,0:T(8,128)(2,1)}, bf16[112,768]{1,0:T(8,128)(2,1)S(1)}, u32[]{:S(2)}, u32[]{:S(2)}) collective-permute-start(bf16[112,768]{1,0:T(8,128)(2,1)} %get-tuple-element.97.token.refs_0_), channel_id=1, source_target_pairs={{0,6},{1,7},{2,4},{3,5},{4,2},{5,3},{6,0},{7,1},{8,14},{9,15},{10,... | collective-permute-start | bytes 516104 | tf_op jit(solution)/shard_map/ppermute | solution.py:1009
  17.0 0.9 copy-done.12
  17.9 4.9 %pick.1 = (bf16[512,768]{1,0:T(8,128)(2,1)S(1)}, f32[4,16,128]{2,1,0:T(8,128)S(1)}, f32[4,16,128]{2,1,0:T(8,128)S(1)}, f32[4,16,128]{2,1,0:T(8,128)S(1)}) custom-call(s32[4,496]{1,0:T(4,128)S(1)} %copy-done.13, s32[4]{0:T(128)S(1)} %copy-done.19, f32[8]{0:T(128)S(1)} %copy-done.18, f32[12]{0:T(128)S(1)} %copy-done.20, bf16[4,496,768]{2,1,0:T(8,128)(2,1)} %tokens.1, ...), custom_call_target="tpu_custom_call" | custom-call | flops 60000002048 | bytes 210000000 | tf_op jit(solution)/shard_map/pick/pallas_call | solution.py:292
  23.7 7.4 %collective-permute-done.1.refs_2_ = bf16[112,768]{1,0:T(8,128)(2,1)S(1)} collective-permute-done((bf16[112,768]{1,0:T(8,128)(2,1)}, bf16[112,768]{1,0:T(8,128)(2,1)S(1)}, u32[]{:S(2)}, u32[]{:S(2)}) %collective-permute-start.1) | collective-permute-done | bytes 172064 | tf_op jit(solution)/shard_map/ppermute | solution.py:1009
  31.1 2.0 first_column.1
  33.3 2.5 collective-permute-start.8
  35.8 1.9 collective-permute-start.6
  37.8 4.4 %all-to-all-start = ((bf16[4,3,96,768]{3,2,1,0:T(8,128)(2,1)}), bf16[4,3,96,768]{3,2,1,0:T(8,128)(2,1)}, u32[]{:S(2)}, u32[]{:S(2)}) async-start(bf16[4,3,96,768]{3,2,1,0:T(8,128)(2,1)} %get-tuple-element.105), calls=%async_computation | async-start | bytes 3538944 | tf_op jit(solution)/shard_map/all_to_all | solution.py:1022
  42.2 8.3 %position.1 = (bf16[4,6,128,256]{3,2,1,0:T(8,128)(2,1)S(1)}, f32[16,768]{1,0:T(8,128)S(1)}) custom-call(s32[3]{0:T(128)S(1)} %copy-done.5, s32[4,496]{1,0:T(4,128)S(1)} %copy-done.13, s32[4]{0:T(128)S(1)} %copy-done.19, s32[1,1024]{1,0:T(1,128)S(1)} %copy-done.22, bf16[4,16,768]{2,1,0:T(8,128)(2,1)S(1)} %get-tuple-element.101.refs_4_, ...), custom_call_target="tpu_custom_call" | custom-call | flops 109999996928 | bytes 385000000 | tf_op jit(solution)/shard_map/position/pallas_call | solution.py:86
  51.1 1.2 copy-done.31
  52.3 12.2 %all-to-all-done.refs_0_ = bf16[4,3,96,768]{3,2,1,0:T(8,128)(2,1)} async-done(((bf16[4,3,96,768]{3,2,1,0:T(8,128)(2,1)}), bf16[4,3,96,768]{3,2,1,0:T(8,128)(2,1)}, u32[]{:S(2)}, u32[]{:S(2)}) %all-to-all-start) | async-done | bytes 1769504 | tf_op jit(solution)/shard_map/all_to_all | solution.py:1022
  65.5 1.2 copy-done
  66.7 4.4 %all-to-all-start.1 = ((bf16[4,3,96,768]{3,2,1,0:T(8,128)(2,1)}), bf16[4,3,96,768]{3,2,1,0:T(8,128)(2,1)}, u32[]{:S(2)}, u32[]{:S(2)}) async-start(bf16[4,3,96,768]{3,2,1,0:T(8,128)(2,1)} %hold.7), calls=%async_computation.1 | async-start | bytes 3538944 | tf_op jit(solution)/shard_map/all_to_all | solution.py:1022
  71.3 14.3 %attend.1 = (bf16[512,768]{1,0:T(8,128)(2,1)S(1)}, bf16[512,768]{1,0:T(8,128)(2,1)}, bf16[512,768]{1,0:T(8,128)(2,1)}, f32[4,6,128,256]{3,2,1,0:T(8,128)}, bf16[...) custom-call(s32[3]{0:T(128)S(1)} %copy-done.5, ...), custom_call_target="tpu_custom_call" | custom-call | flops 140000002048 | bytes 490000000 | tf_op jit(solution)/shard_map/attend/pallas_call | solution.py:86
  86.5 6.2 %all-to-all-done.1.refs_0_ = bf16[4,3,96,768]{3,2,1,0:T(8,128)(2,1)} async-done(((bf16[4,3,96,768]{3,2,1,0:T(8,128)(2,1)}), bf16[4,3,96,768]{3,2,1,0:T(8,128)(2,1)}, u32[]{:S(2)}, u32[]{:S(2)}) %all-to-all-start.1) | async-done | bytes 1769504 | tf_op jit(solution)/shard_map/all_to_all | solution.py:1022
  92.7 1.0 copy-done.10
  93.7 3.5 %collective-permute-done.9.refs_8_ = bf16[4,96,768]{2,1,0:T(8,128)(2,1)S(1)} collective-permute-done((bf16[4,96,768]{2,1,0:T(8,128)(2,1)S(1)}, bf16[4,96,768]{2,1,0:T(8,128)(2,1)S(1)}, u32[]{:S(2)}, u32[]{:S(2)}) %collective-permute-start.9) | collective-permute-done | bytes 589856 | tf_op jit(solution)/shard_map/ppermute | solution.py:1009
  97.3 30.9 %feed.1 = (bf16[4,4,96,768]{3,2,1,0:T(8,128)(2,1)}, bf16[4,4,96,768]{3,2,1,0:T(8,128)(2,1)}, bf16[768,3072]{1,0:T(8,128)(2,1)}, bf16[512,768]{1,0:T(8,128)(2,1)}...) custom-call(s32[3]{0:T(128)S(1)} %copy-done.5, s32[4]{0:T(128)S(1)} %copy-done.19, ...), custom_call_target="tpu_custom_call" | custom-call | flops 320000000000 | bytes 1120000000 | tf_op jit(solution)/shard_map/feed/pallas_call | solution.py:86
  130.5 5.1 %mix_back.1 = (f32[512,768]{1,0:T(8,128)}, bf16[768,768]{1,0:T(8,128)(2,1)}, bf16[512,768]{1,0:T(8,128)(2,1)S(1)}, f32[8,768]{1,0:T(8,128)S(1)}) custom-call(f32[512,768]{1,0:T(8,128)} %get-tuple-element.111.refs_0_, f32[512,768]{1,0:T(8,128)} %get-tuple-element.112.refs_1_, f32[512,1]{1,0:T(8,128)S(1)} %get-tuple-element.113.refs_2_, ...), custom_call_target="tpu_custom_call" | custom-call | flops 60000002048 | bytes 210000000 | tf_op jit(solution)/shard_map/mix_back/pallas_call | solution.py:713
  135.6 1.9 core_sum.2.refs_0_
  137.6 4.6 %all-to-all-start.2 = ((bf16[4,4,96,768]{3,2,1,0:T(8,128)(2,1)}), bf16[4,4,96,768]{3,2,1,0:T(8,128)(2,1)}, u32[]{:S(2)}, u32[]{:S(2)}) async-start(bf16[4,4,96,768]{3,2,1,0:T(8,128)(2,1)} %core_sum.2.refs_0_), calls=%async_computation.2 | async-start | bytes 4718592 | tf_op jit(solution)/shard_map/all_to_all | solution.py:1022
  142.2 13.5 %attend_back.1 = (bf16[4,4,96,768]{3,2,1,0:T(8,128)(2,1)}, bf16[4,4,96,768]{3,2,1,0:T(8,128)(2,1)}, bf16[512,768]{1,0:T(8,128)(2,1)S(1)}, bf16[512,768]{1,0:T(8,...) custom-call(s32[3]{0:T(128)S(1)} %copy-done.5, ...), custom_call_target="tpu_custom_call" | custom-call | flops 149999992832 | bytes 525000000 | tf_op jit(solution)/shard_map/attend_back/pallas_call | solution.py:783
  155.9 1.4 copy-done.32
  157.3 8.8 %table_back.1.refs_2_.refs_5_ = f32[16,1024]{1,0:T(8,128)S(1)} custom-call(s32[4,496]{1,0:T(4,128)S(1)} %copy-done.14, s32[4]{0:T(128)S(1)} %copy-done.19, bf16[4,6,128,256]{3,2,1,0:T(8,128)(2,1)S(1)} %copy-done.32), custom_call_target="tpu_custom_call" | custom-call | flops 120000004096 | bytes 420000000 | tf_op jit(solution)/shard_map/table_back/pallas_call | solution.py:86
  166.1 1.9 core_sum.3.refs_1_
  168.7 1.9 all-to-all-done.2.refs_0_
  170.5 4.8 %all-to-all-start.3 = ((bf16[4,4,96,768]{3,2,1,0:T(8,128)(2,1)}), bf16[4,4,96,768]{3,2,1,0:T(8,128)(2,1)}, u32[]{:S(2)}, u32[]{:S(2)}) async-start(bf16[4,4,96,768]{3,2,1,0:T(8,128)(2,1)} %core_sum.3.refs_1_), calls=%async_computation.4 | async-start | bytes 4718592 | tf_op jit(solution)/shard_map/all_to_all | solution.py:1022
  175.4 2.6 %plane_sum.2 = (bf16[96,768]{1,0:T(8,128)(2,1)S(1)}, bf16[96,768]{1,0:T(8,128)(2,1)}, bf16[96,768]{1,0:T(8,128)(2,1)}, bf16[96,768]{1,0:T(8,128)(2,1)}) custom-call(bf16[4,4,96,768]{3,2,1,0:T(8,128)(2,1)} %all-to-all-done.2.refs_0_, bf16[4,4,96,768]{3,2,1,0:T(8,128)(2,1)} %core_sum.3.refs_1_), custom_call_target="tpu_custom_call" | custom-call | flops 299999985664 | bytes 1050000000 | tf_op jit(solution)/shard_map/plane_sum/pallas_call | solution.py:86
  178.0 3.0 %collective-permute-start.14 = (bf16[96,768]{1,0:T(8,128)(2,1)}, bf16[96,768]{1,0:T(8,128)(2,1)}, u32[]{:S(2)}, u32[]{:S(2)}) collective-permute-start(bf16[96,768]{1,0:T(8,128)(2,1)} %get-tuple-element.145), channel_id=1, source_target_pairs={{0,4},{1,5},{2,6},{3,7},{4,0},{5,1},{6,2},{7,3},{8,12},{9,13},{10,... | collective-permute-start | bytes 442376 | tf_op jit(solution)/shard_map/ppermute | solution.py:1009
  181.0 1.4 collective-permute-start.15
  182.4 9.5 %tokens_back.1 = (bf16[4,496,768]{2,1,0:T(8,128)(2,1)}, f32[8,128]{1,0:T(8,128)S(1)}, f32[32,768]{1,0:T(8,128)S(1)}) custom-call(s32[4,496]{1,0:T(4,128)S(1)} %copy-done.15, s32[4]{0:T(128)S(1)} %copy-done.19, f32[12]{0:T(128)S(1)} %copy-done.21, f32[512,768]{1,0:T(8,128)} %get-tuple-element.116.refs_3_, bf16[512,768]{1,0:T(8,128)(2,1)S(1)} %get-tuple-element.125.refs_4_, ...), custom_call_target="tpu_custom_call" | custom-call | flops 109999996928 | bytes 385000000 | tf_op jit(solution)/shard_map/tokens_back/pallas_call | solution.py:86
  192.0 2.7 %small_grads.1 = (f32[4,16,256]{2,1,0:T(8,128)S(1)}, f32[4,16,256]{2,1,0:T(8,128)}) custom-call(s32[3]{0:T(128)S(1)} %copy-done.5, f32[8,768]{1,0:T(8,128)S(1)} %copy-done.39, f32[8,768]{1,0:T(8,128)S(1)} %copy-done.37, f32[8,768]{1,0:T(8,128)S(1)} %get-tuple-element.139.refs_3_, f32[8,768]{1,0:T(8,128)S(1)} %get-tuple-element.140.refs_4_, ...), custom_call_target="tpu_custom_call" | custom-call | flops 40000000000 | bytes 140000000 | tf_op jit(solution)/shard_map/small_grads/pallas_call | solution.py:86
  194.7 1.1 copy-done.3
  195.8 1.3 column_sum.1.refs_0_.refs_1_
  198.8 2.7 %collective-permute-start.19 = (f32[4,16,256]{2,1,0:T(8,128)S(1)}, f32[4,16,256]{2,1,0:T(8,128)S(1)}, u32[]{:S(2)}, u32[]{:S(2)}) collective-permute-start(f32[4,16,256]{2,1,0:T(8,128)S(1)} %add.11.refs_1_), channel_id=1, source_target_pairs={{0,24},{8,16},{16,8},{24,0},{1,25},{9,17},{17,9},{25,1},{2,26},{10... | collective-permute-start | bytes 196616 | tf_op jit(solution)/shard_map/ppermute | solution.py:1014
  202.5 4.2 %all-to-all-start.4 = ((bf16[4,96,768]{2,1,0:T(8,128)(2,1)}), bf16[4,96,768]{2,1,0:T(8,128)(2,1)}, u32[]{:S(2)}, u32[]{:S(2)}) async-start(bf16[4,96,768]{2,1,0:T(8,128)(2,1)} %hold.9), calls=%async_computation.5 | async-start | bytes 1179648 | tf_op jit(solution)/shard_map/all_to_all | solution.py:1022
  206.7 2.0 plane_sum.3
  209.2 2.6 %collective-permute-start.21 = (bf16[112,768]{1,0:T(8,128)(2,1)S(1)}, bf16[112,768]{1,0:T(8,128)(2,1)S(1)}, u32[]{:S(2)}, u32[]{:S(2)}) collective-permute-start(bf16[112,768]{1,0:T(8,128)(2,1)S(1)} %get-tuple-element.150), channel_id=1, source_target_pairs={{0,4},{1,5},{2,6},{3,7},{4,0},{5,1},{6,2},{7,3},{8,12},{9,13},{10,... | collective-permute-start | bytes 516104 | tf_op jit(solution)/shard_map/ppermute | solution.py:1009
  211.8 1.3 collective-permute-start.22
  213.2 2.3 all-to-all-done.4.refs_1_.refs_2_
  215.5 4.2 %all-to-all-start.5 = ((bf16[4,96,768]{2,1,0:T(8,128)(2,1)}), bf16[4,96,768]{2,1,0:T(8,128)(2,1)}, u32[]{:S(2)}, u32[]{:S(2)}) async-start(bf16[4,96,768]{2,1,0:T(8,128)(2,1)} %hold.10), calls=%async_computation.6 | async-start | bytes 1179648 | tf_op jit(solution)/shard_map/all_to_all | solution.py:1022
  219.6 5.2 %collective-permute-done.21.refs_2_ = bf16[112,768]{1,0:T(8,128)(2,1)S(1)} collective-permute-done((bf16[112,768]{1,0:T(8,128)(2,1)S(1)}, bf16[112,768]{1,0:T(8,128)(2,1)S(1)}, u32[]{:S(2)}, u32[]{:S(2)}) %collective-permute-start.21) | collective-permute-done | bytes 172064 | tf_op jit(solution)/shard_map/ppermute | solution.py:1009
  224.9 2.7 %all-to-all-done.5.refs_0_ = bf16[4,96,768]{2,1,0:T(8,128)(2,1)} async-done(((bf16[4,96,768]{2,1,0:T(8,128)(2,1)}), bf16[4,96,768]{2,1,0:T(8,128)(2,1)}, u32[]{:S(2)}, u32[]{:S(2)}) %all-to-all-start.5) | async-done | bytes 589856 | tf_op jit(solution)/shard_map/all_to_all | solution.py:1022
  227.6 1.2 end_sum.1
  228.7 16.3 %all_to_all.35.refs_0_ = bf16[4,2,96,768]{3,2,1,0:T(8,128)(2,1)S(1)} all-to-all(bf16[4,2,96,768]{3,2,1,0:T(8,128)(2,1)S(1)} %end_sum.1), channel_id=1, replica_groups=mesh['narrow'=4,'wide'=8] {'narrow'}, dimensions={0} | all-to-all | bytes 2359296 | tf_op jit(solution)/shard_map/all_to_all | solution.py:1022
  245.0 2.9 %last.1 = (f32[96,768]{1,0:T(8,128)}, f32[96,768]{1,0:T(8,128)}, f32[96,768]{1,0:T(8,128)}, f32[96,768]{1,0:T(8,128)}, f32[96,3072]{1,0:T(8,128)}, /*index=5*/f3...) custom-call(bf16[4,2,96,768]{3,2,1,0:T(8,128)(2,1)S(1)} %all_to_all., ...), custom_call_target="tpu_custom_call" | custom-call | flops 49999998976 | bytes 175000000 | tf_op jit(solution)/shard_map/last/pallas_call | solution.py:86
  (141 shorter events, 12.2 us)
Async XLA Ops:
  7.2 90.1 %all-gather.2.cloned.1.call-start = ((), (), s32[]{:S(2)}) async-start(), calls=%async_computation.8 | async-start | bytes 5308416 | tf_op jit(solution)/shard_map/all_gather | solution.py:1212
  9.1 7.9 %copy-start.13 = (s32[4,496]{1,0:T(4,128)S(1)}, s32[4,496]{1,0:T(4,128)}, u32[]{:S(2)}) copy-start(s32[4,496]{1,0:T(4,128)} %refs_0_.3) | copy-start | bytes 23812
  9.1 7.9 %copy-start.16 = (f32[64,8]{0,1:T(8,128)S(1)}, f32[64,8]{0,1:T(8,128)}, u32[]{:S(2)}) copy-start(f32[64,8]{0,1:T(8,128)} %param.44) | copy-start | bytes 6148
  9.1 7.9 %copy-start.18 = (f32[8]{0:T(128)S(1)}, f32[8]{0:T(128)}, u32[]{:S(2)}) copy-start(f32[8]{0:T(128)} %gate_bias.1) | copy-start | bytes 100
  9.1 7.9 %copy-start.19 = (s32[4]{0:T(128)S(1)}, s32[4]{0:T(128)}, u32[]{:S(2)}) copy-start(s32[4]{0:T(128)} %refs_1_.13) | copy-start | bytes 52
  9.1 7.9 %copy-start.20 = (f32[12]{0:T(128)S(1)}, f32[12]{0:T(128)}, u32[]{:S(2)}) copy-start(f32[12]{0:T(128)} %refs_2_.5) | copy-start | bytes 148
  11.3 12.4 %collective-permute-start.2 = (bf16[112,768]{1,0:T(8,128)(2,1)}, bf16[112,768]{1,0:T(8,128)(2,1)S(1)}, u32[]{:S(2)}, u32[]{:S(2)}) collective-permute-start(bf16[112,768]{1,0:T(8,128)(2,1)} %get-tuple-element.97.token.refs_0_), channel_id=1, source_target_pairs={{0,6},{1,7},{2,4},{3,5},{4,2},{5,3},{6,0},{7,1},{8,14},{9,15},{10,... | collective-permute-start | bytes 516104 | tf_op jit(solution)/shard_map/ppermute | solution.py:1009
  16.3 14.8 %collective-permute-start.1 = (bf16[112,768]{1,0:T(8,128)(2,1)}, bf16[112,768]{1,0:T(8,128)(2,1)S(1)}, u32[]{:S(2)}, u32[]{:S(2)}) collective-permute-start(bf16[112,768]{1,0:T(8,128)(2,1)} %get-tuple-element.97.token.refs_0_), channel_id=1, source_target_pairs={{0,4},{1,5},{2,6},{3,7},{4,0},{5,1},{6,2},{7,3},{8,12},{9,13},{10,... | collective-permute-start | bytes 516104 | tf_op jit(solution)/shard_map/ppermute | solution.py:1009
  16.3 14.8 %collective-permute-start = (bf16[112,768]{1,0:T(8,128)(2,1)}, bf16[112,768]{1,0:T(8,128)(2,1)S(1)}, u32[]{:S(2)}, u32[]{:S(2)}) collective-permute-start(bf16[112,768]{1,0:T(8,128)(2,1)} %get-tuple-element.97.token.refs_0_), channel_id=1, source_target_pairs={{0,2},{1,3},{2,0},{3,1},{4,6},{5,7},{6,4},{7,5},{8,10},{9,11},{10,... | collective-permute-start | bytes 516104 | tf_op jit(solution)/shard_map/ppermute | solution.py:1009
  22.8 48.5 %copy-start.44 = (f32[4,16,128]{2,1,0:T(8,128)}, f32[4,16,128]{2,1,0:T(8,128)S(1)}, u32[]{:S(2)}) copy-start(f32[4,16,128]{2,1,0:T(8,128)S(1)} %get-tuple-element.99.refs_3_.gates) | copy-start | bytes 98308
  22.8 8.3 %copy-start.8 = (bf16[384,768]{1,0:T(8,128)(2,1)S(1)}, bf16[384,768]{1,0:T(8,128)(2,1)}, u32[]{:S(2)}) copy-start(bf16[384,768]{1,0:T(8,128)(2,1)} %refs_4_.3) | copy-start | bytes 1769476
  23.7 9.5 %copy-start.9 = (bf16[4,96,768]{2,1,0:T(8,128)(2,1)}, bf16[4,96,768]{2,1,0:T(8,128)(2,1)S(1)}, u32[]{:S(2)}) copy-start(bf16[4,96,768]{2,1,0:T(8,128)(2,1)S(1)} %get-tuple-element.100.refs_5_.refs_6_) | copy-start | bytes 1769476
  33.2 9.0 %collective-permute-start.3 = (bf16[4,16,768]{2,1,0:T(8,128)(2,1)S(1)}, bf16[4,16,768]{2,1,0:T(8,128)(2,1)S(1)}, u32[]{:S(2)}, u32[]{:S(2)}) collective-permute-start(bf16[4,16,768]{2,1,0:T(8,128)(2,1)S(1)} %get-tuple-element.101.refs_4_), channel_id=1, source_target_pairs={{0,1},{1,0},{2,3},{3,2},{4,5},{5,4},{6,7},{7,6},{8,9},{9,8},{10,11... | collective-permute-start | bytes 294920 | tf_op jit(solution)/shard_map/ppermute | solution.py:1009
  33.3 31.3 %collective-permute-start.8 = (bf16[96,768]{1,0:T(8,128)(2,1)S(1)}, bf16[96,768]{1,0:T(8,128)(2,1)S(1)}, u32[]{:S(2)}, u32[]{:S(2)}) collective-permute-start(bf16[96,768]{1,0:T(8,128)(2,1)S(1)} %get-tuple-element.108), channel_id=1, source_target_pairs={{0,6},{1,7},{2,4},{3,5},{4,2},{5,3},{6,0},{7,1},{8,14},{9,15},{10,... | collective-permute-start | bytes 442376 | tf_op jit(solution)/shard_map/ppermute | solution.py:1009
  35.8 28.7 %collective-permute-start.7 = (bf16[96,768]{1,0:T(8,128)(2,1)S(1)}, bf16[96,768]{1,0:T(8,128)(2,1)S(1)}, u32[]{:S(2)}, u32[]{:S(2)}) collective-permute-start(bf16[96,768]{1,0:T(8,128)(2,1)S(1)} %get-tuple-element.108), channel_id=1, source_target_pairs={{0,4},{1,5},{2,6},{3,7},{4,0},{5,1},{6,2},{7,3},{8,12},{9,13},{10,... | collective-permute-start | bytes 442376 | tf_op jit(solution)/shard_map/ppermute | solution.py:1009
  35.8 28.8 %collective-permute-start.6 = (bf16[96,768]{1,0:T(8,128)(2,1)S(1)}, bf16[96,768]{1,0:T(8,128)(2,1)S(1)}, u32[]{:S(2)}, u32[]{:S(2)}) collective-permute-start(bf16[96,768]{1,0:T(8,128)(2,1)S(1)} %get-tuple-element.108), channel_id=1, source_target_pairs={{0,2},{1,3},{2,0},{3,1},{4,6},{5,7},{6,4},{7,5},{8,10},{9,11},{10,... | collective-permute-start | bytes 442376 | tf_op jit(solution)/shard_map/ppermute | solution.py:1009
  37.7 33.6 %collective-permute-start.4 = (bf16[4,96,768]{2,1,0:T(8,128)(2,1)S(1)}, bf16[4,96,768]{2,1,0:T(8,128)(2,1)S(1)}, u32[]{:S(2)}, u32[]{:S(2)}) collective-permute-start(bf16[4,96,768]{2,1,0:T(8,128)(2,1)S(1)} %copy-done.11), channel_id=1, source_target_pairs={{0,1},{1,0},{2,3},{3,2},{4,5},{5,4},{6,7},{7,6},{8,9},{9,8},{10,11... | collective-permute-start | bytes 1769480 | tf_op jit(solution)/shard_map/ppermute | solution.py:1009
  37.8 26.8 %all-to-all-start = ((bf16[4,3,96,768]{3,2,1,0:T(8,128)(2,1)}), bf16[4,3,96,768]{3,2,1,0:T(8,128)(2,1)}, u32[]{:S(2)}, u32[]{:S(2)}) async-start(bf16[4,3,96,768]{3,2,1,0:T(8,128)(2,1)} %get-tuple-element.105), calls=%async_computation | async-start | bytes 3538944 | tf_op jit(solution)/shard_map/all_to_all | solution.py:1022
  64.5 6.8 %collective-permute-start.5 = (bf16[4,3,96,768]{3,2,1,0:T(8,128)(2,1)}, bf16[4,3,96,768]{3,2,1,0:T(8,128)(2,1)}, u32[]{:S(2)}, u32[]{:S(2)}) collective-permute-start(bf16[4,3,96,768]{3,2,1,0:T(8,128)(2,1)} %hold.6.refs_7_.refs_1_), channel_id=1, source_target_pairs={{0,1},{1,0},{2,3},{3,2},{4,5},{5,4},{6,7},{7,6},{8,9},{9,8},{10,11... | collective-permute-start | bytes 5308424 | tf_op jit(solution)/shard_map/ppermute | solution.py:1009
  66.7 26.0 %all-to-all-start.1 = ((bf16[4,3,96,768]{3,2,1,0:T(8,128)(2,1)}), bf16[4,3,96,768]{3,2,1,0:T(8,128)(2,1)}, u32[]{:S(2)}, u32[]{:S(2)}) async-start(bf16[4,3,96,768]{3,2,1,0:T(8,128)(2,1)} %hold.7), calls=%async_computation.1 | async-start | bytes 3538944 | tf_op jit(solution)/shard_map/all_to_all | solution.py:1022
  71.1 123.6 %reduce-scatter.2.cloned.1.call-start = ((), (), s32[]{:S(2)}) async-start(), calls=%async_computation.9 | async-start | bytes 5308416 | tf_op jit(solution)/shard_map/reduce_scatter | solution.py:1272
  92.7 4.6 %collective-permute-start.10 = (bf16[4,3,96,768]{3,2,1,0:T(8,128)(2,1)}, bf16[4,3,96,768]{3,2,1,0:T(8,128)(2,1)}, u32[]{:S(2)}, u32[]{:S(2)}) collective-permute-start(bf16[4,3,96,768]{3,2,1,0:T(8,128)(2,1)} %hold.8.refs_7_), channel_id=1, source_target_pairs={{0,1},{1,0},{2,3},{3,2},{4,5},{5,4},{6,7},{7,6},{8,9},{9,8},{10,11... | collective-permute-start | bytes 5308424 | tf_op jit(solution)/shard_map/ppermute | solution.py:1009
  93.7 3.5 %collective-permute-start.9 = (bf16[4,96,768]{2,1,0:T(8,128)(2,1)S(1)}, bf16[4,96,768]{2,1,0:T(8,128)(2,1)S(1)}, u32[]{:S(2)}, u32[]{:S(2)}) collective-permute-start(bf16[4,96,768]{2,1,0:T(8,128)(2,1)S(1)} %copy-done.10), channel_id=1, source_target_pairs={{0,1},{1,0},{2,3},{3,2},{4,5},{5,4},{6,7},{7,6},{8,9},{9,8},{10,11... | collective-permute-start | bytes 1769480 | tf_op jit(solution)/shard_map/ppermute | solution.py:1009
  129.4 6.2 %collective-permute-start.11 = (bf16[4,4,96,768]{3,2,1,0:T(8,128)(2,1)}, bf16[4,4,96,768]{3,2,1,0:T(8,128)(2,1)S(1)}, u32[]{:S(2)}, u32[]{:S(2)}) collective-permute-start(bf16[4,4,96,768]{3,2,1,0:T(8,128)(2,1)} %get-tuple-element.124), channel_id=1, source_target_pairs={{0,1},{1,0},{2,3},{3,2},{4,5},{5,4},{6,7},{7,6},{8,9},{9,8},{10,11... | collective-permute-start | bytes 7077896 | tf_op jit(solution)/shard_map/ppermute | solution.py:1009
  137.6 33.0 %all-to-all-start.2 = ((bf16[4,4,96,768]{3,2,1,0:T(8,128)(2,1)}), bf16[4,4,96,768]{3,2,1,0:T(8,128)(2,1)}, u32[]{:S(2)}, u32[]{:S(2)}) async-start(bf16[4,4,96,768]{3,2,1,0:T(8,128)(2,1)} %core_sum.2.refs_0_), calls=%async_computation.2 | async-start | bytes 4718592 | tf_op jit(solution)/shard_map/all_to_all | solution.py:1022
  142.2 13.7 %copy-start.14 = (s32[4,496]{1,0:T(4,128)S(1)}, s32[4,496]{1,0:T(4,128)}, u32[]{:S(2)}) copy-start(s32[4,496]{1,0:T(4,128)} %refs_0_.3) | copy-start | bytes 23812
  155.7 10.4 %collective-permute-start.12 = (bf16[4,4,96,768]{3,2,1,0:T(8,128)(2,1)}, bf16[4,4,96,768]{3,2,1,0:T(8,128)(2,1)S(1)}, u32[]{:S(2)}, u32[]{:S(2)}) collective-permute-start(bf16[4,4,96,768]{3,2,1,0:T(8,128)(2,1)} %get-tuple-element.132), channel_id=1, source_target_pairs={{0,1},{1,0},{2,3},{3,2},{4,5},{5,4},{6,7},{7,6},{8,9},{9,8},{10,11... | collective-permute-start | bytes 7077896 | tf_op jit(solution)/shard_map/ppermute | solution.py:1009
  157.3 8.8 %copy-start.28 = (bf16[4,4,96,768]{3,2,1,0:T(8,128)(2,1)S(1)}, bf16[4,4,96,768]{3,2,1,0:T(8,128)(2,1)}, u32[]{:S(2)}) copy-start(bf16[4,4,96,768]{3,2,1,0:T(8,128)(2,1)} %get-tuple-element.131.refs_0_) | copy-start | bytes 7077892
  170.5 32.0 %all-to-all-start.3 = ((bf16[4,4,96,768]{3,2,1,0:T(8,128)(2,1)}), bf16[4,4,96,768]{3,2,1,0:T(8,128)(2,1)}, u32[]{:S(2)}, u32[]{:S(2)}) async-start(bf16[4,4,96,768]{3,2,1,0:T(8,128)(2,1)} %core_sum.3.refs_1_), calls=%async_computation.4 | async-start | bytes 4718592 | tf_op jit(solution)/shard_map/all_to_all | solution.py:1022
  175.3 7.0 %copy-start.15 = (s32[4,496]{1,0:T(4,128)S(1)}, s32[4,496]{1,0:T(4,128)}, u32[]{:S(2)}) copy-start(s32[4,496]{1,0:T(4,128)} %refs_0_.3) | copy-start | bytes 23812
  175.3 7.0 %copy-start.17 = (f32[64,8]{0,1:T(8,128)S(1)}, f32[64,8]{0,1:T(8,128)}, u32[]{:S(2)}) copy-start(f32[64,8]{0,1:T(8,128)} %param.44) | copy-start | bytes 6148
  175.3 7.0 %copy-start.21 = (f32[12]{0:T(128)S(1)}, f32[12]{0:T(128)}, u32[]{:S(2)}) copy-start(f32[12]{0:T(128)} %refs_2_.5) | copy-start | bytes 148
  178.0 17.8 %collective-permute-start.13 = (bf16[96,768]{1,0:T(8,128)(2,1)}, bf16[96,768]{1,0:T(8,128)(2,1)}, u32[]{:S(2)}, u32[]{:S(2)}) collective-permute-start(bf16[96,768]{1,0:T(8,128)(2,1)} %get-tuple-element.144), channel_id=1, source_target_pairs={{0,2},{1,3},{2,0},{3,1},{4,6},{5,7},{6,4},{7,5},{8,10},{9,11},{10,... | collective-permute-start | bytes 442376 | tf_op jit(solution)/shard_map/ppermute | solution.py:1009
  178.0 17.8 %collective-permute-start.14 = (bf16[96,768]{1,0:T(8,128)(2,1)}, bf16[96,768]{1,0:T(8,128)(2,1)}, u32[]{:S(2)}, u32[]{:S(2)}) collective-permute-start(bf16[96,768]{1,0:T(8,128)(2,1)} %get-tuple-element.145), channel_id=1, source_target_pairs={{0,4},{1,5},{2,6},{3,7},{4,0},{5,1},{6,2},{7,3},{8,12},{9,13},{10,... | collective-permute-start | bytes 442376 | tf_op jit(solution)/shard_map/ppermute | solution.py:1009
  181.0 14.8 %collective-permute-start.15 = (bf16[96,768]{1,0:T(8,128)(2,1)}, bf16[96,768]{1,0:T(8,128)(2,1)}, u32[]{:S(2)}, u32[]{:S(2)}) collective-permute-start(bf16[96,768]{1,0:T(8,128)(2,1)} %get-tuple-element.146), channel_id=1, source_target_pairs={{0,6},{1,7},{2,4},{3,5},{4,2},{5,3},{6,0},{7,1},{8,14},{9,15},{10,... | collective-permute-start | bytes 442376 | tf_op jit(solution)/shard_map/ppermute | solution.py:1009
  182.4 9.6 %copy-start.23 = (s32[1,1024]{1,0:T(1,128)S(1)}, s32[1,1024]{1,0:T(1,128)}, u32[]{:S(2)}) copy-start(s32[1,1024]{1,0:T(1,128)} %constant.34.clone.refs_3_.refs_6_) | copy-start | bytes 12292
  182.4 9.6 %copy-start.34 = (f32[16,1024]{1,0:T(8,128)S(1)}, f32[16,1024]{1,0:T(8,128)}, u32[]{:S(2)}) copy-start(f32[16,1024]{1,0:T(8,128)} %copy-done.33) | copy-start | bytes 196612
  182.4 9.5 %copy-start.37 = (f32[8,768]{1,0:T(8,128)S(1)}, f32[8,768]{1,0:T(8,128)}, u32[]{:S(2)}) copy-start(f32[8,768]{1,0:T(8,128)} %copy-done.36) | copy-start | bytes 73732
  182.4 9.5 %copy-start.39 = (f32[8,768]{1,0:T(8,128)S(1)}, f32[8,768]{1,0:T(8,128)}, u32[]{:S(2)}) copy-start(f32[8,768]{1,0:T(8,128)} %copy-done.38) | copy-start | bytes 73732
  194.6 3.3 %collective-permute-start.16 = (f32[4,16,256]{2,1,0:T(8,128)}, f32[4,16,256]{2,1,0:T(8,128)}, u32[]{:S(2)}, u32[]{:S(2)}) collective-permute-start(f32[4,16,256]{2,1,0:T(8,128)} %get-tuple-element.147), channel_id=1, source_target_pairs={{0,1},{1,0},{2,3},{3,2},{4,5},{5,4},{6,7},{7,6},{8,9},{9,8},{10,11... | collective-permute-start | bytes 196616 | tf_op jit(solution)/shard_map/ppermute | solution.py:1009
  198.8 7.9 %collective-permute-start.19 = (f32[4,16,256]{2,1,0:T(8,128)S(1)}, f32[4,16,256]{2,1,0:T(8,128)S(1)}, u32[]{:S(2)}, u32[]{:S(2)}) collective-permute-start(f32[4,16,256]{2,1,0:T(8,128)S(1)} %add.11.refs_1_), channel_id=1, source_target_pairs={{0,24},{8,16},{16,8},{24,0},{1,25},{9,17},{17,9},{25,1},{2,26},{10... | collective-permute-start | bytes 196616 | tf_op jit(solution)/shard_map/ppermute | solution.py:1014
  201.5 5.2 %collective-permute-start.18 = (f32[4,16,256]{2,1,0:T(8,128)S(1)}, f32[4,16,256]{2,1,0:T(8,128)S(1)}, u32[]{:S(2)}, u32[]{:S(2)}) collective-permute-start(f32[4,16,256]{2,1,0:T(8,128)S(1)} %add.11.refs_1_), channel_id=1, source_target_pairs={{0,16},{8,24},{16,0},{24,8},{1,17},{9,25},{17,1},{25,9},{2,18},{10... | collective-permute-start | bytes 196616 | tf_op jit(solution)/shard_map/ppermute | solution.py:1014
  202.0 4.7 %collective-permute-start.17 = (f32[4,16,256]{2,1,0:T(8,128)S(1)}, f32[4,16,256]{2,1,0:T(8,128)S(1)}, u32[]{:S(2)}, u32[]{:S(2)}) collective-permute-start(f32[4,16,256]{2,1,0:T(8,128)S(1)} %add.11.refs_1_), channel_id=1, source_target_pairs={{0,8},{8,0},{16,24},{24,16},{1,9},{9,1},{17,25},{25,17},{2,10},{10... | collective-permute-start | bytes 196616 | tf_op jit(solution)/shard_map/ppermute | solution.py:1014
  202.5 12.9 %all-to-all-start.4 = ((bf16[4,96,768]{2,1,0:T(8,128)(2,1)}), bf16[4,96,768]{2,1,0:T(8,128)(2,1)}, u32[]{:S(2)}, u32[]{:S(2)}) async-start(bf16[4,96,768]{2,1,0:T(8,128)(2,1)} %hold.9), calls=%async_computation.5 | async-start | bytes 1179648 | tf_op jit(solution)/shard_map/all_to_all | solution.py:1022
  208.7 10.9 %collective-permute-start.20 = (bf16[112,768]{1,0:T(8,128)(2,1)S(1)}, bf16[112,768]{1,0:T(8,128)(2,1)S(1)}, u32[]{:S(2)}, u32[]{:S(2)}) collective-permute-start(bf16[112,768]{1,0:T(8,128)(2,1)S(1)} %get-tuple-element.149), channel_id=1, source_target_pairs={{0,2},{1,3},{2,0},{3,1},{4,6},{5,7},{6,4},{7,5},{8,10},{9,11},{10,... | collective-permute-start | bytes 516104 | tf_op jit(solution)/shard_map/ppermute | solution.py:1009
  209.2 15.6 %collective-permute-start.21 = (bf16[112,768]{1,0:T(8,128)(2,1)S(1)}, bf16[112,768]{1,0:T(8,128)(2,1)S(1)}, u32[]{:S(2)}, u32[]{:S(2)}) collective-permute-start(bf16[112,768]{1,0:T(8,128)(2,1)S(1)} %get-tuple-element.150), channel_id=1, source_target_pairs={{0,4},{1,5},{2,6},{3,7},{4,0},{5,1},{6,2},{7,3},{8,12},{9,13},{10,... | collective-permute-start | bytes 516104 | tf_op jit(solution)/shard_map/ppermute | solution.py:1009
  211.8 13.0 %collective-permute-start.22 = (bf16[112,768]{1,0:T(8,128)(2,1)S(1)}, bf16[112,768]{1,0:T(8,128)(2,1)S(1)}, u32[]{:S(2)}, u32[]{:S(2)}) collective-permute-start(bf16[112,768]{1,0:T(8,128)(2,1)S(1)} %get-tuple-element.151), channel_id=1, source_target_pairs={{0,6},{1,7},{2,4},{3,5},{4,2},{5,3},{6,0},{7,1},{8,14},{9,15},{10,... | collective-permute-start | bytes 516104 | tf_op jit(solution)/shard_map/ppermute | solution.py:1009
  215.5 12.1 %all-to-all-start.5 = ((bf16[4,96,768]{2,1,0:T(8,128)(2,1)}), bf16[4,96,768]{2,1,0:T(8,128)(2,1)}, u32[]{:S(2)}, u32[]{:S(2)}) async-start(bf16[4,96,768]{2,1,0:T(8,128)(2,1)} %hold.10), calls=%async_computation.6 | async-start | bytes 1179648 | tf_op jit(solution)/shard_map/all_to_all | solution.py:1022
  (29 other events, 72.9 us)
Sparse Core Ops, SparseCore 0:
  37.9 51.9 all-gather.1
  129.5 55.2 reduce-scatter.1

commit v2 on v1

--- a/solution.py
+++ b/solution.py
@@ -35,7 +35,7 @@
 
 def size_of(x):
     shape = list(x.shape)
-    shape[-1] = -(-shape[-1] // 128) * 128
+    shape[-1] = -(-shape[-1] // 1024) * 1024 if len(shape) == 1 else -(-shape[-1] // 128) * 128
     if len(shape) > 1:
         shape[-2] = -(-shape[-2] // 8) * 8
     return math.prod(shape) * jnp.dtype(x.dtype).itemsize
@@ -146,30 +146,31 @@
     return widen(block, width) if width > 256 else block
 
 
-def first_kernel(where, query, key, value, out, *refs):
+def first_kernel(query, key, value, out, *refs):
     vectors, up_b, table = refs[:8], refs[8], refs[9]
     own, quarter = refs[10:]
     share, width = query.shape
     for j, weight in enumerate((query, key, value, out)):
         own[j] = weight[...]
-    quarter[:share, :] = own[where[0]]
+    quarter[:share, :] = own[lax.axis_index("narrow")]
     lines = [widen(v[...].astype(F32), 128) for v in vectors]
+    wide_b = up_b[...].astype(F32).reshape(1, 4 * share)
     for j in range(4):
-        lines.append(widen(up_b[...].astype(F32)[:, j * share : (j + 1) * share], 128))
+        lines.append(widen(wide_b[:, j * share : (j + 1) * share], 128))
     lines.append(jnp.zeros((4, 128), F32))
     small = small_block(jnp.concatenate(lines, 0), table[...].astype(F32), width)
     quarter[share:, :] = small.astype(BF16)
 
 
-def first_blocks(where, weights, vectors, up_b, table):
+def first_blocks(weights, vectors, up_b, table):
     share, width = weights[0].shape
     return call(
         first_kernel,
         "first_blocks",
         3,
         [sds((4, share, width), BF16), sds((share + 16, width), BF16)],
-        [where, *weights, *vectors, up_b, table],
-        "s" + "v" * 14,
+        [*weights, *vectors, up_b, table],
+        "v" * 14,
         large=56,
     )
 
@@ -416,23 +417,22 @@
     return center * inverse, inverse
 
 
-def load_squares(where, mine, other, weights, sem):
+def load_squares(where, mine, other, weights, sems):
     share = weights.shape[1] // 8
-    started = []
-
-    def start(source, quarter, shard):
-        line = pl.ds(pl.multiple_of(shard * share, share), share)
-        copy = pltpu.make_async_copy(source, weights.at[quarter, line, :], sem)
-        copy.start()
-        started.append(copy)
-
-    for side, (own, plane) in enumerate((mine, other)):
-        core = where[2] ^ side
-        for j in range(4):
-            start(own.at[j], j, where[1] * 2 + core)
-            for k in range(1, 4):
-                start(plane.at[j, k - 1], j, (where[1] ^ k) * 2 + core)
-    return started
+    quarters = []
+    for j in range(4):
+        started = []
+        for side, (own, plane) in enumerate((mine, other)):
+            core = where[2] ^ side
+            sources = [own.at[j]] + [plane.at[j, k - 1] for k in range(1, 4)]
+            for k, source in enumerate(sources):
+                shard = (where[1] ^ k) * 2 + core
+                line = pl.ds(pl.multiple_of(shard * share, share), share)
+                copy = pltpu.make_async_copy(source, weights.at[j, line, :], sems.at[j])
+                copy.start()
+                started.append(copy)
+        quarters.append(started)
+    return quarters
 
 
 def finish(copies):
@@ -444,12 +444,15 @@
     mine, other = refs[:2], refs[2:4]
     query, key, value, soft, mixed, unit, inverse, normed, normed_low, weights, sem = refs[4:]
     clips, pairs, rows = position.shape[:3]
-    finish(load_squares(where, mine, other, weights, sem))
+    quarters = load_squares(where, mine, other, weights, sem)
+    finish(quarters[0])
     query_b, value_b, out_b = vectors[0:1, :], vectors[1:2, :], vectors[2:3, :]
     gain, shift = vectors[4:5, :], vectors[5:6, :]
     x = picked[...]
     query[...] = ((dot(x, weights[0]) + query_b).astype(BF16).astype(F32) * 0.125).astype(BF16)
+    finish(quarters[1])
     key[...] = dot(x, weights[1]).astype(BF16)
+    finish(quarters[2])
     value[...] = (dot(x, weights[2]) + value_b).astype(BF16)
 
     def clip_step(c, carry):
@@ -471,6 +474,7 @@
         return carry
 
     lax.fori_loop(0, clips, clip_step, 0)
+    finish(quarters[3])
     attended = dot(mixed[...], weights[3]) + out_b
     units, inv = unit_norm(ALPHA * x.astype(F32) + attended)
     unit[...] = units
@@ -503,7 +507,7 @@
         ],
         [where, visible, picked, gates, position, vectors, *mine, *other],
         "ssvvvv" + "a" * 4,
-        [pltpu.SemaphoreType.DMA],
+        [pltpu.SemaphoreType.DMA((4,))],
         after,
         large=MOST,
     )
@@ -553,20 +557,14 @@
     up_copies = load_squares(where, *ups, up_w, up_sem)
     down_copies = [pltpu.make_async_copy(down, down_w, down_sem)]
     down_copies[0].start()
-    finish(up_copies)
-
-    def up_step(k, carry):
-        bias = vectors[pl.ds(8 + k, 1), :]
-        parts = [
-            dot(normed_low[r : r + UPROWS, :], up_w[k]) for r in range(0, rows, UPROWS)
-        ]
-        for i, part in enumerate(parts):
-            activated, derivative = gelu_parts(part + bias)
-            active[k, i * UPROWS : (i + 1) * UPROWS, :] = activated.astype(BF16)
-            slope[k, i * UPROWS : (i + 1) * UPROWS, :] = derivative
-        return carry
-
-    lax.fori_loop(0, chunks, up_step, 0)
+    for k in range(chunks):
+        finish(up_copies[k])
+        for r in range(0, rows, UPROWS):
+            cut = slice(r, r + UPROWS)
+            hidden = dot(normed_low[cut, :], up_w[k]) + vectors[8 + k : 9 + k, :]
+            activated, derivative = gelu_parts(hidden)
+            active[k, cut, :] = activated.astype(BF16)
+            slope[k, cut, :] = derivative
     finish(down_copies)
     total = dot(active[0], down_w[0])
     for k in range(1, chunks):
@@ -664,7 +662,8 @@
             parts,
             deep,
         ]
-        + [pltpu.SemaphoreType.DMA] * 4,
+        + [pltpu.SemaphoreType.DMA((4,))]
+        + [pltpu.SemaphoreType.DMA] * 3,
         after,
         "aaavvvv",
         large=MOST,
@@ -1018,6 +1017,10 @@
     return [swap_wide(quarter, 2 * k) for k in range(1, 4)]
 
 
+def plane_of(part):
+    return [swap_narrow(part, m) for m in range(1, 4)]
+
+
 def trade(parts):
     return lax.all_to_all(parts, "narrow", 0, 0)
 
@@ -1038,6 +1041,15 @@
 
 def sum_four(a, b, c, d):
     return (a.astype(F32) + b.astype(F32)) + (c.astype(F32) + d.astype(F32))
+
+
+def halves(small, width):
+    high = small.astype(BF16).astype(F32)
+    return widen(jnp.concatenate([high, small - high], 1), width).astype(BF16)
+
+
+def whole_of(both, lanes):
+    return both[:, :lanes] + both[:, lanes : 2 * lanes]
 
 
 def plane_sum_kernel(parts, *refs):
@@ -1046,10 +1058,7 @@
     for k, out in enumerate(outs):
         out[:share, :] = sum_four(*(parts[j, k] for j in range(4))).astype(BF16)
         if smalls:
-            small = sum_four(*(small[k] for small in smalls))
-            high = small.astype(BF16).astype(F32)
-            split = jnp.concatenate([high, small - high], 1)
-            out[share:, :] = widen(split, out.shape[1]).astype(BF16)
+            out[share:, :] = halves(smalls[0][k] + smalls[1][k], out.shape[1])
 
 
 def plane_sum(parts, smalls=(), after=()):
@@ -1074,52 +1083,52 @@
 
 
 def column_sum_kernel(a, b, c, d, out):
-    total = sum_four(a[...], b[...], c[...], d[...]).astype(BF16)
-    for j in range(4):
-        out[j] = total
+    out[...] = sum_four(a[...], b[...], c[...], d[...]).astype(BF16)
 
 
 def column_sum(parts, after=()):
-    out = sds((4,) + parts[0].shape, BF16)
-    return call(column_sum_kernel, "column_sum", 20, out, parts, "vvvv", after=after)
-
-
-def square_sum_kernel(a, b, c, d, out, small):
-    share = out.shape[0]
+    out = [sds(parts[0].shape, BF16)]
+    return call(column_sum_kernel, "column_sum", 20, out, parts, "vvvv", after=after)[0]
+
+
+def square_sum_kernel(a, b, c, d, out):
+    share = out.shape[0] - 16
     total = sum_four(a[...], b[...], c[...], d[...])
-    out[...] = total[:share].astype(BF16)
-    lanes = small.shape[1]
-    small[...] = total[share:, :lanes] + total[share:, lanes : 2 * lanes]
-
-
-def square_sum(parts, share, after=()):
-    lines, width = parts[0].shape
-    out = [sds((share, width), BF16), sds((lines - share, 256), F32)]
-    return call(square_sum_kernel, "square_sum", 20, out, parts, "vvvv", after=after)
+    out[:share, :] = total[:share].astype(BF16)
+    out[share:, :] = halves(whole_of(total[share:], 256), out.shape[1])
+
+
+def square_sum(parts, after=()):
+    out = [sds(parts[0].shape, BF16)]
+    return call(square_sum_kernel, "square_sum", 20, out, parts, "vvvv", after=after)[0]
 
 
 def end_sum_kernel(ups, square, out):
+    share = ups.shape[1]
     up = sum_four(*(ups[j] for j in range(4))).astype(BF16)
     for j in range(4):
-        out[j, 0] = up
-        out[j, 1] = square[...]
+        out[j, :share, :] = up
+        out[j, share:, :] = square[...]
 
 
 def end_sum(ups, square, after=()):
-    out = sds((4, 2) + square.shape, BF16)
+    share, width = ups.shape[1:]
+    out = sds((4, share + square.shape[0], width), BF16)
     return call(end_sum_kernel, "end_sum", 2, out, [ups, square], "vv", after=after)
 
 
-def last_kernel(*refs):
-    ends, small, downs = refs[:3]
-    query, key, value, out, up, down = refs[3:9]
-    vectors = refs[9:18]
-    table, gate_weight, gate_bias, gate_scale = refs[18:]
+def last_kernel(where, *refs):
+    ends, downs = refs[0], refs[1:5]
+    query, key, value, out, up, down = refs[5:11]
+    vectors = refs[11:20]
+    table, gate_weight, gate_bias, gate_scale = refs[20:]
     share, width = query.shape
     for j, target in enumerate((query, key, value, out)):
-        up[:, j * width : (j + 1) * width] = ends[j, 0].astype(F32)
-        target[...] = ends[j, 1].astype(F32)
-        down[j * share : (j + 1) * share, :] = downs[j].astype(F32)
+        up[:, j * width : (j + 1) * width] = ends[j, :share].astype(F32)
+        target[...] = ends[j, share : 2 * share].astype(F32)
+        line = pl.multiple_of((where[0] ^ j) * share, share)
+        down[pl.ds(line, share), :] = downs[j][...].astype(F32)
+    small = whole_of(sum_four(*(ends[j, 2 * share :] for j in range(4))), 256)
     sums = small[:, :128]
     heads, count = table.shape
     table[...] = small[:heads, 128 : 128 + count]
@@ -1131,7 +1140,7 @@
     for target, line in zip(
         vectors, (query_b, value_b, out_b, up_b, down_b, gain1, shift1, gain2, shift2)
     ):
-        target[...] = line
+        target[...] = line.reshape(target.shape)
     logits, size = gate_weight.shape
     half = logits // 2
     gate_weight[...] = jnp.where(
@@ -1145,8 +1154,8 @@
     gate_scale[...] = pltpu.roll(line, 96, 1)[:, :heads]
 
 
-def last(ends, small, downs, heads, logits):
-    share, width = ends.shape[2:]
+def last(where, ends, downs, heads, logits):
+    share, width = downs[0].shape
     line = sds((1, share), F32)
     return call(
         last_kernel,
@@ -1155,7 +1164,7 @@
         [sds((share, width), F32)] * 4
         + [sds((share, 4 * width), F32), sds((4 * share, width), F32)]
         + [line] * 3
-        + [sds((1, 4 * share), F32)]
+        + [sds((4 * share,), F32)]
         + [line] * 5
         + [
             sds((heads, NUM_BUCKETS // 8), F32),
@@ -1163,8 +1172,8 @@
             sds((1, logits), F32),
             sds((1, heads), F32),
         ],
-        [ends, small, downs],
-        "vvv",
+        [where, ends, *downs],
+        "s" + "v" * 5,
     )
 
 
@@ -1214,7 +1223,7 @@
     if fast:
         where = jnp.stack([me_narrow, me_wide // 2, me_wide % 2]).astype(jnp.int32)
         own_square, square_quarter = first_blocks(
-            where, squares, [v[None, :] for v in vectors], up_bias[None, :], bias_table.T
+            squares, [v[None, :] for v in vectors], up_bias, bias_table.T
         )
         picked, first, second, gates = pick(
             patch_order, visible, gate_bias, gate_scale, tokens, gate_lines, rows, square_quarter
@@ -1299,15 +1308,12 @@
         spread = lambda parts: [parts[0]] + [swap_wide(parts[k], 2 * k) for k in range(1, 4)]
         up_part = up_parts(up_sum, width, (small_keep,))
         down_part = column_sum(spread(down_parts), (up_part,))
-        small = small_keep + hold(swap_wide(small_send, 1), (down_part,))
-        smalls = [small] + [swap_narrow(small, m) for m in range(1, 4)]
-        square_plane = trade(square_parts)
-        square_parts = plane_sum(square_plane, smalls)
-        downs = trade(hold(down_part, (square_plane,)))
-        ups = trade(hold(up_part, (downs,)))
-        square, small = square_sum(spread(square_parts), share)
-        ends = trade(end_sum(ups, square))
-        ends = last(ends, small, downs, heads, gate_lines.shape[0])
+        smalls = (small_keep, hold(swap_wide(small_send, 1), (down_part,)))
+        square_parts = plane_sum(trade(square_parts), smalls)
+        downs = [down_part, *plane_of(down_part)]
+        ups = trade(hold(up_part, (square_parts[0],)))
+        ends = trade(end_sum(ups, square_sum(spread(square_parts))))
+        ends = last(where, ends, downs, heads, gate_lines.shape[0])
         weight_grads, ends = ends[:6], ends[6:]
         vector_grads = [v.reshape(-1) for v in ends[:9]]
         table_grad, gate_weight_grad = ends[9].T, ends[10].T

time: 257 us -> 255 us (level)
  waiting for transfers between devices: 41.6 us -> 59.4 us
  blocking collectives: 16.3 us -> 0 us
    ppermute x3, waiting for transfers between devices: 0.01 us -> 16.6 us  [swap_narrow(): return lax.ppermute(x, 'narrow', [(i, i ^ flip) for i in range(size)])]
    all_to_all x1 -> x0, blocking collectives: 16.3 us -> none  [trade(): return lax.all_to_all(parts, 'narrow', 0, 0)]
    unnamed x92 -> x100, local copies, waits for them, and re-layouts: 13 us -> 13.6 us
  transfers between devices with their start and end apart: 31 -> 31, of which waited for: 9 -> 11; matrix products, arithmetic and copies ran while one was open for 0% -> 0% of each run, Pallas kernels for 30% -> 30%
where the time goes in v2:
time: 255 us; the launch traced here: 253 us
  Pallas kernels  116 us (45%)
  waiting for transfers between devices  59.4 us (23%)
  starting transfers between devices  49.2 us (19%)
  between operations  14.7 us (6%)
  local copies, waits for them, and re-layouts  13.6 us (5%)
    pallas_call x19, Pallas kernels, call(): pl.pallas_call(run, in_specs=[spaces[k] for k in kinds] + [ANY] * len(aft...  92.8 us
    all_to_all x6, starting transfers between devices, trade(): return lax.all_to_all(parts, 'narrow', 0, 0)  26.2 us
    all_to_all x6, waiting for transfers between devices, trade(): return lax.all_to_all(parts, 'narrow', 0, 0)  25 us
    ppermute x20, starting transfers between devices, swap_wide(): return lax.ppermute(x, 'wide', [(i, i ^ flip) for i in range(size)])  19.4 us
    ppermute x20, waiting for transfers between devices, swap_wide(): return lax.ppermute(x, 'wide', [(i, i ^ flip) for i in range(size)])  17.8 us
    ppermute x3, waiting for transfers between devices, swap_narrow(): return lax.ppermute(x, 'narrow', [(i, i ^ flip) for i in range(size)])  16.6 us
    unnamed x100, local copies, waits for them, and re-layouts  13.6 us
    pallas_call x1, Pallas kernels, attend_back(): pl.pallas_call(attend_back_kernel, grid=(clips,), in_specs=[SMEM, lines,...  13.5 us
  transfers between devices with their start and end apart: 31, of which 11 were waited for; matrix products, arithmetic and copies ran while one was open for 0% of the time, Pallas kernels for 30%

profile of v2, /device:TPU:0, one launch (start us, length us, event | category | flops | bytes accessed | tf_op | source)
XLA Modules:
  0.0 253.3 jit_solution(5931822911286321569)
XLA Ops:
  7.3 2.1 first_blocks.1
  9.4 5.0 %collective-permute-start.2 = (bf16[112,768]{1,0:T(8,128)(2,1)}, bf16[112,768]{1,0:T(8,128)(2,1)S(1)}, u32[]{:S(2)}, u32[]{:S(2)}) collective-permute-start(bf16[112,768]{1,0:T(8,128)(2,1)} %get-tuple-element.95.token.refs_0_), channel_id=1, source_target_pairs={{0,6},{1,7},{2,4},{3,5},{4,2},{5,3},{6,0},{7,1},{8,14},{9,15},{10,... | collective-permute-start | bytes 516104 | tf_op jit(solution)/shard_map/ppermute | solution.py:1008
  15.2 0.9 copy-done.12
  16.1 4.9 %pick.1 = (bf16[512,768]{1,0:T(8,128)(2,1)S(1)}, f32[4,16,128]{2,1,0:T(8,128)S(1)}, f32[4,16,128]{2,1,0:T(8,128)S(1)}, f32[4,16,128]{2,1,0:T(8,128)S(1)}) custom-call(s32[4,496]{1,0:T(4,128)S(1)} %copy-done.15, s32[4]{0:T(128)S(1)} %copy-done.21, f32[8]{0:T(128)S(1)} %copy-done.20, f32[12]{0:T(128)S(1)} %copy-done.22, bf16[4,496,768]{2,1,0:T(8,128)(2,1)} %tokens.1, ...), custom_call_target="tpu_custom_call" | custom-call | flops 60000002048 | bytes 210000000 | tf_op jit(solution)/shard_map/pick/pallas_call | solution.py:293
  21.9 7.4 %collective-permute-done.1.refs_2_ = bf16[112,768]{1,0:T(8,128)(2,1)S(1)} collective-permute-done((bf16[112,768]{1,0:T(8,128)(2,1)}, bf16[112,768]{1,0:T(8,128)(2,1)S(1)}, u32[]{:S(2)}, u32[]{:S(2)}) %collective-permute-start.1) | collective-permute-done | bytes 172064 | tf_op jit(solution)/shard_map/ppermute | solution.py:1008
  29.3 2.0 first_column.1
  31.4 2.5 %collective-permute-start.8 = (bf16[96,768]{1,0:T(8,128)(2,1)S(1)}, bf16[96,768]{1,0:T(8,128)(2,1)S(1)}, u32[]{:S(2)}, u32[]{:S(2)}) collective-permute-start(bf16[96,768]{1,0:T(8,128)(2,1)S(1)} %get-tuple-element.106), channel_id=1, source_target_pairs={{0,6},{1,7},{2,4},{3,5},{4,2},{5,3},{6,0},{7,1},{8,14},{9,15},{10,... | collective-permute-start | bytes 442376 | tf_op jit(solution)/shard_map/ppermute | solution.py:1008
  34.0 1.9 collective-permute-start.6
  35.9 4.4 %all-to-all-start = ((bf16[4,3,96,768]{3,2,1,0:T(8,128)(2,1)}), bf16[4,3,96,768]{3,2,1,0:T(8,128)(2,1)}, u32[]{:S(2)}, u32[]{:S(2)}) async-start(bf16[4,3,96,768]{3,2,1,0:T(8,128)(2,1)} %get-tuple-element.103), calls=%async_computation | async-start | bytes 3538944 | tf_op jit(solution)/shard_map/all_to_all | solution.py:1025
  40.4 8.3 %position.1 = (bf16[4,6,128,256]{3,2,1,0:T(8,128)(2,1)S(1)}, f32[16,768]{1,0:T(8,128)S(1)}) custom-call(s32[3]{0:T(128)S(1)} %pad_add_fusion.refs_0_.where, s32[4,496]{1,0:T(4,128)S(1)} %copy-done.15, s32[4]{0:T(128)S(1)} %copy-done.21, s32[1,1024]{1,0:T(1,128)S(1)} %copy-done.24, bf16[4,16,768]{2,1,0:T(8,128)(2,1)S(1)} %get-tuple-element.99.refs_4_, ...), custom_call_target="tpu_custom_call" | custom-call | flops 109999996928 | bytes 385000000 | tf_op jit(solution)/shard_map/position/pallas_call | solution.py:86
  49.3 1.2 copy-done.35
  50.5 12.2 %all-to-all-done.refs_0_ = bf16[4,3,96,768]{3,2,1,0:T(8,128)(2,1)} async-done(((bf16[4,3,96,768]{3,2,1,0:T(8,128)(2,1)}), bf16[4,3,96,768]{3,2,1,0:T(8,128)(2,1)}, u32[]{:S(2)}, u32[]{:S(2)}) %all-to-all-start) | async-done | bytes 1769504 | tf_op jit(solution)/shard_map/all_to_all | solution.py:1025
  63.6 1.2 copy-done
  64.8 4.4 %all-to-all-start.1 = ((bf16[4,3,96,768]{3,2,1,0:T(8,128)(2,1)}), bf16[4,3,96,768]{3,2,1,0:T(8,128)(2,1)}, u32[]{:S(2)}, u32[]{:S(2)}) async-start(bf16[4,3,96,768]{3,2,1,0:T(8,128)(2,1)} %hold.6), calls=%async_computation.1 | async-start | bytes 3538944 | tf_op jit(solution)/shard_map/all_to_all | solution.py:1025
  69.3 14.8 %attend.1 = (bf16[512,768]{1,0:T(8,128)(2,1)S(1)}, bf16[512,768]{1,0:T(8,128)(2,1)}, bf16[512,768]{1,0:T(8,128)(2,1)}, f32[4,6,128,256]{3,2,1,0:T(8,128)}, bf16[...) custom-call(s32[3]{0:T(128)S(1)} %pad_add_fusion.refs_0_.where, ...), custom_call_target="tpu_custom_call" | custom-call | flops 140000002048 | bytes 490000000 | tf_op jit(solution)/shard_map/attend/pallas_call | solution.py:86
  84.2 0.9 copy-done.39
  85.1 5.8 %all-to-all-done.1.refs_0_ = bf16[4,3,96,768]{3,2,1,0:T(8,128)(2,1)} async-done(((bf16[4,3,96,768]{3,2,1,0:T(8,128)(2,1)}), bf16[4,3,96,768]{3,2,1,0:T(8,128)(2,1)}, u32[]{:S(2)}, u32[]{:S(2)}) %all-to-all-start.1) | async-done | bytes 1769504 | tf_op jit(solution)/shard_map/all_to_all | solution.py:1025
  90.9 1.0 copy-done.11
  91.9 3.5 %collective-permute-done.9.refs_8_ = bf16[4,96,768]{2,1,0:T(8,128)(2,1)S(1)} collective-permute-done((bf16[4,96,768]{2,1,0:T(8,128)(2,1)S(1)}, bf16[4,96,768]{2,1,0:T(8,128)(2,1)S(1)}, u32[]{:S(2)}, u32[]{:S(2)}) %collective-permute-start.9) | collective-permute-done | bytes 589856 | tf_op jit(solution)/shard_map/ppermute | solution.py:1008
  95.5 29.3 %feed.1 = (bf16[4,4,96,768]{3,2,1,0:T(8,128)(2,1)}, bf16[4,4,96,768]{3,2,1,0:T(8,128)(2,1)}, bf16[768,3072]{1,0:T(8,128)(2,1)}, bf16[512,768]{1,0:T(8,128)(2,1)}...) custom-call(s32[3]{0:T(128)S(1)} %pad_add_fusion.refs_0_.where, s32[4]{0:T(128)S(1)} %copy-done.21, ...), custom_call_target="tpu_custom_call" | custom-call | flops 320000000000 | bytes 1120000000 | tf_op jit(solution)/shard_map/feed/pallas_call | solution.py:86
  126.2 0.9 copy-done.34
  127.1 5.1 %mix_back.1 = (f32[512,768]{1,0:T(8,128)}, bf16[768,768]{1,0:T(8,128)(2,1)}, bf16[512,768]{1,0:T(8,128)(2,1)S(1)}, f32[8,768]{1,0:T(8,128)S(1)}) custom-call(f32[512,768]{1,0:T(8,128)} %get-tuple-element.109.refs_0_, f32[512,768]{1,0:T(8,128)} %get-tuple-element.110.refs_1_, f32[512,1]{1,0:T(8,128)S(1)} %get-tuple-element.111.refs_2_, ...), custom_call_target="tpu_custom_call" | custom-call | flops 60000002048 | bytes 210000000 | tf_op jit(solution)/shard_map/mix_back/pallas_call | solution.py:712
  132.2 1.9 core_sum.2.refs_0_
  134.1 4.6 %all-to-all-start.2 = ((bf16[4,4,96,768]{3,2,1,0:T(8,128)(2,1)}), bf16[4,4,96,768]{3,2,1,0:T(8,128)(2,1)}, u32[]{:S(2)}, u32[]{:S(2)}) async-start(bf16[4,4,96,768]{3,2,1,0:T(8,128)(2,1)} %core_sum.2.refs_0_), calls=%async_computation.2 | async-start | bytes 4718592 | tf_op jit(solution)/shard_map/all_to_all | solution.py:1025
  138.8 13.5 %attend_back.1 = (bf16[4,4,96,768]{3,2,1,0:T(8,128)(2,1)}, bf16[4,4,96,768]{3,2,1,0:T(8,128)(2,1)}, bf16[512,768]{1,0:T(8,128)(2,1)S(1)}, bf16[512,768]{1,0:T(8,...) custom-call(s32[3]{0:T(128)S(1)} %pad_add_fusion.refs_0_.where, ...), custom_call_target="tpu_custom_call" | custom-call | flops 149999992832 | bytes 525000000 | tf_op jit(solution)/shard_map/attend_back/pallas_call | solution.py:782
  152.5 1.4 copy-done.36
  153.9 8.8 %table_back.1.refs_2_.refs_5_ = f32[16,1024]{1,0:T(8,128)S(1)} custom-call(s32[4,496]{1,0:T(4,128)S(1)} %copy-done.16, s32[4]{0:T(128)S(1)} %copy-done.21, bf16[4,6,128,256]{3,2,1,0:T(8,128)(2,1)S(1)} %copy-done.36), custom_call_target="tpu_custom_call" | custom-call | flops 120000004096 | bytes 420000000 | tf_op jit(solution)/shard_map/table_back/pallas_call | solution.py:86
  162.7 1.9 core_sum.3.refs_1_
  165.2 1.9 all-to-all-done.2.refs_0_
  167.1 4.8 %all-to-all-start.3 = ((bf16[4,4,96,768]{3,2,1,0:T(8,128)(2,1)}), bf16[4,4,96,768]{3,2,1,0:T(8,128)(2,1)}, u32[]{:S(2)}, u32[]{:S(2)}) async-start(bf16[4,4,96,768]{3,2,1,0:T(8,128)(2,1)} %core_sum.3.refs_1_), calls=%async_computation.4 | async-start | bytes 4718592 | tf_op jit(solution)/shard_map/all_to_all | solution.py:1025
  172.0 2.6 %plane_sum.2 = (bf16[96,768]{1,0:T(8,128)(2,1)S(1)}, bf16[96,768]{1,0:T(8,128)(2,1)}, bf16[96,768]{1,0:T(8,128)(2,1)}, bf16[96,768]{1,0:T(8,128)(2,1)}) custom-call(bf16[4,4,96,768]{3,2,1,0:T(8,128)(2,1)} %all-to-all-done.2.refs_0_, bf16[4,4,96,768]{3,2,1,0:T(8,128)(2,1)} %core_sum.3.refs_1_), custom_call_target="tpu_custom_call" | custom-call | flops 299999985664 | bytes 1050000000 | tf_op jit(solution)/shard_map/plane_sum/pallas_call | solution.py:86
  174.6 2.9 %collective-permute-start.15 = (bf16[96,768]{1,0:T(8,128)(2,1)}, bf16[96,768]{1,0:T(8,128)(2,1)}, u32[]{:S(2)}, u32[]{:S(2)}) collective-permute-start(bf16[96,768]{1,0:T(8,128)(2,1)} %get-tuple-element.144), channel_id=1, source_target_pairs={{0,4},{1,5},{2,6},{3,7},{4,0},{5,1},{6,2},{7,3},{8,12},{9,13},{10,... | collective-permute-start | bytes 442376 | tf_op jit(solution)/shard_map/ppermute | solution.py:1008
  177.6 1.4 collective-permute-start.16
  179.0 9.5 %tokens_back.1 = (bf16[4,496,768]{2,1,0:T(8,128)(2,1)}, f32[8,128]{1,0:T(8,128)S(1)}, f32[32,768]{1,0:T(8,128)S(1)}) custom-call(s32[4,496]{1,0:T(4,128)S(1)} %copy-done.17, s32[4]{0:T(128)S(1)} %copy-done.21, f32[12]{0:T(128)S(1)} %copy-done.23, f32[512,768]{1,0:T(8,128)} %get-tuple-element.114.refs_3_, bf16[512,768]{1,0:T(8,128)(2,1)S(1)} %get-tuple-element.123.refs_4_, ...), custom_call_target="tpu_custom_call" | custom-call | flops 109999996928 | bytes 385000000 | tf_op jit(solution)/shard_map/tokens_back/pallas_call | solution.py:86
  188.6 2.7 %small_grads.1 = (f32[4,16,256]{2,1,0:T(8,128)S(1)}, f32[4,16,256]{2,1,0:T(8,128)}) custom-call(s32[3]{0:T(128)S(1)} %pad_add_fusion.refs_0_.where, f32[8,768]{1,0:T(8,128)S(1)} %copy-done.43, f32[8,768]{1,0:T(8,128)S(1)} %copy-done.41, f32[8,768]{1,0:T(8,128)S(1)} %get-tuple-element.137.refs_3_, f32[8,768]{1,0:T(8,128)S(1)} %get-tuple-element.138.refs_4_, ...), custom_call_target="tpu_custom_call" | custom-call | flops 40000000000 | bytes 140000000 | tf_op jit(solution)/shard_map/small_grads/pallas_call | solution.py:86
  191.3 1.1 copy-done.3
  192.4 1.3 column_sum.1.refs_1_.refs_2_
  194.4 4.7 %all-to-all-done.3.refs_0_ = bf16[4,4,96,768]{3,2,1,0:T(8,128)(2,1)} async-done(((bf16[4,4,96,768]{3,2,1,0:T(8,128)(2,1)}), bf16[4,4,96,768]{3,2,1,0:T(8,128)(2,1)}, u32[]{:S(2)}, u32[]{:S(2)}) %all-to-all-start.3) | async-done | bytes 2359328 | tf_op jit(solution)/shard_map/all_to_all | solution.py:1025
  199.1 2.0 plane_sum.3
  201.9 3.0 %collective-permute-start.18 = (bf16[112,768]{1,0:T(8,128)(2,1)S(1)}, bf16[112,768]{1,0:T(8,128)(2,1)S(1)}, u32[]{:S(2)}, u32[]{:S(2)}) collective-permute-start(bf16[112,768]{1,0:T(8,128)(2,1)S(1)} %get-tuple-element.148), channel_id=1, source_target_pairs={{0,4},{1,5},{2,6},{3,7},{4,0},{5,1},{6,2},{7,3},{8,12},{9,13},{10,... | collective-permute-start | bytes 516104 | tf_op jit(solution)/shard_map/ppermute | solution.py:1008
  204.8 1.4 collective-permute-start.19
  206.2 4.3 %all-to-all-start.4 = ((bf16[4,96,768]{2,1,0:T(8,128)(2,1)}), bf16[4,96,768]{2,1,0:T(8,128)(2,1)}, u32[]{:S(2)}, u32[]{:S(2)}) async-start(bf16[4,96,768]{2,1,0:T(8,128)(2,1)} %hold.9), calls=%async_computation.5 | async-start | bytes 1179648 | tf_op jit(solution)/shard_map/all_to_all | solution.py:1025
  210.5 6.9 %collective-permute-done.18.refs_2_ = bf16[112,768]{1,0:T(8,128)(2,1)S(1)} collective-permute-done((bf16[112,768]{1,0:T(8,128)(2,1)S(1)}, bf16[112,768]{1,0:T(8,128)(2,1)S(1)}, u32[]{:S(2)}, u32[]{:S(2)}) %collective-permute-start.18) | collective-permute-done | bytes 172064 | tf_op jit(solution)/shard_map/ppermute | solution.py:1008
  217.9 2.2 end_sum.1
  220.2 3.7 %all-to-all-start.5 = ((bf16[4,208,768]{2,1,0:T(8,128)(2,1)}), bf16[4,208,768]{2,1,0:T(8,128)(2,1)S(1)}, u32[]{:S(2)}, u32[]{:S(2)}) async-start(bf16[4,208,768]{2,1,0:T(8,128)(2,1)} %end_sum.1), calls=%async_computation.6 | async-start | bytes 2555904 | tf_op jit(solution)/shard_map/all_to_all | solution.py:1025
  223.9 2.9 %collective-permute-start.22 = (bf16[96,768]{1,0:T(8,128)(2,1)S(1)}, bf16[96,768]{1,0:T(8,128)(2,1)S(1)}, u32[]{:S(2)}, u32[]{:S(2)}) collective-permute-start(bf16[96,768]{1,0:T(8,128)(2,1)S(1)} %copy-done.14), channel_id=1, source_target_pairs={{0,24},{8,16},{16,8},{24,0},{1,25},{9,17},{17,9},{25,1},{2,26},{10... | collective-permute-start | bytes 442376 | tf_op jit(solution)/shard_map/ppermute | solution.py:1013
  227.4 16.0 %collective-permute-done.22.refs_5_ = bf16[96,768]{1,0:T(8,128)(2,1)S(1)} collective-permute-done((bf16[96,768]{1,0:T(8,128)(2,1)S(1)}, bf16[96,768]{1,0:T(8,128)(2,1)S(1)}, u32[]{:S(2)}, u32[]{:S(2)}) %collective-permute-start.22) | collective-permute-done | bytes 147488 | tf_op jit(solution)/shard_map/ppermute | solution.py:1013
  244.0 2.4 last.1
  (144 shorter events, 9.1 us)
Async XLA Ops:
  7.2 88.2 %all-gather.2.cloned.1.call-start = ((), (), s32[]{:S(2)}) async-start(), calls=%async_computation.7 | async-start | bytes 5308416 | tf_op jit(solution)/shard_map/all_gather | solution.py:1221
  7.2 7.9 %copy-start.15 = (s32[4,496]{1,0:T(4,128)S(1)}, s32[4,496]{1,0:T(4,128)}, u32[]{:S(2)}) copy-start(s32[4,496]{1,0:T(4,128)} %refs_0_.5) | copy-start | bytes 23812
  7.3 7.9 %copy-start.18 = (f32[64,8]{0,1:T(8,128)S(1)}, f32[64,8]{0,1:T(8,128)}, u32[]{:S(2)}) copy-start(f32[64,8]{0,1:T(8,128)} %param.44) | copy-start | bytes 6148
  7.3 7.9 %copy-start.20 = (f32[8]{0:T(128)S(1)}, f32[8]{0:T(128)}, u32[]{:S(2)}) copy-start(f32[8]{0:T(128)} %gate_bias.1) | copy-start | bytes 100
  7.3 7.9 %copy-start.21 = (s32[4]{0:T(128)S(1)}, s32[4]{0:T(128)}, u32[]{:S(2)}) copy-start(s32[4]{0:T(128)} %refs_1_.13) | copy-start | bytes 52
  7.3 7.9 %copy-start.22 = (f32[12]{0:T(128)S(1)}, f32[12]{0:T(128)}, u32[]{:S(2)}) copy-start(f32[12]{0:T(128)} %refs_2_.5) | copy-start | bytes 148
  9.4 12.5 %collective-permute-start.2 = (bf16[112,768]{1,0:T(8,128)(2,1)}, bf16[112,768]{1,0:T(8,128)(2,1)S(1)}, u32[]{:S(2)}, u32[]{:S(2)}) collective-permute-start(bf16[112,768]{1,0:T(8,128)(2,1)} %get-tuple-element.95.token.refs_0_), channel_id=1, source_target_pairs={{0,6},{1,7},{2,4},{3,5},{4,2},{5,3},{6,0},{7,1},{8,14},{9,15},{10,... | collective-permute-start | bytes 516104 | tf_op jit(solution)/shard_map/ppermute | solution.py:1008
  14.5 14.8 %collective-permute-start.1 = (bf16[112,768]{1,0:T(8,128)(2,1)}, bf16[112,768]{1,0:T(8,128)(2,1)S(1)}, u32[]{:S(2)}, u32[]{:S(2)}) collective-permute-start(bf16[112,768]{1,0:T(8,128)(2,1)} %get-tuple-element.95.token.refs_0_), channel_id=1, source_target_pairs={{0,4},{1,5},{2,6},{3,7},{4,0},{5,1},{6,2},{7,3},{8,12},{9,13},{10,... | collective-permute-start | bytes 516104 | tf_op jit(solution)/shard_map/ppermute | solution.py:1008
  14.5 14.8 %collective-permute-start = (bf16[112,768]{1,0:T(8,128)(2,1)}, bf16[112,768]{1,0:T(8,128)(2,1)S(1)}, u32[]{:S(2)}, u32[]{:S(2)}) collective-permute-start(bf16[112,768]{1,0:T(8,128)(2,1)} %get-tuple-element.95.token.refs_0_), channel_id=1, source_target_pairs={{0,2},{1,3},{2,0},{3,1},{4,6},{5,7},{6,4},{7,5},{8,10},{9,11},{10,... | collective-permute-start | bytes 516104 | tf_op jit(solution)/shard_map/ppermute | solution.py:1008
  15.2 173.4 %copy-start.4 = (s32[3]{0:T(128)}, s32[3]{0:T(128)S(1)}, u32[]{:S(2)}) copy-start(s32[3]{0:T(128)S(1)} %pad_add_fusion.refs_0_.where) | copy-start | bytes 40
  21.1 48.2 %copy-start.48 = (f32[4,16,128]{2,1,0:T(8,128)}, f32[4,16,128]{2,1,0:T(8,128)S(1)}, u32[]{:S(2)}) copy-start(f32[4,16,128]{2,1,0:T(8,128)S(1)} %get-tuple-element.97.refs_3_.gates) | copy-start | bytes 98308
  21.1 8.2 %copy-start.8 = (bf16[384,768]{1,0:T(8,128)(2,1)S(1)}, bf16[384,768]{1,0:T(8,128)(2,1)}, u32[]{:S(2)}) copy-start(bf16[384,768]{1,0:T(8,128)(2,1)} %refs_4_.1) | copy-start | bytes 1769476
  21.9 9.4 %copy-start.10 = (bf16[4,96,768]{2,1,0:T(8,128)(2,1)}, bf16[4,96,768]{2,1,0:T(8,128)(2,1)S(1)}, u32[]{:S(2)}) copy-start(bf16[4,96,768]{2,1,0:T(8,128)(2,1)S(1)} %get-tuple-element.98.refs_5_.refs_6_) | copy-start | bytes 1769476
  31.3 9.0 %collective-permute-start.3 = (bf16[4,16,768]{2,1,0:T(8,128)(2,1)S(1)}, bf16[4,16,768]{2,1,0:T(8,128)(2,1)S(1)}, u32[]{:S(2)}, u32[]{:S(2)}) collective-permute-start(bf16[4,16,768]{2,1,0:T(8,128)(2,1)S(1)} %get-tuple-element.99.refs_4_), channel_id=1, source_target_pairs={{0,1},{1,0},{2,3},{3,2},{4,5},{5,4},{6,7},{7,6},{8,9},{9,8},{10,11... | collective-permute-start | bytes 294920 | tf_op jit(solution)/shard_map/ppermute | solution.py:1008
  31.4 31.3 %collective-permute-start.8 = (bf16[96,768]{1,0:T(8,128)(2,1)S(1)}, bf16[96,768]{1,0:T(8,128)(2,1)S(1)}, u32[]{:S(2)}, u32[]{:S(2)}) collective-permute-start(bf16[96,768]{1,0:T(8,128)(2,1)S(1)} %get-tuple-element.106), channel_id=1, source_target_pairs={{0,6},{1,7},{2,4},{3,5},{4,2},{5,3},{6,0},{7,1},{8,14},{9,15},{10,... | collective-permute-start | bytes 442376 | tf_op jit(solution)/shard_map/ppermute | solution.py:1008
  34.0 28.8 %collective-permute-start.7 = (bf16[96,768]{1,0:T(8,128)(2,1)S(1)}, bf16[96,768]{1,0:T(8,128)(2,1)S(1)}, u32[]{:S(2)}, u32[]{:S(2)}) collective-permute-start(bf16[96,768]{1,0:T(8,128)(2,1)S(1)} %get-tuple-element.106), channel_id=1, source_target_pairs={{0,4},{1,5},{2,6},{3,7},{4,0},{5,1},{6,2},{7,3},{8,12},{9,13},{10,... | collective-permute-start | bytes 442376 | tf_op jit(solution)/shard_map/ppermute | solution.py:1008
  34.0 28.8 %collective-permute-start.6 = (bf16[96,768]{1,0:T(8,128)(2,1)S(1)}, bf16[96,768]{1,0:T(8,128)(2,1)S(1)}, u32[]{:S(2)}, u32[]{:S(2)}) collective-permute-start(bf16[96,768]{1,0:T(8,128)(2,1)S(1)} %get-tuple-element.106), channel_id=1, source_target_pairs={{0,2},{1,3},{2,0},{3,1},{4,6},{5,7},{6,4},{7,5},{8,10},{9,11},{10,... | collective-permute-start | bytes 442376 | tf_op jit(solution)/shard_map/ppermute | solution.py:1008
  35.9 33.4 %collective-permute-start.4 = (bf16[4,96,768]{2,1,0:T(8,128)(2,1)S(1)}, bf16[4,96,768]{2,1,0:T(8,128)(2,1)S(1)}, u32[]{:S(2)}, u32[]{:S(2)}) collective-permute-start(bf16[4,96,768]{2,1,0:T(8,128)(2,1)S(1)} %copy-done.9), channel_id=1, source_target_pairs={{0,1},{1,0},{2,3},{3,2},{4,5},{5,4},{6,7},{7,6},{8,9},{9,8},{10,11... | collective-permute-start | bytes 1769480 | tf_op jit(solution)/shard_map/ppermute | solution.py:1008
  35.9 26.8 %all-to-all-start = ((bf16[4,3,96,768]{3,2,1,0:T(8,128)(2,1)}), bf16[4,3,96,768]{3,2,1,0:T(8,128)(2,1)}, u32[]{:S(2)}, u32[]{:S(2)}) async-start(bf16[4,3,96,768]{3,2,1,0:T(8,128)(2,1)} %get-tuple-element.103), calls=%async_computation | async-start | bytes 3538944 | tf_op jit(solution)/shard_map/all_to_all | solution.py:1025
  62.7 6.6 %collective-permute-start.5 = (bf16[4,3,96,768]{3,2,1,0:T(8,128)(2,1)}, bf16[4,3,96,768]{3,2,1,0:T(8,128)(2,1)}, u32[]{:S(2)}, u32[]{:S(2)}) collective-permute-start(bf16[4,3,96,768]{3,2,1,0:T(8,128)(2,1)} %hold.5.refs_7_.refs_1_), channel_id=1, source_target_pairs={{0,1},{1,0},{2,3},{3,2},{4,5},{5,4},{6,7},{7,6},{8,9},{9,8},{10,11... | collective-permute-start | bytes 5308424 | tf_op jit(solution)/shard_map/ppermute | solution.py:1008
  64.8 26.0 %all-to-all-start.1 = ((bf16[4,3,96,768]{3,2,1,0:T(8,128)(2,1)}), bf16[4,3,96,768]{3,2,1,0:T(8,128)(2,1)}, u32[]{:S(2)}, u32[]{:S(2)}) async-start(bf16[4,3,96,768]{3,2,1,0:T(8,128)(2,1)} %hold.6), calls=%async_computation.1 | async-start | bytes 3538944 | tf_op jit(solution)/shard_map/all_to_all | solution.py:1025
  69.2 122.0 %reduce-scatter.2.cloned.1.call-start = ((), (), s32[]{:S(2)}) async-start(), calls=%async_computation.8 | async-start | bytes 5308416 | tf_op jit(solution)/shard_map/reduce_scatter | solution.py:1281
  90.8 4.6 %collective-permute-start.10 = (bf16[4,3,96,768]{3,2,1,0:T(8,128)(2,1)}, bf16[4,3,96,768]{3,2,1,0:T(8,128)(2,1)}, u32[]{:S(2)}, u32[]{:S(2)}) collective-permute-start(bf16[4,3,96,768]{3,2,1,0:T(8,128)(2,1)} %hold.7.refs_7_), channel_id=1, source_target_pairs={{0,1},{1,0},{2,3},{3,2},{4,5},{5,4},{6,7},{7,6},{8,9},{9,8},{10,11... | collective-permute-start | bytes 5308424 | tf_op jit(solution)/shard_map/ppermute | solution.py:1008
  91.9 3.5 %collective-permute-start.9 = (bf16[4,96,768]{2,1,0:T(8,128)(2,1)S(1)}, bf16[4,96,768]{2,1,0:T(8,128)(2,1)S(1)}, u32[]{:S(2)}, u32[]{:S(2)}) collective-permute-start(bf16[4,96,768]{2,1,0:T(8,128)(2,1)S(1)} %copy-done.11), channel_id=1, source_target_pairs={{0,1},{1,0},{2,3},{3,2},{4,5},{5,4},{6,7},{7,6},{8,9},{9,8},{10,11... | collective-permute-start | bytes 1769480 | tf_op jit(solution)/shard_map/ppermute | solution.py:1008
  126.0 6.2 %collective-permute-start.11 = (bf16[4,4,96,768]{3,2,1,0:T(8,128)(2,1)}, bf16[4,4,96,768]{3,2,1,0:T(8,128)(2,1)S(1)}, u32[]{:S(2)}, u32[]{:S(2)}) collective-permute-start(bf16[4,4,96,768]{3,2,1,0:T(8,128)(2,1)} %get-tuple-element.122), channel_id=1, source_target_pairs={{0,1},{1,0},{2,3},{3,2},{4,5},{5,4},{6,7},{7,6},{8,9},{9,8},{10,11... | collective-permute-start | bytes 7077896 | tf_op jit(solution)/shard_map/ppermute | solution.py:1008
  134.1 33.0 %all-to-all-start.2 = ((bf16[4,4,96,768]{3,2,1,0:T(8,128)(2,1)}), bf16[4,4,96,768]{3,2,1,0:T(8,128)(2,1)}, u32[]{:S(2)}, u32[]{:S(2)}) async-start(bf16[4,4,96,768]{3,2,1,0:T(8,128)(2,1)} %core_sum.2.refs_0_), calls=%async_computation.2 | async-start | bytes 4718592 | tf_op jit(solution)/shard_map/all_to_all | solution.py:1025
  138.8 13.7 %copy-start.16 = (s32[4,496]{1,0:T(4,128)S(1)}, s32[4,496]{1,0:T(4,128)}, u32[]{:S(2)}) copy-start(s32[4,496]{1,0:T(4,128)} %refs_0_.5) | copy-start | bytes 23812
  152.3 10.4 %collective-permute-start.12 = (bf16[4,4,96,768]{3,2,1,0:T(8,128)(2,1)}, bf16[4,4,96,768]{3,2,1,0:T(8,128)(2,1)S(1)}, u32[]{:S(2)}, u32[]{:S(2)}) collective-permute-start(bf16[4,4,96,768]{3,2,1,0:T(8,128)(2,1)} %get-tuple-element.130), channel_id=1, source_target_pairs={{0,1},{1,0},{2,3},{3,2},{4,5},{5,4},{6,7},{7,6},{8,9},{9,8},{10,11... | collective-permute-start | bytes 7077896 | tf_op jit(solution)/shard_map/ppermute | solution.py:1008
  153.9 8.8 %copy-start.32 = (bf16[4,4,96,768]{3,2,1,0:T(8,128)(2,1)S(1)}, bf16[4,4,96,768]{3,2,1,0:T(8,128)(2,1)}, u32[]{:S(2)}) copy-start(bf16[4,4,96,768]{3,2,1,0:T(8,128)(2,1)} %get-tuple-element.129.refs_0_) | copy-start | bytes 7077892
  167.1 32.0 %all-to-all-start.3 = ((bf16[4,4,96,768]{3,2,1,0:T(8,128)(2,1)}), bf16[4,4,96,768]{3,2,1,0:T(8,128)(2,1)}, u32[]{:S(2)}, u32[]{:S(2)}) async-start(bf16[4,4,96,768]{3,2,1,0:T(8,128)(2,1)} %core_sum.3.refs_1_), calls=%async_computation.4 | async-start | bytes 4718592 | tf_op jit(solution)/shard_map/all_to_all | solution.py:1025
  174.6 17.8 %collective-permute-start.14 = (bf16[96,768]{1,0:T(8,128)(2,1)}, bf16[96,768]{1,0:T(8,128)(2,1)}, u32[]{:S(2)}, u32[]{:S(2)}) collective-permute-start(bf16[96,768]{1,0:T(8,128)(2,1)} %get-tuple-element.143), channel_id=1, source_target_pairs={{0,2},{1,3},{2,0},{3,1},{4,6},{5,7},{6,4},{7,5},{8,10},{9,11},{10,... | collective-permute-start | bytes 442376 | tf_op jit(solution)/shard_map/ppermute | solution.py:1008
  174.6 17.8 %collective-permute-start.15 = (bf16[96,768]{1,0:T(8,128)(2,1)}, bf16[96,768]{1,0:T(8,128)(2,1)}, u32[]{:S(2)}, u32[]{:S(2)}) collective-permute-start(bf16[96,768]{1,0:T(8,128)(2,1)} %get-tuple-element.144), channel_id=1, source_target_pairs={{0,4},{1,5},{2,6},{3,7},{4,0},{5,1},{6,2},{7,3},{8,12},{9,13},{10,... | collective-permute-start | bytes 442376 | tf_op jit(solution)/shard_map/ppermute | solution.py:1008
  177.6 14.8 %collective-permute-start.16 = (bf16[96,768]{1,0:T(8,128)(2,1)}, bf16[96,768]{1,0:T(8,128)(2,1)}, u32[]{:S(2)}, u32[]{:S(2)}) collective-permute-start(bf16[96,768]{1,0:T(8,128)(2,1)} %get-tuple-element.145), channel_id=1, source_target_pairs={{0,6},{1,7},{2,4},{3,5},{4,2},{5,3},{6,0},{7,1},{8,14},{9,15},{10,... | collective-permute-start | bytes 442376 | tf_op jit(solution)/shard_map/ppermute | solution.py:1008
  179.0 9.6 %copy-start.25 = (s32[1,1024]{1,0:T(1,128)S(1)}, s32[1,1024]{1,0:T(1,128)}, u32[]{:S(2)}) copy-start(s32[1,1024]{1,0:T(1,128)} %constant.34.clone.refs_3_.refs_6_) | copy-start | bytes 12292
  179.0 9.6 %copy-start.38 = (f32[16,1024]{1,0:T(8,128)S(1)}, f32[16,1024]{1,0:T(8,128)}, u32[]{:S(2)}) copy-start(f32[16,1024]{1,0:T(8,128)} %copy-done.37) | copy-start | bytes 196612
  179.0 9.5 %copy-start.41 = (f32[8,768]{1,0:T(8,128)S(1)}, f32[8,768]{1,0:T(8,128)}, u32[]{:S(2)}) copy-start(f32[8,768]{1,0:T(8,128)} %copy-done.40) | copy-start | bytes 73732
  179.0 9.5 %copy-start.43 = (f32[8,768]{1,0:T(8,128)S(1)}, f32[8,768]{1,0:T(8,128)}, u32[]{:S(2)}) copy-start(f32[8,768]{1,0:T(8,128)} %copy-done.42) | copy-start | bytes 73732
  191.2 3.2 %collective-permute-start.13 = (f32[4,16,256]{2,1,0:T(8,128)}, f32[4,16,256]{2,1,0:T(8,128)}, u32[]{:S(2)}, u32[]{:S(2)}) collective-permute-start(f32[4,16,256]{2,1,0:T(8,128)} %get-tuple-element.142), channel_id=1, source_target_pairs={{0,1},{1,0},{2,3},{3,2},{4,5},{5,4},{6,7},{7,6},{8,9},{9,8},{10,11... | collective-permute-start | bytes 196616 | tf_op jit(solution)/shard_map/ppermute | solution.py:1008
  201.8 8.7 %collective-permute-start.17 = (bf16[112,768]{1,0:T(8,128)(2,1)S(1)}, bf16[112,768]{1,0:T(8,128)(2,1)S(1)}, u32[]{:S(2)}, u32[]{:S(2)}) collective-permute-start(bf16[112,768]{1,0:T(8,128)(2,1)S(1)} %get-tuple-element.147), channel_id=1, source_target_pairs={{0,2},{1,3},{2,0},{3,1},{4,6},{5,7},{6,4},{7,5},{8,10},{9,11},{10,... | collective-permute-start | bytes 516104 | tf_op jit(solution)/shard_map/ppermute | solution.py:1008
  201.9 15.5 %collective-permute-start.18 = (bf16[112,768]{1,0:T(8,128)(2,1)S(1)}, bf16[112,768]{1,0:T(8,128)(2,1)S(1)}, u32[]{:S(2)}, u32[]{:S(2)}) collective-permute-start(bf16[112,768]{1,0:T(8,128)(2,1)S(1)} %get-tuple-element.148), channel_id=1, source_target_pairs={{0,4},{1,5},{2,6},{3,7},{4,0},{5,1},{6,2},{7,3},{8,12},{9,13},{10,... | collective-permute-start | bytes 516104 | tf_op jit(solution)/shard_map/ppermute | solution.py:1008
  204.8 12.5 %collective-permute-start.19 = (bf16[112,768]{1,0:T(8,128)(2,1)S(1)}, bf16[112,768]{1,0:T(8,128)(2,1)S(1)}, u32[]{:S(2)}, u32[]{:S(2)}) collective-permute-start(bf16[112,768]{1,0:T(8,128)(2,1)S(1)} %get-tuple-element.149), channel_id=1, source_target_pairs={{0,6},{1,7},{2,4},{3,5},{4,2},{5,3},{6,0},{7,1},{8,14},{9,15},{10,... | collective-permute-start | bytes 516104 | tf_op jit(solution)/shard_map/ppermute | solution.py:1008
  206.2 11.2 %copy-start.29 = (bf16[112,768]{1,0:T(8,128)(2,1)S(1)}, bf16[112,768]{1,0:T(8,128)(2,1)}, u32[]{:S(2)}) copy-start(bf16[112,768]{1,0:T(8,128)(2,1)} %copy-done.28) | copy-start | bytes 516100
  206.2 11.8 %all-to-all-start.4 = ((bf16[4,96,768]{2,1,0:T(8,128)(2,1)}), bf16[4,96,768]{2,1,0:T(8,128)(2,1)}, u32[]{:S(2)}, u32[]{:S(2)}) async-start(bf16[4,96,768]{2,1,0:T(8,128)(2,1)} %hold.9), calls=%async_computation.5 | async-start | bytes 1179648 | tf_op jit(solution)/shard_map/all_to_all | solution.py:1025
  220.2 23.8 %copy-start.5 = (s32[3]{0:T(128)S(1)}, s32[3]{0:T(128)}, u32[]{:S(2)}) copy-start(s32[3]{0:T(128)} %copy-done.4) | copy-start | bytes 40
  220.2 23.8 %all-to-all-start.5 = ((bf16[4,208,768]{2,1,0:T(8,128)(2,1)}), bf16[4,208,768]{2,1,0:T(8,128)(2,1)S(1)}, u32[]{:S(2)}, u32[]{:S(2)}) async-start(bf16[4,208,768]{2,1,0:T(8,128)(2,1)} %end_sum.1), calls=%async_computation.6 | async-start | bytes 2555904 | tf_op jit(solution)/shard_map/all_to_all | solution.py:1025
  223.9 19.5 %collective-permute-start.22 = (bf16[96,768]{1,0:T(8,128)(2,1)S(1)}, bf16[96,768]{1,0:T(8,128)(2,1)S(1)}, u32[]{:S(2)}, u32[]{:S(2)}) collective-permute-start(bf16[96,768]{1,0:T(8,128)(2,1)S(1)} %copy-done.14), channel_id=1, source_target_pairs={{0,24},{8,16},{16,8},{24,0},{1,25},{9,17},{17,9},{25,1},{2,26},{10... | collective-permute-start | bytes 442376 | tf_op jit(solution)/shard_map/ppermute | solution.py:1013
  226.7 17.2 %collective-permute-start.21 = (bf16[96,768]{1,0:T(8,128)(2,1)S(1)}, bf16[96,768]{1,0:T(8,128)(2,1)S(1)}, u32[]{:S(2)}, u32[]{:S(2)}) collective-permute-start(bf16[96,768]{1,0:T(8,128)(2,1)S(1)} %copy-done.14), channel_id=1, source_target_pairs={{0,16},{8,24},{16,0},{24,8},{1,17},{9,25},{17,1},{25,9},{2,18},{10... | collective-permute-start | bytes 442376 | tf_op jit(solution)/shard_map/ppermute | solution.py:1013
  227.3 16.7 %collective-permute-start.20 = (bf16[96,768]{1,0:T(8,128)(2,1)S(1)}, bf16[96,768]{1,0:T(8,128)(2,1)S(1)}, u32[]{:S(2)}, u32[]{:S(2)}) collective-permute-start(bf16[96,768]{1,0:T(8,128)(2,1)S(1)} %copy-done.14), channel_id=1, source_target_pairs={{0,8},{8,0},{16,24},{24,16},{1,9},{9,1},{17,25},{25,17},{2,10},{10... | collective-permute-start | bytes 442376 | tf_op jit(solution)/shard_map/ppermute | solution.py:1013
  (33 other events, 93.3 us)
Sparse Core Ops, SparseCore 0:
  36.0 51.9 all-gather.1
  126.1 55.3 reduce-scatter.1
